TPU v7x, 512 devices: a whole 4x8x8 slice. The times are simulated.
512 devices in a mesh: ctx: 32 (over x_lo, z, core), heads: 16 (over x_hi, y).
Axes of the slice: x: 4 (x_hi: 2, x_lo: 2; x = x_hi * 2 + x_lo), y: 8, z: 8, core: 2. Of those that a mesh axis runs over, the one named last changes fastest.
Arguments:
- queries: bfloat16 [8192, 8192], P('ctx', 'heads'), may hold values from -6 to 6
- keys: bfloat16 [8192, 8192], P('ctx', 'heads'), may hold values from -6 to 6
- values: bfloat16 [8192, 8192], P('ctx', 'heads'), may hold values from -60 to 60
- hyena_inputs: bfloat16 [3, 8192, 8192], P(None, 'ctx', 'heads'), may hold values from -6 to 6
- hyena_filter: float32 [7, 8192], P(None, 'heads'), may hold values from -2.4 to 2.4
- norm_gain: float32 [8192], P('heads'), may hold values from 0.5 to 1.5
Outputs:
- mixed: bfloat16 [8192, 8192], P('ctx', 'heads')
All inputs are finite; a program needn't handle non-finite values.
Results may differ from a plain program's by a relative error of at most 0.009.
Values may be sent and summed in bfloat16 or wider, within the bound.
No kernel may reach another device: no remote copies, remote signals or barrier semaphores. Data moves between devices by JAX's collectives and lax.ppermute only.
A program may use at most 64 MiB of HBM per device.

v0:
```python
import math

import jax
import jax.numpy as jnp
from jax import lax
from jax.sharding import PartitionSpec as P

DH = 128
WIDTH = 8192


def from_behind(array, axis, by):
    size = lax.axis_size(axis)
    pairs = [(i, i + by) for i in range(size) if 0 <= i + by < size]
    return lax.ppermute(array, axis, pairs)


def attend(half_state, query_block, query_place, key_block, value_block, key_place):
    numerator, maxima, totals = half_state
    score_scale = 1.0 / math.sqrt(query_block.shape[2])
    scores = (
        jnp.einsum("qhd,khd->qhk", query_block, key_block, preferred_element_type=jnp.float32)
        * score_scale
    )
    visible = key_place[None, None, :] <= query_place[:, None, None]
    scores = jnp.where(visible, scores, -1e30)
    row_top = jnp.maximum(maxima, jnp.max(scores, axis=2))
    rescale = jnp.exp(maxima - row_top)
    weights = jnp.where(visible, jnp.exp(scores - row_top[:, :, None]), 0.0)
    totals = totals * rescale + jnp.sum(weights, axis=2)
    summed = jnp.einsum(
        "qhk,khd->qhd",
        weights.astype(jnp.bfloat16),
        value_block,
        preferred_element_type=jnp.float32,
    )
    numerator = numerator * rescale[:, :, None] + summed
    return (numerator, row_top, totals)


def fresh_state(row_total, head_total, head_size):
    return (
        jnp.zeros((row_total, head_total, head_size), jnp.float32),
        jnp.full((row_total, head_total), -1e30, jnp.float32),
        jnp.zeros((row_total, head_total), jnp.float32),
    )


def cycle_attention(queries, keys, values):
    row_count, col_count = queries.shape
    head_count = col_count // DH
    half_rows = row_count // 2
    ctx_index = lax.axis_index("ctx")
    query_starts = (ctx_index * row_count, ctx_index * row_count + half_rows)
    query_heads = queries.reshape(row_count, head_count, DH)
    query_halves = (query_heads[:half_rows], query_heads[half_rows:])
    query_places = tuple(
        (query_starts[number] + jnp.arange(half_rows, dtype=jnp.int32) for number in range(2))
    )
    empty_state = fresh_state(half_rows, head_count, DH)
    key_rows = lax.all_gather(keys, "ctx", axis=0, tiled=True)
    value_rows = lax.all_gather(values, "ctx", axis=0, tiled=True)
    count = key_rows.shape[0]
    block_rows = math.gcd(count, half_rows)
    key_heads = key_rows.reshape(count, head_count, DH)
    value_heads = value_rows.reshape(count, head_count, DH)

    def inner(block_index, state):
        first = block_index * block_rows
        key_block = lax.dynamic_slice_in_dim(key_heads, first, block_rows, 0)
        value_block = lax.dynamic_slice_in_dim(value_heads, first, block_rows, 0)
        key_place = first + jnp.arange(block_rows, dtype=jnp.int32)
        updated = []
        for number in range(2):
            query_block = query_halves[number]
            query_place = query_places[number]

            def update(half_state):
                return attend(
                    half_state, query_block, query_place, key_block, value_block, key_place
                )

            needed = key_place[0] <= query_place[half_rows - 1]
            updated.append(lax.cond(needed, update, lambda half_state: half_state, state[number]))
        return tuple(updated)

    finished = lax.fori_loop(0, count // block_rows, inner, (empty_state, empty_state))
    halves_out = [finished[number][0] / finished[number][2][:, :, None] for number in range(2)]
    return jnp.concatenate(halves_out, axis=0).reshape(row_count, col_count).astype(jnp.bfloat16)


def on_device(queries, keys, values, hyena_inputs, hyena_filter, norm_gain):
    row_count, col_count = queries.shape
    rim_rows = hyena_filter.shape[0] - 1
    tail_rows = hyena_inputs[1:, row_count - rim_rows :, :]
    earlier = from_behind(tail_rows, "ctx", 1)
    joined = jnp.concatenate([earlier, hyena_inputs[1:]], axis=1)
    product = joined[0].astype(jnp.float32) * joined[1].astype(jnp.float32)
    convolved = jnp.zeros((row_count, col_count), jnp.float32)
    for filter_tap in range(rim_rows + 1):
        convolved = (
            convolved
            + hyena_filter[filter_tap][None, :]
            * product[rim_rows - filter_tap : rim_rows - filter_tap + row_count]
        )
    hyena_out = hyena_inputs[0].astype(jnp.float32) * convolved
    attention = cycle_attention(queries, keys, values)
    attention_wide = lax.optimization_barrier(attention).astype(jnp.float32)
    local_squares = jnp.sum(attention_wide * attention_wide, axis=1)
    square_total = lax.psum(local_squares, "heads")
    square_mean = square_total / WIDTH
    normed = attention_wide * lax.rsqrt(square_mean + 1e-06)[:, None] * norm_gain[None, :]
    return (normed + hyena_out).astype(jnp.bfloat16)


def solution(mesh):
    placed = (
        P("ctx", "heads"),
        P("ctx", "heads"),
        P("ctx", "heads"),
        P(None, "ctx", "heads"),
        P(None, "heads"),
        P("heads"),
    )
    return jax.shard_map(
        on_device, mesh=mesh, in_specs=placed, out_specs=P("ctx", "heads"), check_vma=False
    )
```

profile of v0, /device:TPU:454, one launch (start us, length us, event | category | flops | bytes accessed | tf_op | source)
XLA Modules:
  0.0 578.1 jit_solution(9762113327099716798)
XLA Ops:
  6.5 1.8 copy.12
  8.4 1.8 copy.13
  10.9 1.9 collective-permute-start
  14.9 1.1 slice.119
  16.6 81.6 %all-gather.3.cloned.1.call-done = bf16[8192,512]{0,1:T(8,128)(2,1)} async-done(((bf16[256,512]{0,1:T(8,128)(2,1)}), bf16[8192,512]{0,1:T(8,128)(2,1)}) %all-gather.3.cloned.1.call-update) | async-done | bytes 8388624 | tf_op jit(solution)/shard_map/all_gather | solution.py:61
  98.3 92.8 %all-gather.5.cloned.1.call-done = bf16[8192,512]{0,1:T(8,128)(2,1)} async-done(((bf16[256,512]{0,1:T(8,128)(2,1)}), bf16[8192,512]{0,1:T(8,128)(2,1)}) %all-gather.5.cloned.1.call-update) | async-done | bytes 8388624 | tf_op jit(solution)/shard_map/all_gather | solution.py:62
  191.1 337.4 %while.23 = (s32[]{:T(128)}, f32[128,4,128]{2,0,1:T(8,128)S(1)}, f32[128,4]{0,1:T(4,128)S(1)}, f32[128,4]{0,1:T(4,128)S(1)}, f32[128,4,128]{2,0,1:T(8,128)S(1)},...) while((s32[]{:T(128)}, f32[128,4,128]{2,0,1:T(8,128)S(1)}, ...), condition=%wide.region_9.10_spmd, body=%wide.region_0.9_spmd.sunk | while | flops 68585608 | bytes 4656111 | solution.py:87
  191.2 1.0 constant_dynamic-slice_fusion.3
  196.5 1.0 constant_dynamic-slice_fusion.3
  201.8 1.0 constant_dynamic-slice_fusion.3
  207.1 1.0 constant_dynamic-slice_fusion.3
  212.5 1.0 constant_dynamic-slice_fusion.3
  217.8 1.0 constant_dynamic-slice_fusion.3
  223.1 1.0 constant_dynamic-slice_fusion.3
  228.5 1.0 constant_dynamic-slice_fusion.3
  233.8 1.0 constant_dynamic-slice_fusion.3
  239.1 1.0 constant_dynamic-slice_fusion.3
  244.4 1.0 constant_dynamic-slice_fusion.3
  249.8 1.0 constant_dynamic-slice_fusion.3
  255.1 1.0 constant_dynamic-slice_fusion.3
  260.4 1.0 constant_dynamic-slice_fusion.3
  265.8 1.0 constant_dynamic-slice_fusion.3
  271.1 1.0 constant_dynamic-slice_fusion.3
  276.4 1.0 constant_dynamic-slice_fusion.3
  281.7 1.0 constant_dynamic-slice_fusion.3
  287.1 1.0 constant_dynamic-slice_fusion.3
  292.4 1.0 constant_dynamic-slice_fusion.3
  297.7 1.0 constant_dynamic-slice_fusion.3
  303.0 1.0 constant_dynamic-slice_fusion.3
  308.4 1.0 constant_dynamic-slice_fusion.3
  313.7 1.0 constant_dynamic-slice_fusion.3
  319.0 1.0 constant_dynamic-slice_fusion.3
  383.0 1.0 constant_dynamic-slice_fusion.3
  398.9 1.0 constant_dynamic-slice_fusion.3
  404.3 1.0 constant_dynamic-slice_fusion.3
  409.6 1.0 constant_dynamic-slice_fusion.3
  414.9 1.0 constant_dynamic-slice_fusion.3
  420.3 1.0 constant_dynamic-slice_fusion.3
  425.6 1.0 constant_dynamic-slice_fusion.3
  430.9 1.0 constant_dynamic-slice_fusion.3
  436.2 1.0 constant_dynamic-slice_fusion.3
  441.6 1.0 constant_dynamic-slice_fusion.3
  452.2 1.0 constant_dynamic-slice_fusion.3
  457.5 1.0 constant_dynamic-slice_fusion.3
  473.5 1.0 constant_dynamic-slice_fusion.3
  520.8 1.0 constant_dynamic-slice_fusion.3
  529.0 40.1 %psum.7 = f32[256]{0:T(256)S(1)} all-reduce(f32[256]{0:T(256)S(1)} %fusion.20), channel_id=1, replica_groups=mesh['ctx'=32,'heads'=16] {'heads'}, use_global_device_ids=true, to_apply=%region_11.12 | all-reduce | flops 256 | bytes 2048 | tf_op jit(solution)/shard_map/psum | solution.py:110
  569.1 2.2 fusion.23
  (1361 shorter events, 293.9 us)
Async XLA Ops:
  6.5 91.7 %all-gather.3.cloned.1.call-start = ((), (), s32[]{:S(2)}) async-start(), calls=%async_computation | async-start | bytes 8650752 | tf_op jit(solution)/shard_map/all_gather | solution.py:61
  8.4 182.7 %all-gather.5.cloned.1.call-start = ((), (), s32[]{:S(2)}) async-start(), calls=%async_computation.1 | async-start | bytes 8650752 | tf_op jit(solution)/shard_map/all_gather | solution.py:62
  10.9 5.5 collective-permute-start
  191.1 378.0 %copy-start = (f32[512]{0:T(512)S(1)}, f32[512]{0:T(512)}, u32[]{:S(2)}) copy-start(f32[512]{0:T(512)} %param.17) | copy-start | bytes 6148
Sparse Core Ops, SparseCore 0:
  9.4 88.8 all-gather.2
  100.3 90.6 all-gather.4
where the time goes:
time: 582 us; the launch traced here: 578 us
  waiting for transfers between devices  174 us (30%)
  local copies, waits for them, and re-layouts  164 us (28%)
  loops' own time  98.4 us (17%)
  matrix products  62 us (11%)
  blocking collectives  40.1 us (7%)
  other arithmetic  24.2 us (4%)
  between operations  13.6 us (2%)
    all_gather x1, waiting for transfers between devices, cycle_attention(): value_rows = lax.all_gather(values, 'ctx', axis=0, tiled=True)  92.8 us
    another operation x1, loops' own time, cycle_attention(): lax.fori_loop(0, count // block_rows, inner, (empty_state, empty_state))  92.1 us
    all_gather x1, waiting for transfers between devices, cycle_attention(): key_rows = lax.all_gather(keys, 'ctx', axis=0, tiled=True)  81.6 us
    slice x128, local copies, waits for them, and re-layouts, inner(): needed = key_place[0] <= query_place[half_rows - 1]  74.4 us
    dynamic_slice x128, local copies, waits for them, and re-layouts, inner(): value_block = lax.dynamic_slice_in_dim(value_heads, first, block_rows, 0)  72.4 us
    psum x1, blocking collectives, on_device(): square_total = lax.psum(local_squares, 'heads')  40.1 us
    dot_general x123, matrix products, attend(): jnp.einsum('qhk,khd->qhd', weights.astype(jnp.bfloat16), value_block, pre...  34.3 us
    dot_general x123, matrix products, attend(): jnp.einsum('qhd,khd->qhk', query_block, key_block, preferred_element_type...  27.8 us
  transfers between devices with their start and end apart: 3, of which 2 were waited for; matrix products, arithmetic and copies ran while one was open for 1% of the time, Pallas kernels for 0%

commit v1 on v0

v1 whole, which is shorter than its diff:
```python
import functools
import math

import jax
import jax.numpy as jnp
from jax import lax
from jax.experimental import pallas as pl
from jax.experimental.pallas import tpu as pltpu
from jax.sharding import PartitionSpec as P

DH = 128
WIDTH = 8192
Z = 8
ROWS = 256
SCALE2 = math.log2(math.e) / math.sqrt(DH)
LOW = -1e29
HIDDEN = -1e30
F32 = jnp.float32
BF16 = jnp.bfloat16


def chip(x, z, c):
    return (x * Z + z % Z) * 2 + c


RING = [
    (chip(x, z, c), chip(x, z + 1 - 2 * c, c)) for x in range(2) for z in range(Z) for c in range(2)
]
CORES = [(chip(x, z, c), chip(x, z, 1 - c)) for x in range(2) for z in range(Z) for c in range(2)]
DOWN = [(chip(1, z, c), chip(0, z, c)) for z in range(Z) for c in range(2)]
UP = [(chip(0, z, c), chip(1, z, c)) for z in range(Z) for c in range(2)]


def lanes(shape):
    return lax.broadcasted_iota(jnp.int32, shape, 1)


def place_columns(columns):
    lane = lanes((ROWS, 128))
    result = jnp.zeros((ROWS, 128), F32)
    for number, column in columns:
        result = jnp.where(lane == number, column, result)
    return result


def exact_parts(value):
    high = value.astype(BF16).astype(F32)
    rest = value - high
    middle = rest.astype(BF16).astype(F32)
    return high, middle, rest - middle


def attend_kernel(chunk_count, first, last, heads, where_ref, q_ref, *refs):
    chunks = refs[:chunk_count]
    refs = refs[chunk_count:]
    if not first:
        acc_in, stat_in = refs[:2]
        refs = refs[2:]
    tile = pl.program_id(0)
    above = where_ref[0]

    def run(masked):
        if masked:
            query_start = where_ref[1 + tile]
            drift = lax.broadcasted_iota(jnp.int32, (ROWS, ROWS), 0) - lanes((ROWS, ROWS))
            seen = [drift >= where_ref[3 + j] - query_start for j in range(chunk_count)]
        columns = []
        for h in range(heads):
            span = slice(h * DH, (h + 1) * DH)
            query = q_ref[0, :, span]
            scores = []
            for j in range(chunk_count):
                score = lax.dot_general(
                    query, chunks[j][0, :, span], (((1,), (1,)), ((), ())), preferred_element_type=F32
                )
                if masked:
                    score = jnp.where(seen[j], score, HIDDEN)
                scores.append(score)
            top = jnp.max(functools.reduce(jnp.maximum, scores), axis=1, keepdims=True)
            if first:
                top = jnp.maximum(top, LOW)
            else:
                old_top = stat_in[0, :, h : h + 1]
                top = jnp.maximum(top, old_top)
                fade = jnp.exp2((old_top - top) * SCALE2)
            weights = [jnp.exp2((score - top) * SCALE2) for score in scores]
            total = jnp.sum(functools.reduce(jnp.add, weights), axis=1, keepdims=True)
            summed = None
            for j in range(chunk_count):
                part = jnp.dot(
                    weights[j].astype(BF16), chunks[j][1, :, span], preferred_element_type=F32
                )
                summed = part if summed is None else summed + part
            if not first:
                total = total + fade * stat_in[0, :, heads + h : heads + h + 1]
                summed = summed + fade * acc_in[0, :, span]
            if last:
                refs[0][0, :, span] = (summed / jnp.maximum(total, 1e-30)).astype(BF16)
                level = jnp.where(total > 0, top * SCALE2 + jnp.log2(jnp.maximum(total, 1e-30)), HIDDEN)
                for k, part in enumerate(exact_parts(level)):
                    columns.append((k * heads + h, part))
            else:
                refs[0][0, :, span] = summed
                columns.append((h, top))
                columns.append((heads + h, total))
        if last:
            refs[0][0, :, heads * DH :] = place_columns(columns).astype(BF16)
        else:
            refs[1][0] = place_columns(columns)

    @pl.when(tile < 2)
    def _():
        run(True)

    @pl.when((tile >= 2) & (above == 0))
    def _():
        run(False)

    if first or last:

        @pl.when((tile >= 2) & (above != 0))
        def _():
            for ref in refs:
                ref[...] = jnp.zeros(ref.shape, ref.dtype)


def attend_call(where, queries, chunks, state, last):
    first = state is None
    width = queries.shape[2]
    heads = width // DH
    tile = lambda cols: pl.BlockSpec((1, ROWS, cols), lambda i, *_: (i, 0, 0))
    whole = pl.BlockSpec((2, ROWS, width), lambda i, *_: (0, 0, 0))
    in_specs = [tile(width)] + [whole] * len(chunks)
    operands = [queries, *chunks]
    if not first:
        in_specs += [tile(width), tile(128)]
        operands += list(state)
    if last:
        out_shape = jax.ShapeDtypeStruct((4, ROWS, width + 128), BF16)
        out_specs = tile(width + 128)
        aliases = {}
    else:
        out_shape = (
            jax.ShapeDtypeStruct((4, ROWS, width), F32),
            jax.ShapeDtypeStruct((4, ROWS, 128), F32),
        )
        out_specs = (tile(width), tile(128))
        aliases = {} if first else {len(operands) - 1: 0, len(operands): 1}
    keys = ROWS * len(chunks)
    return pl.pallas_call(
        functools.partial(attend_kernel, len(chunks), first, last, heads),
        out_shape=out_shape,
        grid_spec=pltpu.PrefetchScalarGridSpec(
            num_scalar_prefetch=1, grid=(4,), in_specs=in_specs, out_specs=out_specs
        ),
        input_output_aliases=aliases,
        compiler_params=pltpu.CompilerParams(vmem_limit_bytes=32 * 1024 * 1024),
        cost_estimate=pl.CostEstimate(
            flops=4 * 4 * ROWS * keys * width,
            bytes_accessed=8 * ROWS * width * 4,
            transcendentals=4 * ROWS * keys * heads,
        ),
    )(where, *operands)


def level_of(ref_value, heads, h):
    wide = ref_value.astype(F32)
    return sum(wide[:, k * heads + h : k * heads + h + 1] for k in range(3))


def merged(parts, levels):
    top = functools.reduce(jnp.maximum, levels)
    shares = [jnp.exp2(level - top) for level in levels]
    total = functools.reduce(jnp.add, shares)
    blend = functools.reduce(
        jnp.add, [part.astype(F32) * share for part, share in zip(parts, shares)]
    )
    return blend / total, top + jnp.log2(total)


def merge_kernel(heads, a_ref, b_ref, o_ref):
    width = heads * DH
    tails = (a_ref[:, width:], b_ref[:, width:])
    columns = []
    for h in range(heads):
        span = slice(h * DH, (h + 1) * DH)
        out, level = merged(
            (a_ref[:, span], b_ref[:, span]), [level_of(tail, heads, h) for tail in tails]
        )
        o_ref[:, span] = out.astype(BF16)
        for k, part in enumerate(exact_parts(level)):
            columns.append((k * heads + h, part))
    o_ref[:, width:] = place_columns(columns).astype(BF16)


def merge_call(a, b):
    heads = a.shape[1] // DH - 1
    return pl.pallas_call(
        functools.partial(merge_kernel, heads), out_shape=jax.ShapeDtypeStruct(a.shape, BF16)
    )(a, b)


def combine_kernel(heads, where_ref, a_ref, b_ref, s_ref, att_ref, square_ref):
    width = heads * DH
    tails = [ref[:, width:] for ref in (a_ref, b_ref, s_ref)]
    squares = jnp.zeros((ROWS, DH), F32)
    for h in range(heads):
        span = slice(h * DH, (h + 1) * DH)
        levels = [level_of(tail, heads, h) for tail in tails]
        levels[2] = jnp.where(where_ref[0] != 0, levels[2], HIDDEN)
        out, _ = merged((a_ref[:, span], b_ref[:, span], s_ref[:, span]), levels)
        half = out.astype(BF16)
        att_ref[:, span] = half
        wide = half.astype(F32)
        squares = squares + wide * wide
    row_sums = jnp.sum(squares, axis=1, keepdims=True)
    square_ref[...] = jnp.broadcast_to(row_sums, (ROWS, 128)).T[: square_ref.shape[0]]


def combine_call(where, a, b, s, group):
    heads = a.shape[1] // DH - 1
    return pl.pallas_call(
        functools.partial(combine_kernel, heads),
        out_shape=(
            jax.ShapeDtypeStruct((ROWS, heads * DH), BF16),
            jax.ShapeDtypeStruct((group, ROWS), F32),
        ),
        in_specs=[pl.BlockSpec(memory_space=pltpu.SMEM)]
        + [pl.BlockSpec(memory_space=pltpu.VMEM)] * 3,
    )(where, a, b, s)


def hyena(hyena_inputs, hyena_filter):
    row_count, col_count = hyena_inputs.shape[1:]
    rim_rows = hyena_filter.shape[0] - 1
    size = lax.axis_size("ctx")
    earlier = lax.ppermute(
        hyena_inputs[1:, row_count - rim_rows :, :], "ctx", [(i, i + 1) for i in range(size - 1)]
    )
    joined = jnp.concatenate([earlier, hyena_inputs[1:]], axis=1)
    product = joined[0].astype(F32) * joined[1].astype(F32)
    convolved = jnp.zeros((row_count, col_count), F32)
    for tap in range(rim_rows + 1):
        start = rim_rows - tap
        convolved = convolved + hyena_filter[tap][None, :] * product[start : start + row_count]
    return hyena_inputs[0].astype(F32) * convolved


def on_device(queries, keys, values, hyena_inputs, hyena_filter, norm_gain):
    ctx = lax.axis_index("ctx")
    x, z, c = ctx // (2 * Z), (ctx // 2) % Z, ctx % 2
    toward = 2 * c - 1
    own = jnp.stack([keys, values])
    other = lax.ppermute(jnp.stack([keys, values, queries]), "ctx", CORES)
    a, b = [own], [other[:2]]
    for step in range(4):
        a.append(lax.ppermute(a[-1], "ctx", RING))
        if step < 3:
            b.append(lax.ppermute(b[-1], "ctx", RING))
    chip_queries = jnp.stack([queries, other[2]])
    queries_all = jnp.concatenate([chip_queries, lax.ppermute(chip_queries, "ctx", DOWN)])

    def where(*chunks):
        starts = [
            ((z + step * toward) % Z) * 2 * ROWS + (c if same else 1 - c) * ROWS
            for same, step in chunks
        ]
        rows = [z * 2 * ROWS + c * ROWS, z * 2 * ROWS + (1 - c) * ROWS]
        return jnp.stack([x, *rows, *starts]).astype(jnp.int32)

    state = attend_call(
        where((1, 0), (1, 1), (0, 1)), queries_all, [a[0], a[1], b[1]], None, False
    )
    state = attend_call(where((1, 2), (0, 2)), queries_all, [a[2], b[2]], state, False)
    state = attend_call(where((1, 3), (0, 3)), queries_all, [a[3], b[3]], state, False)
    parts = attend_call(where((1, 4)), queries_all, [a[4]], state, True)

    below = merge_call(parts[2], lax.ppermute(parts[3], "ctx", CORES))
    across = lax.ppermute(below, "ctx", UP)
    mine = lax.ppermute(parts[1], "ctx", CORES)
    group = lax.axis_size("heads")
    attention, squares = combine_call(
        x.astype(jnp.int32).reshape(1), parts[0], mine, across, group
    )
    spread = lax.all_to_all(squares, "heads", 0, 0, tiled=True)
    square_mean = jnp.sum(spread, axis=0) / WIDTH
    normed = attention.astype(F32) * lax.rsqrt(square_mean + 1e-06)[:, None] * norm_gain[None, :]
    return (normed + hyena(hyena_inputs, hyena_filter)).astype(BF16)


def solution(mesh):
    placed = (
        P("ctx", "heads"),
        P("ctx", "heads"),
        P("ctx", "heads"),
        P(None, "ctx", "heads"),
        P(None, "heads"),
        P("heads"),
    )
    return jax.shard_map(
        on_device, mesh=mesh, in_specs=placed, out_specs=P("ctx", "heads"), check_vma=False
    )
```

time: 582 us -> 139 us (0.24)
  the two profiles are of different devices: /device:TPU:454 before, /device:TPU:2 now
where the time goes in v1:
time: 139 us; the launch traced here: 138 us
  waiting for transfers between devices  59.6 us (43%)
  starting transfers between devices  40.3 us (29%)
  Pallas kernels  24.6 us (18%)
  other arithmetic  6.84 us (5%)
  local copies, waits for them, and re-layouts  6.18 us (4%)
    ppermute x1, waiting for transfers between devices, on_device(): across = lax.ppermute(below, 'ctx', UP)  24.6 us
    pallas_call x4, Pallas kernels, attend_call(): pl.pallas_call(functools.partial(attend_kernel, len(chunks), first, last,...  19.2 us
    ppermute x4, waiting for transfers between devices, on_device(): a.append(lax.ppermute(a[-1], 'ctx', RING))  18.4 us
    ppermute x4, starting transfers between devices, on_device(): a.append(lax.ppermute(a[-1], 'ctx', RING))  10 us
    all_to_all x1, waiting for transfers between devices, on_device(): spread = lax.all_to_all(squares, 'heads', 0, 0, tiled=True)  9.83 us
    all_to_all x1, starting transfers between devices, on_device(): spread = lax.all_to_all(squares, 'heads', 0, 0, tiled=True)  9.05 us
    ppermute x3, starting transfers between devices, on_device(): b.append(lax.ppermute(b[-1], 'ctx', RING))  8.1 us
    ppermute x3, waiting for transfers between devices, on_device(): b.append(lax.ppermute(b[-1], 'ctx', RING))  3.7 us
  transfers between devices with their start and end apart: 14, of which 7 were waited for; matrix products, arithmetic and copies ran while one was open for 4% of the time, Pallas kernels for 13%

profile of v1, /device:TPU:2, one launch (start us, length us, event | category | flops | bytes accessed | tf_op | source)
XLA Modules:
  0.0 138.0 jit_solution(10361926022267865468)
XLA Ops:
  0.0 1.2 pad_maximum_fusion.1
  1.2 1.9 %collective-permute-start = (bf16[3,256,512]{2,1,0:T(8,128)(2,1)S(1)}, bf16[3,256,512]{2,1,0:T(8,128)(2,1)S(1)}, u32[]{:S(2)}, u32[]{:S(2)}) collective-permute-start(bf16[3,256,512]{2,1,0:T(8,128)(2,1)S(1)} %pad_maximum_fusion.1), channel_id=1, source_target_pairs={{0,16},{16,0},{32,48},{48,32},{64,80},{80,64},{96,112},{112,96},{1... | collective-permute-start | bytes 2359304 | tf_op jit(solution)/shard_map/ppermute | solution.py:254
  3.2 1.1 pad_maximum_fusion.3.refs_0_
  4.3 4.3 %collective-permute-start.2 = (bf16[2,256,512]{2,1,0:T(8,128)(2,1)S(1)}, bf16[2,256,512]{2,1,0:T(8,128)(2,1)S(1)}, u32[]{:S(2)}, u32[]{:S(2)}) collective-permute-start(bf16[2,256,512]{2,1,0:T(8,128)(2,1)S(1)} %pad_maximum_fusion.3.refs_0_), channel_id=1, source_target_pairs={{0,32},{16,240},{32,64},{48,16},{64,96},{80,48},{96,128},{112,80},... | collective-permute-start | bytes 1572872 | tf_op jit(solution)/shard_map/ppermute | solution.py:257
  8.5 0.0 collective-permute-done
  8.6 4.3 %collective-permute-start.6 = (bf16[2,256,512]{2,1,0:T(8,128)(2,1)S(1)}, bf16[2,256,512]{2,1,0:T(8,128)(2,1)S(1)}, u32[]{:S(2)}, u32[]{:S(2)}) collective-permute-start(bf16[2,256,512]{2,1,0:T(8,128)(2,1)S(1)} %slice.129), channel_id=1, source_target_pairs={{0,32},{16,240},{32,64},{48,16},{64,96},{80,48},{96,128},{112,80},... | collective-permute-start | bytes 1572872 | tf_op jit(solution)/shard_map/ppermute | solution.py:259
  12.9 9.5 %collective-permute-done.2.refs_1_ = bf16[2,256,512]{2,1,0:T(8,128)(2,1)S(1)} collective-permute-done((bf16[2,256,512]{2,1,0:T(8,128)(2,1)S(1)}, bf16[2,256,512]{2,1,0:T(8,128)(2,1)S(1)}, u32[]{:S(2)}, u32[]{:S(2)}) %collective-permute-start.2) | collective-permute-done | bytes 524320 | tf_op jit(solution)/shard_map/ppermute | solution.py:257
  22.4 1.9 %collective-permute-start.3 = (bf16[2,256,512]{2,1,0:T(8,128)(2,1)S(1)}, bf16[2,256,512]{2,1,0:T(8,128)(2,1)S(1)}, u32[]{:S(2)}, u32[]{:S(2)}) collective-permute-start(bf16[2,256,512]{2,1,0:T(8,128)(2,1)S(1)} %collective-permute-done.2.refs_1_), channel_id=1, source_target_pairs={{0,32},{16,240},{32,64},{48,16},{64,96},{80,48},{96,128},{112,80},... | collective-permute-start | bytes 1572872 | tf_op jit(solution)/shard_map/ppermute | solution.py:257
  24.3 3.7 %collective-permute-done.6.refs_2_ = bf16[2,256,512]{2,1,0:T(8,128)(2,1)S(1)} collective-permute-done((bf16[2,256,512]{2,1,0:T(8,128)(2,1)S(1)}, bf16[2,256,512]{2,1,0:T(8,128)(2,1)S(1)}, u32[]{:S(2)}, u32[]{:S(2)}) %collective-permute-start.6) | collective-permute-done | bytes 524320 | tf_op jit(solution)/shard_map/ppermute | solution.py:259
  28.0 1.9 %collective-permute-start.7 = (bf16[2,256,512]{2,1,0:T(8,128)(2,1)S(1)}, bf16[2,256,512]{2,1,0:T(8,128)(2,1)S(1)}, u32[]{:S(2)}, u32[]{:S(2)}) collective-permute-start(bf16[2,256,512]{2,1,0:T(8,128)(2,1)S(1)} %collective-permute-done.6.refs_2_), channel_id=1, source_target_pairs={{0,32},{16,240},{32,64},{48,16},{64,96},{80,48},{96,128},{112,80},... | collective-permute-start | bytes 1572872 | tf_op jit(solution)/shard_map/ppermute | solution.py:259
  29.9 4.7 %collective-permute-done.3.refs_0_ = bf16[2,256,512]{2,1,0:T(8,128)(2,1)S(1)} collective-permute-done((bf16[2,256,512]{2,1,0:T(8,128)(2,1)S(1)}, bf16[2,256,512]{2,1,0:T(8,128)(2,1)S(1)}, u32[]{:S(2)}, u32[]{:S(2)}) %collective-permute-start.3) | collective-permute-done | bytes 524320 | tf_op jit(solution)/shard_map/ppermute | solution.py:257
  34.6 1.9 %collective-permute-start.4 = (bf16[2,256,512]{2,1,0:T(8,128)(2,1)S(1)}, bf16[2,256,512]{2,1,0:T(8,128)(2,1)S(1)}, u32[]{:S(2)}, u32[]{:S(2)}) collective-permute-start(bf16[2,256,512]{2,1,0:T(8,128)(2,1)S(1)} %collective-permute-done.3.refs_0_), channel_id=1, source_target_pairs={{0,32},{16,240},{32,64},{48,16},{64,96},{80,48},{96,128},{112,80},... | collective-permute-start | bytes 1572872 | tf_op jit(solution)/shard_map/ppermute | solution.py:257
  36.6 0.9 pad_maximum_fusion.2
  37.4 3.2 %collective-permute-start.1 = (bf16[2,256,512]{2,1,0:T(8,128)(2,1)}, bf16[2,256,512]{2,1,0:T(8,128)(2,1)}, u32[]{:S(2)}, u32[]{:S(2)}) collective-permute-start(bf16[2,256,512]{2,1,0:T(8,128)(2,1)} %pad_maximum_fusion.2), channel_id=1, source_target_pairs={{256,0},{272,16},{288,32},{304,48},{320,64},{336,80},{352,96},{368... | collective-permute-start | bytes 1572872 | tf_op jit(solution)/shard_map/ppermute | solution.py:261
  40.7 0.0 collective-permute-done.7.refs_1_
  40.7 1.9 %collective-permute-start.8 = (bf16[2,256,512]{2,1,0:T(8,128)(2,1)S(1)}, bf16[2,256,512]{2,1,0:T(8,128)(2,1)S(1)}, u32[]{:S(2)}, u32[]{:S(2)}) collective-permute-start(bf16[2,256,512]{2,1,0:T(8,128)(2,1)S(1)} %collective-permute-done.7.refs_1_), channel_id=1, source_target_pairs={{0,32},{16,240},{32,64},{48,16},{64,96},{80,48},{96,128},{112,80},... | collective-permute-start | bytes 1572872 | tf_op jit(solution)/shard_map/ppermute | solution.py:259
  42.6 4.3 %collective-permute-done.4.refs_0_ = bf16[2,256,512]{2,1,0:T(8,128)(2,1)S(1)} collective-permute-done((bf16[2,256,512]{2,1,0:T(8,128)(2,1)S(1)}, bf16[2,256,512]{2,1,0:T(8,128)(2,1)S(1)}, u32[]{:S(2)}, u32[]{:S(2)}) %collective-permute-start.4) | collective-permute-done | bytes 524320 | tf_op jit(solution)/shard_map/ppermute | solution.py:257
  46.9 1.9 %collective-permute-start.5 = (bf16[2,256,512]{2,1,0:T(8,128)(2,1)S(1)}, bf16[2,256,512]{2,1,0:T(8,128)(2,1)S(1)}, u32[]{:S(2)}, u32[]{:S(2)}) collective-permute-start(bf16[2,256,512]{2,1,0:T(8,128)(2,1)S(1)} %collective-permute-done.4.refs_0_), channel_id=1, source_target_pairs={{0,32},{16,240},{32,64},{48,16},{64,96},{80,48},{96,128},{112,80},... | collective-permute-start | bytes 1572872 | tf_op jit(solution)/shard_map/ppermute | solution.py:257
  48.8 0.1 pad_add_fusion.where_ref
  48.9 0.1 stack.88.where_ref
  49.0 0.1 stack.85.where_ref
  49.1 0.1 stack.92.where_ref
  49.2 3.0 %collective-permute-done.1 = bf16[2,256,512]{2,1,0:T(8,128)(2,1)} collective-permute-done((bf16[2,256,512]{2,1,0:T(8,128)(2,1)}, bf16[2,256,512]{2,1,0:T(8,128)(2,1)}, u32[]{:S(2)}, u32[]{:S(2)}) %collective-permute-start.1) | collective-permute-done | bytes 524320 | tf_op jit(solution)/shard_map/ppermute | solution.py:261
  52.2 1.2 pad_maximum_fusion.q_ref
  53.4 1.0 copy-done.1
  54.5 1.0 copy-done.3
  55.5 4.3 %shard_map.64 = (f32[4,256,512]{2,1,0:T(8,128)S(1)}, f32[4,256,128]{2,1,0:T(8,128)S(1)}) custom-call(s32[6]{0:T(128)S(1)} %stack.92.where_ref, bf16[4,256,512]{2,1,0:T(8,128)(2,1)S(1)} %pad_maximum_fusion.q_ref, bf16[2,256,512]{2,1,0:T(8,128)(2,1)S(1)} %pad_maximum_fusion.3.refs_0_, bf16[2,256,512]{2,1,0:T(8,128)(2,1)S(1)} %copy-done.1, ...), custom_call_target="tpu_custom_call" | custom-call | flops 1610612736 | bytes 4194304 | tf_op jit(solution)/shard_map/pallas_call | solution.py:150
  59.8 4.2 %shard_map.65 = (f32[4,256,512]{2,1,0:T(8,128)S(1)}, f32[4,256,128]{2,1,0:T(8,128)S(1)}) custom-call(s32[5]{0:T(128)S(1)} %stack.88.where_ref, bf16[4,256,512]{2,1,0:T(8,128)(2,1)S(1)} %pad_maximum_fusion.q_ref, bf16[2,256,512]{2,1,0:T(8,128)(2,1)S(1)} %collective-permute-done.3.refs_0_, ...), custom_call_target="tpu_custom_call", output_to_operand_aliasing={{0}: (4, {}), {1}: (5, {})} | custom-call | flops 1073741824 | bytes 4194304 | tf_op jit(solution)/shard_map/pallas_call | solution.py:150
  64.1 4.2 %shard_map.66 = (f32[4,256,512]{2,1,0:T(8,128)S(1)}, f32[4,256,128]{2,1,0:T(8,128)S(1)}) custom-call(s32[5]{0:T(128)S(1)} %stack.85.where_ref, bf16[4,256,512]{2,1,0:T(8,128)(2,1)S(1)} %pad_maximum_fusion.q_ref, bf16[2,256,512]{2,1,0:T(8,128)(2,1)S(1)} %collective-permute-done.4.refs_0_, ...), custom_call_target="tpu_custom_call", output_to_operand_aliasing={{0}: (4, {}), {1}: (5, {})} | custom-call | flops 1073741824 | bytes 4194304 | tf_op jit(solution)/shard_map/pallas_call | solution.py:150
  68.3 0.0 collective-permute-done.5.refs_0_
  68.3 6.4 %shard_map.67 = bf16[4,256,640]{2,1,0:T(8,128)(2,1)S(1)} custom-call(s32[4]{0:T(128)S(1)} %pad_add_fusion.where_ref, bf16[4,256,512]{2,1,0:T(8,128)(2,1)S(1)} %pad_maximum_fusion.q_ref, bf16[2,256,512]{2,1,0:T(8,128)(2,1)S(1)} %collective-permute-done.5.refs_0_, f32[4,256,512]{2,1,0:T(8,128)S(1)} %get-tuple-element.17.refs_1_, ...), custom_call_target="tpu_custom_call" | custom-call | flops 536870912 | bytes 4194304 | tf_op jit(solution)/shard_map/pallas_call | solution.py:150
  74.7 0.0 copy-start.5
  74.7 0.0 copy-start.9
  74.7 1.0 slice_bitcast_fusion.7
  75.7 2.4 %collective-permute-start.10 = (bf16[256,640]{1,0:T(8,128)(2,1)S(1)}, bf16[256,640]{1,0:T(8,128)(2,1)S(1)}, u32[]{:S(2)}, u32[]{:S(2)}) collective-permute-start(bf16[256,640]{1,0:T(8,128)(2,1)S(1)} %get-tuple-element.21), channel_id=1, source_target_pairs={{0,16},{16,0},{32,48},{48,32},{64,80},{80,64},{96,112},{112,96},{1... | collective-permute-start | bytes 983048 | tf_op jit(solution)/shard_map/ppermute | solution.py:278
  78.1 2.0 %collective-permute-start.9 = (bf16[256,640]{1,0:T(8,128)(2,1)S(1)}, bf16[256,640]{1,0:T(8,128)(2,1)S(1)}, u32[]{:S(2)}, u32[]{:S(2)}) collective-permute-start(bf16[256,640]{1,0:T(8,128)(2,1)S(1)} %get-tuple-element.23), channel_id=1, source_target_pairs={{0,16},{16,0},{32,48},{48,32},{64,80},{80,64},{96,112},{112,96},{1... | collective-permute-start | bytes 983048 | tf_op jit(solution)/shard_map/ppermute | solution.py:280
  80.2 0.7 copy-done.8
  80.9 2.7 %shard_map.68 = bf16[256,640]{1,0:T(8,128)(2,1)} custom-call(bf16[256,640]{1,0:T(8,128)(2,1)} %get-tuple-element.22.a_ref, bf16[256,640]{1,0:T(8,128)(2,1)} %copy-done.8), custom_call_target="tpu_custom_call" | custom-call | tf_op jit(solution)/shard_map/pallas_call | solution.py:198
  83.6 1.3 collective-permute-start.11
  84.9 2.3 %collective-permute-start.12 = (bf16[2,6,512]{2,1,0:T(8,128)(2,1)S(1)}, bf16[2,6,512]{2,1,0:T(8,128)(2,1)S(1)}, u32[]{:S(2)}, u32[]{:S(2)}) collective-permute-start(bf16[2,6,512]{2,1,0:T(8,128)(2,1)S(1)} %slice.104), channel_id=1, source_target_pairs={{0,16},{16,32},{32,48},{48,64},{64,80},{80,96},{96,112},{112,128},... | collective-permute-start | bytes 36872 | tf_op jit(solution)/shard_map/ppermute | solution.py:237
  87.2 24.6 %collective-permute-done.11.s_ref = bf16[256,640]{1,0:T(8,128)(2,1)S(1)} collective-permute-done((bf16[256,640]{1,0:T(8,128)(2,1)}, bf16[256,640]{1,0:T(8,128)(2,1)S(1)}, u32[]{:S(2)}, u32[]{:S(2)}) %collective-permute-start.11) | collective-permute-done | bytes 327712 | tf_op jit(solution)/shard_map/ppermute | solution.py:279
  111.9 0.7 copy-done.7
  112.6 2.7 %shard_map.69 = (bf16[256,512]{1,0:T(8,128)(2,1)}, f32[16,256]{1,0:T(8,128)}) custom-call(s32[1]{0:T(128)} %bitcast.where_ref, bf16[256,640]{1,0:T(8,128)(2,1)} %get-tuple-element.24.a_ref, bf16[256,640]{1,0:T(8,128)(2,1)} %copy-done.6, bf16[256,640]{1,0:T(8,128)(2,1)} %copy-done.7), custom_call_target="tpu_custom_call" | custom-call | tf_op jit(solution)/shard_map/pallas_call | solution.py:222
  115.4 1.3 copy.11
  116.7 9.1 %all-to-all-start = ((f32[16,1,256]{2,1,0:T(1,128)}), f32[16,1,256]{2,1,0:T(1,128)S(1)}, u32[]{:S(2)}, u32[]{:S(2)}) async-start(f32[16,1,256]{2,1,0:T(1,128)} %copy.11), calls=%async_computation | async-start | bytes 32768 | tf_op jit(solution)/shard_map/all_to_all | solution.py:285
  125.8 0.1 convert_multiply_fusion
  125.9 9.8 %all-to-all-done = f32[16,1,256]{2,1,0:T(1,128)S(1)} async-done(((f32[16,1,256]{2,1,0:T(1,128)}), f32[16,1,256]{2,1,0:T(1,128)S(1)}, u32[]{:S(2)}, u32[]{:S(2)}) %all-to-all-start) | async-done | bytes 16416 | tf_op jit(solution)/shard_map/all_to_all | solution.py:285
  135.8 2.2 %fusion.4 = bf16[256,512]{1,0:T(8,128)(2,1)} fusion(f32[1,262,512]{2,1,0:T(8,128)S(1)} %convert_multiply_fusion, bf16[256,512]{1,0:T(8,128)(2,1)} %get-tuple-element.19, f32[512]{0:T(512)S(1)} %bitcast.104, f32[512]{0:T(512)S(1)} %bitcast.105, f32[512]{0:T(512)S(1)} %bitcast.100, f32[512]{0:T(512)S(1)} %bitcast.101, f32[512]{0:T(512)S(1)} %bitcast.102, ...), kind=kLoop, calls=%fused_computation.10 | loop fusion | flops 2621440 | bytes 4473856 | tf_op jit(solution)/shard_map/convert_element_type | solution.py:288
  (28 shorter events, 0.2 us)
Async XLA Ops:
  0.0 36.6 %copy-start.4 = (bf16[256,512]{1,0:T(8,128)(2,1)S(1)}, bf16[256,512]{1,0:T(8,128)(2,1)}, u32[]{:S(2)}) copy-start(bf16[256,512]{1,0:T(8,128)(2,1)} %param.6) | copy-start | bytes 786436
  1.2 7.3 %collective-permute-start = (bf16[3,256,512]{2,1,0:T(8,128)(2,1)S(1)}, bf16[3,256,512]{2,1,0:T(8,128)(2,1)S(1)}, u32[]{:S(2)}, u32[]{:S(2)}) collective-permute-start(bf16[3,256,512]{2,1,0:T(8,128)(2,1)S(1)} %pad_maximum_fusion.1), channel_id=1, source_target_pairs={{0,16},{16,0},{32,48},{48,32},{64,80},{80,64},{96,112},{112,96},{1... | collective-permute-start | bytes 2359304 | tf_op jit(solution)/shard_map/ppermute | solution.py:254
  4.3 18.1 %collective-permute-start.2 = (bf16[2,256,512]{2,1,0:T(8,128)(2,1)S(1)}, bf16[2,256,512]{2,1,0:T(8,128)(2,1)S(1)}, u32[]{:S(2)}, u32[]{:S(2)}) collective-permute-start(bf16[2,256,512]{2,1,0:T(8,128)(2,1)S(1)} %pad_maximum_fusion.3.refs_0_), channel_id=1, source_target_pairs={{0,32},{16,240},{32,64},{48,16},{64,96},{80,48},{96,128},{112,80},... | collective-permute-start | bytes 1572872 | tf_op jit(solution)/shard_map/ppermute | solution.py:257
  8.6 19.4 %collective-permute-start.6 = (bf16[2,256,512]{2,1,0:T(8,128)(2,1)S(1)}, bf16[2,256,512]{2,1,0:T(8,128)(2,1)S(1)}, u32[]{:S(2)}, u32[]{:S(2)}) collective-permute-start(bf16[2,256,512]{2,1,0:T(8,128)(2,1)S(1)} %slice.129), channel_id=1, source_target_pairs={{0,32},{16,240},{32,64},{48,16},{64,96},{80,48},{96,128},{112,80},... | collective-permute-start | bytes 1572872 | tf_op jit(solution)/shard_map/ppermute | solution.py:259
  22.4 7.6 %copy-start = (bf16[2,256,512]{2,1,0:T(8,128)(2,1)}, bf16[2,256,512]{2,1,0:T(8,128)(2,1)S(1)}, u32[]{:S(2)}) copy-start(bf16[2,256,512]{2,1,0:T(8,128)(2,1)S(1)} %collective-permute-done.2.refs_1_) | copy-start | bytes 1572868
  22.4 12.3 %collective-permute-start.3 = (bf16[2,256,512]{2,1,0:T(8,128)(2,1)S(1)}, bf16[2,256,512]{2,1,0:T(8,128)(2,1)S(1)}, u32[]{:S(2)}, u32[]{:S(2)}) collective-permute-start(bf16[2,256,512]{2,1,0:T(8,128)(2,1)S(1)} %collective-permute-done.2.refs_1_), channel_id=1, source_target_pairs={{0,32},{16,240},{32,64},{48,16},{64,96},{80,48},{96,128},{112,80},... | collective-permute-start | bytes 1572872 | tf_op jit(solution)/shard_map/ppermute | solution.py:257
  28.0 12.7 %copy-start.2 = (bf16[2,256,512]{2,1,0:T(8,128)(2,1)}, bf16[2,256,512]{2,1,0:T(8,128)(2,1)S(1)}, u32[]{:S(2)}) copy-start(bf16[2,256,512]{2,1,0:T(8,128)(2,1)S(1)} %collective-permute-done.6.refs_2_) | copy-start | bytes 1572868
  28.0 12.7 %collective-permute-start.7 = (bf16[2,256,512]{2,1,0:T(8,128)(2,1)S(1)}, bf16[2,256,512]{2,1,0:T(8,128)(2,1)S(1)}, u32[]{:S(2)}, u32[]{:S(2)}) collective-permute-start(bf16[2,256,512]{2,1,0:T(8,128)(2,1)S(1)} %collective-permute-done.6.refs_2_), channel_id=1, source_target_pairs={{0,32},{16,240},{32,64},{48,16},{64,96},{80,48},{96,128},{112,80},... | collective-permute-start | bytes 1572872 | tf_op jit(solution)/shard_map/ppermute | solution.py:259
  34.6 12.3 %collective-permute-start.4 = (bf16[2,256,512]{2,1,0:T(8,128)(2,1)S(1)}, bf16[2,256,512]{2,1,0:T(8,128)(2,1)S(1)}, u32[]{:S(2)}, u32[]{:S(2)}) collective-permute-start(bf16[2,256,512]{2,1,0:T(8,128)(2,1)S(1)} %collective-permute-done.3.refs_0_), channel_id=1, source_target_pairs={{0,32},{16,240},{32,64},{48,16},{64,96},{80,48},{96,128},{112,80},... | collective-permute-start | bytes 1572872 | tf_op jit(solution)/shard_map/ppermute | solution.py:257
  37.4 14.8 %collective-permute-start.1 = (bf16[2,256,512]{2,1,0:T(8,128)(2,1)}, bf16[2,256,512]{2,1,0:T(8,128)(2,1)}, u32[]{:S(2)}, u32[]{:S(2)}) collective-permute-start(bf16[2,256,512]{2,1,0:T(8,128)(2,1)} %pad_maximum_fusion.2), channel_id=1, source_target_pairs={{256,0},{272,16},{288,32},{304,48},{320,64},{336,80},{352,96},{368... | collective-permute-start | bytes 1572872 | tf_op jit(solution)/shard_map/ppermute | solution.py:261
  40.7 23.4 %collective-permute-start.8 = (bf16[2,256,512]{2,1,0:T(8,128)(2,1)S(1)}, bf16[2,256,512]{2,1,0:T(8,128)(2,1)S(1)}, u32[]{:S(2)}, u32[]{:S(2)}) collective-permute-start(bf16[2,256,512]{2,1,0:T(8,128)(2,1)S(1)} %collective-permute-done.7.refs_1_), channel_id=1, source_target_pairs={{0,32},{16,240},{32,64},{48,16},{64,96},{80,48},{96,128},{112,80},... | collective-permute-start | bytes 1572872 | tf_op jit(solution)/shard_map/ppermute | solution.py:259
  46.9 21.4 %collective-permute-start.5 = (bf16[2,256,512]{2,1,0:T(8,128)(2,1)S(1)}, bf16[2,256,512]{2,1,0:T(8,128)(2,1)S(1)}, u32[]{:S(2)}, u32[]{:S(2)}) collective-permute-start(bf16[2,256,512]{2,1,0:T(8,128)(2,1)S(1)} %collective-permute-done.4.refs_0_), channel_id=1, source_target_pairs={{0,32},{16,240},{32,64},{48,16},{64,96},{80,48},{96,128},{112,80},... | collective-permute-start | bytes 1572872 | tf_op jit(solution)/shard_map/ppermute | solution.py:257
  53.4 1.0 copy-start.1
  54.5 1.0 copy-start.3
  74.7 10.1 %copy-start.5 = (bf16[3,256,512]{2,1,0:T(8,128)(2,1)S(1)}, bf16[3,256,512]{2,1,0:T(8,128)(2,1)}, u32[]{:S(2)}) copy-start(bf16[3,256,512]{2,1,0:T(8,128)(2,1)} %param.9) | copy-start | bytes 2359300
  74.7 12.5 %copy-start.9 = (f32[7,512]{1,0:T(8,128)S(1)}, f32[7,512]{1,0:T(8,128)}, u32[]{:S(2)}) copy-start(f32[7,512]{1,0:T(8,128)} %param.10) | copy-start | bytes 43012
  75.7 50.1 %slice-start = ((bf16[3,256,512]{2,1,0:T(8,128)(2,1)}), bf16[2,256,512]{2,1,0:T(8,128)(2,1)S(1)}, s32[]{:S(2)}) async-start(bf16[3,256,512]{2,1,0:T(8,128)(2,1)} %param.9), calls=%async_computation.1 | async-start | bytes 1048576 | tf_op jit(solution)/shard_map/slice | solution.py:240
  75.7 4.5 %collective-permute-start.10 = (bf16[256,640]{1,0:T(8,128)(2,1)S(1)}, bf16[256,640]{1,0:T(8,128)(2,1)S(1)}, u32[]{:S(2)}, u32[]{:S(2)}) collective-permute-start(bf16[256,640]{1,0:T(8,128)(2,1)S(1)} %get-tuple-element.21), channel_id=1, source_target_pairs={{0,16},{16,0},{32,48},{48,32},{64,80},{80,64},{96,112},{112,96},{1... | collective-permute-start | bytes 983048 | tf_op jit(solution)/shard_map/ppermute | solution.py:278
  78.1 9.1 %collective-permute-start.9 = (bf16[256,640]{1,0:T(8,128)(2,1)S(1)}, bf16[256,640]{1,0:T(8,128)(2,1)S(1)}, u32[]{:S(2)}, u32[]{:S(2)}) collective-permute-start(bf16[256,640]{1,0:T(8,128)(2,1)S(1)} %get-tuple-element.23), channel_id=1, source_target_pairs={{0,16},{16,0},{32,48},{48,32},{64,80},{80,64},{96,112},{112,96},{1... | collective-permute-start | bytes 983048 | tf_op jit(solution)/shard_map/ppermute | solution.py:280
  80.2 0.7 copy-start.8
  80.9 54.9 %copy-start.10 = (f32[512]{0:T(512)S(1)}, f32[512]{0:T(512)}, u32[]{:S(2)}) copy-start(f32[512]{0:T(512)} %param.11) | copy-start | bytes 6148
  83.6 28.3 %collective-permute-start.11 = (bf16[256,640]{1,0:T(8,128)(2,1)}, bf16[256,640]{1,0:T(8,128)(2,1)S(1)}, u32[]{:S(2)}, u32[]{:S(2)}) collective-permute-start(bf16[256,640]{1,0:T(8,128)(2,1)} %shard_map.68), channel_id=1, source_target_pairs={{0,256},{16,272},{32,288},{48,304},{64,320},{80,336},{96,352},{112... | collective-permute-start | bytes 983048 | tf_op jit(solution)/shard_map/ppermute | solution.py:279
  84.9 40.9 %collective-permute-start.12 = (bf16[2,6,512]{2,1,0:T(8,128)(2,1)S(1)}, bf16[2,6,512]{2,1,0:T(8,128)(2,1)S(1)}, u32[]{:S(2)}, u32[]{:S(2)}) collective-permute-start(bf16[2,6,512]{2,1,0:T(8,128)(2,1)S(1)} %slice.104), channel_id=1, source_target_pairs={{0,16},{16,32},{32,48},{48,64},{64,80},{80,96},{96,112},{112,128},... | collective-permute-start | bytes 36872 | tf_op jit(solution)/shard_map/ppermute | solution.py:237
  87.2 24.7 %copy-start.6 = (bf16[256,640]{1,0:T(8,128)(2,1)}, bf16[256,640]{1,0:T(8,128)(2,1)S(1)}, u32[]{:S(2)}) copy-start(bf16[256,640]{1,0:T(8,128)(2,1)S(1)} %collective-permute-done.9.b_ref) | copy-start | bytes 983044
  111.9 0.7 copy-start.7
  116.7 19.0 %all-to-all-start = ((f32[16,1,256]{2,1,0:T(1,128)}), f32[16,1,256]{2,1,0:T(1,128)S(1)}, u32[]{:S(2)}, u32[]{:S(2)}) async-start(f32[16,1,256]{2,1,0:T(1,128)} %copy.11), calls=%async_computation | async-start | bytes 32768 | tf_op jit(solution)/shard_map/all_to_all | solution.py:285

commit v2 on v0

v2 whole, which is shorter than its diff:
```python
import functools
import math

import jax
import jax.numpy as jnp
from jax import lax
from jax.experimental import pallas as pl
from jax.experimental.pallas import tpu as pltpu
from jax.sharding import PartitionSpec as P

DH = 128
WIDTH = 8192
Z = 8
ROWS = 256
SCALE2 = math.log2(math.e) / math.sqrt(DH)
LOW = -1e29
HIDDEN = -1e30
F32 = jnp.float32
BF16 = jnp.bfloat16


def chip(x, z, c):
    return (x * Z + z % Z) * 2 + c


RING = [
    (chip(x, z, c), chip(x, z + 1 - 2 * c, c)) for x in range(2) for z in range(Z) for c in range(2)
]
CORES = [(chip(x, z, c), chip(x, z, 1 - c)) for x in range(2) for z in range(Z) for c in range(2)]
DOWN = [(chip(1, z, c), chip(0, z, c)) for z in range(Z) for c in range(2)]
UP = [(chip(0, z, c), chip(1, z, c)) for z in range(Z) for c in range(2)]


def kept(shape, dtype):
    return pltpu.VMEM(shape, dtype)


def room(mebibytes):
    return pltpu.CompilerParams(vmem_limit_bytes=mebibytes * 1024 * 1024)


def rows_placed(count, numbered):
    row = lax.broadcasted_iota(jnp.int32, (count, ROWS), 0)
    result = jnp.zeros((count, ROWS), F32)
    for number, value in numbered:
        result = jnp.where(row == number, value, result)
    return result


def exact_parts(value):
    high = value.astype(BF16).astype(F32)
    rest = value - high
    middle = rest.astype(BF16).astype(F32)
    return high, middle, rest - middle


def prepare_kernel(heads, k_ref, v_ref, q_ref, pair_ref, triple_ref, held, sems):
    copies = [
        pltpu.make_async_copy(source, target, sems.at[number])
        for number, (source, target) in enumerate(
            (
                (v_ref, held),
                (k_ref, pair_ref.at[0]),
                (k_ref, triple_ref.at[0]),
                (q_ref, triple_ref.at[2]),
            )
        )
    ]
    for copy in copies:
        copy.start()
    copies[0].wait()
    for h in range(heads):
        turned = held[:, h * DH : (h + 1) * DH].T
        place = (slice(h % 2 * DH, (h % 2 + 1) * DH), slice(h // 2 * ROWS, (h // 2 + 1) * ROWS))
        for ref in (pair_ref, triple_ref):
            ref[(1, *place)] = turned
    for copy in copies[1:]:
        copy.wait()


def prepare_call(keys, values, queries):
    return pl.pallas_call(
        functools.partial(prepare_kernel, keys.shape[1] // DH),
        out_shape=tuple(kept((n, *keys.shape), BF16) for n in (2, 3)),
        in_specs=[pl.BlockSpec(memory_space=pl.ANY)] * 3,
        scratch_shapes=[pltpu.VMEM(values.shape, BF16), pltpu.SemaphoreType.DMA((4,))],
        compiler_params=room(56),
    )(keys, values, queries)


def attend_kernel(places, plan, last, heads, where_ref, *refs):
    query_refs = (refs[0].at[2], refs[1].at[2], refs[2], refs[3])
    held = refs[4 : 4 + len(places)]
    refs = refs[4 + len(places) :]
    carried = 2 * sum(not first for _, _, first in plan)
    given, results = refs[:carried], refs[carried:]
    above = where_ref[0]

    for tiles, used, first in plan:
        chunks, spots = [held[k] for k in used], [places[k] for k in used]
        if not first:
            (acc_in, stat_in), given = given[:2], given[2:]
        if last:
            outs = [results[t % 2].at[t // 2] for t in range(4)]
        else:
            (acc_out, stat_out), results = results[:2], results[2:]

        def run(tiles, masked):
            pieces = [(tile, h) for tile in tiles for h in range(heads)]
            spans = [slice(h * DH, (h + 1) * DH) for h in range(heads)]
            scores = [
                [
                    lax.dot_general(
                        chunk[0, :, spans[h]],
                        query_refs[tile][:, spans[h]],
                        (((1,), (1,)), ((), ())),
                        preferred_element_type=F32,
                    )
                    for chunk in chunks
                ]
                for tile, h in pieces
            ]
            if masked:
                drift = lax.broadcasted_iota(jnp.int32, (ROWS, ROWS), 1) - lax.broadcasted_iota(
                    jnp.int32, (ROWS, ROWS), 0
                )
                scores = [
                    [
                        jnp.where(drift >= where_ref[spots[j]] - where_ref[1 + tile], score, HIDDEN)
                        for j, score in enumerate(group)
                    ]
                    for (tile, h), group in zip(pieces, scores)
                ]
            tops = [
                jnp.max(functools.reduce(jnp.maximum, group), axis=0, keepdims=True)
                for group in scores
            ]
            if first:
                tops = [jnp.maximum(top, LOW) for top in tops]
            else:
                old_tops = [stat_in[tile % 2, h : h + 1] for tile, h in pieces]
                tops = [jnp.maximum(top, old) for top, old in zip(tops, old_tops)]
                fades = [jnp.exp2((old - top) * SCALE2) for top, old in zip(tops, old_tops)]
            weights = [
                [jnp.exp2((score - top) * SCALE2) for score in group]
                for group, top in zip(scores, tops)
            ]
            totals = [
                jnp.sum(functools.reduce(jnp.add, group), axis=0, keepdims=True) for group in weights
            ]
            sums = [
                functools.reduce(
                    jnp.add,
                    [
                        jnp.dot(
                            chunk[1, h % 2 * DH : (h % 2 + 1) * DH, h // 2 * ROWS : (h // 2 + 1) * ROWS],
                            weight.astype(BF16),
                            preferred_element_type=F32,
                        )
                        for chunk, weight in zip(chunks, group)
                    ],
                )
                for (tile, h), group in zip(pieces, weights)
            ]
            numbered = {tile: [] for tile in tiles}
            for number, (tile, h) in enumerate(pieces):
                local, span = tile % 2, spans[h]
                top, total, summed = tops[number], totals[number], sums[number]
                if not first:
                    total = total + fades[number] * stat_in[tile % 2, heads + h : heads + h + 1]
                    summed = summed + fades[number] * acc_in[local, span]
                if last:
                    safe = jnp.maximum(total, 1e-30)
                    outs[tile][span] = (summed * (1.0 / safe)).astype(BF16)
                    level = jnp.where(total > 0, top * SCALE2 + jnp.log2(safe), HIDDEN)
                    for k, part in enumerate(exact_parts(level)):
                        numbered[tile].append((k * heads + h, part))
                else:
                    acc_out[local, span] = summed
                    numbered[tile].append((h, top))
                    numbered[tile].append((heads + h, total))
            for tile in tiles:
                if last:
                    outs[tile][heads * DH :] = rows_placed(16, numbered[tile]).astype(BF16)
                else:
                    stat_out[tile % 2] = rows_placed(8, numbered[tile])

        if tiles == NEAR:
            run(tiles, True)
        else:

            @pl.when(above == 0)
            def _():
                run(tiles, False)

            @pl.when(above != 0)
            def _():
                if last:
                    for ref in results:
                        ref[1] = jnp.zeros(ref.shape[1:], BF16)
                else:
                    for ref in (acc_out, stat_out):
                        ref[...] = jnp.zeros(ref.shape, F32)


NEAR, ABOVE = (0, 1), (2, 3)


def attend_call(where, queries, numbered, plan, last=False):
    places, chunks = [3 + number for number, _ in numbered], [chunk for _, chunk in numbered]
    width = queries[2].shape[1]
    heads = width // DH
    operands = [*queries, *chunks, *(array for _, _, state in plan for array in state or ())]
    if last:
        out_shape = tuple(kept((2, width + 16, ROWS), BF16) for _ in range(2))
    else:
        out_shape = tuple(
            kept((2, rows, ROWS), F32) for _ in plan for rows in (width, 8)
        )
    work = 2 * ROWS * ROWS * sum(len(used) for _, used, _ in plan)
    return pl.pallas_call(
        functools.partial(
            attend_kernel,
            places,
            [(tiles, used, state is None) for tiles, used, state in plan],
            last,
            heads,
        ),
        out_shape=out_shape,
        in_specs=[pl.BlockSpec(memory_space=pltpu.SMEM)]
        + [pl.BlockSpec(memory_space=pltpu.VMEM)] * len(operands),
        compiler_params=room(8 + 6 * len(chunks)),
        cost_estimate=pl.CostEstimate(
            flops=4 * work * width,
            bytes_accessed=2 * work * heads,
            transcendentals=work * heads,
        ),
    )(where, *operands)


def levels_of(ref, heads):
    tail = ref[heads * DH :].astype(F32)
    return tail[:heads] + tail[heads : 2 * heads] + tail[2 * heads : 3 * heads]


def shares_of(levels):
    top = functools.reduce(jnp.maximum, levels)
    shares = [jnp.exp2(level - top) for level in levels]
    total = functools.reduce(jnp.add, shares)
    return [share / total for share in shares], top + jnp.log2(total)


def blended(refs, shares, h):
    span = slice(h * DH, (h + 1) * DH)
    return functools.reduce(
        jnp.add, [ref[span].astype(F32) * share[h : h + 1] for ref, share in zip(refs, shares)]
    )


def merge_kernel(heads, a_ref, b_ref, o_ref):
    refs = (a_ref.at[1], b_ref.at[1])
    shares, level = shares_of([levels_of(ref, heads) for ref in refs])
    for h in range(heads):
        o_ref[h * DH : (h + 1) * DH] = blended(refs, shares, h).astype(BF16)
    parts = [
        (k * heads + h, part[h : h + 1])
        for k, part in enumerate(exact_parts(level))
        for h in range(heads)
    ]
    o_ref[heads * DH :] = rows_placed(16, parts).astype(BF16)


def merge_call(a, b):
    heads = a.shape[1] // DH
    return pl.pallas_call(
        functools.partial(merge_kernel, heads),
        out_shape=kept(a.shape[1:], BF16),
        compiler_params=room(8),
    )(a, b)


def combine_kernel(heads, where_ref, a_ref, b_ref, s_ref, att_ref, square_ref):
    refs = (a_ref.at[0], b_ref.at[0], s_ref)
    levels = [levels_of(ref, heads) for ref in refs]
    levels[2] = jnp.where(where_ref[0] != 0, levels[2], HIDDEN)
    shares, _ = shares_of(levels)
    squares = jnp.zeros((DH, ROWS), F32)
    for h in range(heads):
        half = blended(refs, shares, h).astype(BF16)
        att_ref[h * DH : (h + 1) * DH] = half
        wide = half.astype(F32)
        squares = squares + wide * wide
    square_ref[...] = jnp.broadcast_to(
        jnp.sum(squares, axis=0, keepdims=True)[None], square_ref.shape
    )


def combine_call(where, a, b, s, group):
    heads = s.shape[0] // DH
    return pl.pallas_call(
        functools.partial(combine_kernel, heads),
        out_shape=(
            kept((heads * DH, ROWS), BF16),
            kept((group, 1, ROWS), F32),
        ),
        in_specs=[pl.BlockSpec(memory_space=pltpu.SMEM)]
        + [pl.BlockSpec(memory_space=pltpu.VMEM)] * 3,
        compiler_params=room(8),
    )(where, a, b, s)


def turn_kernel(heads, att_ref, gain_ref, o_ref):
    for h in range(heads):
        span = slice(h * DH, (h + 1) * DH)
        o_ref[:, span] = att_ref[span].astype(F32).T * gain_ref[:, span]


def turn_call(attention, gain):
    return pl.pallas_call(
        functools.partial(turn_kernel, attention.shape[0] // DH),
        out_shape=kept(attention.shape[::-1], F32),
        compiler_params=room(8),
    )(attention, gain.reshape(1, -1))


def finish_kernel(heads, spread_ref, wide_ref, hyena_ref, o_ref):
    factor = lax.rsqrt(jnp.sum(spread_ref[...], axis=0) / WIDTH + 1e-06)
    factor = jnp.broadcast_to(factor, (DH, ROWS)).T
    for h in range(heads):
        span = slice(h * DH, (h + 1) * DH)
        o_ref[:, span] = (wide_ref[:, span] * factor + hyena_ref[:, span]).astype(BF16)


def finish_call(spread, wide, hyena_out):
    return pl.pallas_call(
        functools.partial(finish_kernel, wide.shape[1] // DH),
        out_shape=jax.ShapeDtypeStruct(wide.shape, BF16),
        compiler_params=room(8),
    )(spread, wide, hyena_out)


def gate_kernel(rim_ref, input_ref, filter_ref, o_ref, product):
    rim_rows = rim_ref.shape[1]
    product[8 - rim_rows : 8] = rim_ref[0].astype(F32) * rim_ref[1].astype(F32)
    product[8:] = input_ref[1].astype(F32) * input_ref[2].astype(F32)
    convolved = filter_ref[0:1] * product[8:]
    for tap in range(1, rim_rows + 1):
        convolved = convolved + filter_ref[tap : tap + 1] * product[8 - tap : 8 - tap + ROWS]
    o_ref[...] = input_ref[0].astype(F32) * convolved


def gate_call(rim, hyena_inputs, hyena_filter):
    width = hyena_filter.shape[1]
    return pl.pallas_call(
        gate_kernel,
        out_shape=kept((ROWS, width), F32),
        scratch_shapes=[pltpu.VMEM((8 + ROWS, width), F32)],
        compiler_params=room(8),
    )(rim, hyena_inputs, hyena_filter)


def rim_of(hyena_inputs, rim_rows):
    tails = hyena_inputs[1:, hyena_inputs.shape[1] - rim_rows :, :]
    size = lax.axis_size("ctx")
    return lax.ppermute(tails, "ctx", [(i, i + 1) for i in range(size - 1)])


def on_device(queries, keys, values, hyena_inputs, hyena_filter, norm_gain):
    ctx = lax.axis_index("ctx")
    x, z, c = ctx // (2 * Z), (ctx // 2) % Z, ctx % 2
    toward = 2 * c - 1
    own, own_all = prepare_call(keys, values, queries)
    other = lax.ppermute(own_all, "ctx", CORES)
    ring = lambda chunk: lax.ppermute(chunk, "ctx", RING)
    after = lambda chunk, token: lax.optimization_barrier((chunk, token))

    same, near_row, far_row = z * 2 * ROWS, c * ROWS, (1 - c) * ROWS
    blocks = [((z + step * toward) % Z) * 2 * ROWS for step in range(5)]
    where = jnp.stack(
        [x, same + near_row, same + far_row]
        + [block + near_row for block in blocks]
        + [block + far_row for block in blocks]
    ).astype(jnp.int32)

    above = lax.ppermute(queries, "ctx", DOWN)
    rim = rim_of(hyena_inputs, hyena_filter.shape[0] - 1)
    a0, b0 = own, other[:2]
    a1, b1 = ring(a0), ring(b0)
    a2, b2 = ring(a1), ring(b1)
    near = attend_call(
        where,
        (own_all, other, queries, queries),
        [(0, a0), (1, a1), (6, b1)],
        [(NEAR, (0, 1, 2), None)],
    )
    a2, stat, above, rim = lax.optimization_barrier((a2, near[1], above, rim))
    near = (near[0], stat)
    queries_all = (own_all, other, above, lax.ppermute(above, "ctx", CORES))
    a3, b3 = ring(a2), ring(b2)
    acc, stat = attend_call(
        where,
        queries_all,
        [(0, a0), (1, a1), (6, b1)],
        [(ABOVE, (0, 1, 2), None)],
    )
    a3, stat = after(a3, stat)
    a4 = ring(a3)
    *near, acc, stat = attend_call(
        where,
        queries_all,
        [(2, a2), (7, b2), (3, a3), (8, b3)],
        [(NEAR, (0, 1, 2, 3), near), (ABOVE, (0, 1, 2, 3), (acc, stat))],
    )
    near, far = attend_call(
        where,
        queries_all,
        [(4, a4)],
        [(NEAR, (0,), near), (ABOVE, (0,), (acc, stat))],
        True,
    )
    crossed = lax.ppermute(far, "ctx", CORES)
    rim, below = after(rim, merge_call(near, crossed))
    gate = gate_call(rim, hyena_inputs, hyena_filter)
    across = lax.ppermute(below, "ctx", UP)
    group = lax.axis_size("heads")
    attention, squares = combine_call(
        where, near, crossed, across, group
    )
    spread = lax.all_to_all(squares, "heads", 0, 0, tiled=True)
    wide = turn_call(attention, norm_gain)
    return finish_call(spread, wide, gate)


def solution(mesh):
    placed = (
        P("ctx", "heads"),
        P("ctx", "heads"),
        P("ctx", "heads"),
        P(None, "ctx", "heads"),
        P(None, "heads"),
        P("heads"),
    )
    return jax.shard_map(
        on_device, mesh=mesh, in_specs=placed, out_specs=P("ctx", "heads"), check_vma=False
    )
```

time: 582 us -> 102 us (0.18)
  the two profiles are of different devices: /device:TPU:454 before, /device:TPU:2 now
where the time goes in v2:
time: 102 us; the launch traced here: 101 us
  starting transfers between devices  44.1 us (43%)
  waiting for transfers between devices  38.9 us (38%)
  Pallas kernels  16 us (16%)
  local copies, waits for them, and re-layouts  1.55 us (2%)
    ppermute x7, starting transfers between devices, on_device(): ring = lambda chunk: lax.ppermute(chunk, 'ctx', RING)  20.4 us
    ppermute x7, waiting for transfers between devices, on_device(): ring = lambda chunk: lax.ppermute(chunk, 'ctx', RING)  18.8 us
    pallas_call x4, Pallas kernels, attend_call(): pl.pallas_call(functools.partial(attend_kernel, places, [(tiles, used, st...  11.4 us
    ppermute x1, waiting for transfers between devices, on_device(): across = lax.ppermute(below, 'ctx', UP)  9.92 us
    all_to_all x1, starting transfers between devices, on_device(): spread = lax.all_to_all(squares, 'heads', 0, 0, tiled=True)  9.19 us
    all_to_all x1, waiting for transfers between devices, on_device(): spread = lax.all_to_all(squares, 'heads', 0, 0, tiled=True)  8.31 us
    ppermute x1, starting transfers between devices, rim_of(): return lax.ppermute(tails, 'ctx', [(i, i + 1) for i in range(size - 1)])  4.18 us
    ppermute x1, starting transfers between devices, on_device(): above = lax.ppermute(queries, 'ctx', DOWN)  3.15 us
  transfers between devices with their start and end apart: 14, of which 8 were waited for; matrix products, arithmetic and copies ran while one was open for 1% of the time, Pallas kernels for 10%

profile of v2, /device:TPU:2, one launch (start us, length us, event | category | flops | bytes accessed | tf_op | source)
XLA Modules:
  0.0 101.0 jit_solution(11466502194163561530)
XLA Ops:
  0.0 1.2 %shard_map.64 = (bf16[2,256,512]{2,1,0:T(8,128)(2,1)S(1)}, bf16[3,256,512]{2,1,0:T(8,128)(2,1)S(1)}) custom-call(bf16[256,512]{1,0:T(8,128)(2,1)} %k_ref.1, bf16[256,512]{1,0:T(8,128)(2,1)} %v_ref.1, bf16[256,512]{1,0:T(8,128)(2,1)} %refs_3_.1), custom_call_target="tpu_custom_call" | custom-call | tf_op jit(solution)/shard_map/pallas_call | solution.py:82
  1.2 1.9 %collective-permute-start = (bf16[3,256,512]{2,1,0:T(8,128)(2,1)S(1)}, bf16[3,256,512]{2,1,0:T(8,128)(2,1)S(1)}, u32[]{:S(2)}, u32[]{:S(2)}) collective-permute-start(bf16[3,256,512]{2,1,0:T(8,128)(2,1)S(1)} %get-tuple-element.27.refs_0_), channel_id=1, source_target_pairs={{0,16},{16,0},{32,48},{48,32},{64,80},{80,64},{96,112},{112,96},{1... | collective-permute-start | bytes 2359304 | tf_op jit(solution)/shard_map/ppermute | solution.py:373
  3.2 0.0 copy-start
  3.2 4.4 %collective-permute-start.1 = (bf16[2,256,512]{2,1,0:T(8,128)(2,1)S(1)}, bf16[2,256,512]{2,1,0:T(8,128)(2,1)S(1)}, u32[]{:S(2)}, u32[]{:S(2)}) collective-permute-start(bf16[2,256,512]{2,1,0:T(8,128)(2,1)S(1)} %get-tuple-element.28.refs_4_), channel_id=1, source_target_pairs={{0,32},{16,240},{32,64},{48,16},{64,96},{80,48},{96,128},{112,80},... | collective-permute-start | bytes 1572872 | tf_op jit(solution)/shard_map/ppermute | solution.py:374
  7.6 0.0 collective-permute-done.refs_1_
  7.7 4.3 %collective-permute-start.3 = (bf16[2,256,512]{2,1,0:T(8,128)(2,1)S(1)}, bf16[2,256,512]{2,1,0:T(8,128)(2,1)S(1)}, u32[]{:S(2)}, u32[]{:S(2)}) collective-permute-start(bf16[2,256,512]{2,1,0:T(8,128)(2,1)S(1)} %slice.8), channel_id=1, source_target_pairs={{0,32},{16,240},{32,64},{48,16},{64,96},{80,48},{96,128},{112,80},... | collective-permute-start | bytes 1572872 | tf_op jit(solution)/shard_map/ppermute | solution.py:374
  11.9 9.5 %collective-permute-done.1.refs_5_ = bf16[2,256,512]{2,1,0:T(8,128)(2,1)S(1)} collective-permute-done((bf16[2,256,512]{2,1,0:T(8,128)(2,1)S(1)}, bf16[2,256,512]{2,1,0:T(8,128)(2,1)S(1)}, u32[]{:S(2)}, u32[]{:S(2)}) %collective-permute-start.1) | collective-permute-done | bytes 524320 | tf_op jit(solution)/shard_map/ppermute | solution.py:374
  21.4 1.9 %collective-permute-start.2 = (bf16[2,256,512]{2,1,0:T(8,128)(2,1)S(1)}, bf16[2,256,512]{2,1,0:T(8,128)(2,1)}, u32[]{:S(2)}, u32[]{:S(2)}) collective-permute-start(bf16[2,256,512]{2,1,0:T(8,128)(2,1)S(1)} %collective-permute-done.1.refs_5_), channel_id=1, source_target_pairs={{0,32},{16,240},{32,64},{48,16},{64,96},{80,48},{96,128},{112,80},... | collective-permute-start | bytes 1572872 | tf_op jit(solution)/shard_map/ppermute | solution.py:374
  23.3 0.0 copy-done
  23.3 3.2 %collective-permute-start.4 = (bf16[256,512]{1,0:T(8,128)(2,1)S(1)}, bf16[256,512]{1,0:T(8,128)(2,1)}, u32[]{:S(2)}, u32[]{:S(2)}) collective-permute-start(bf16[256,512]{1,0:T(8,128)(2,1)S(1)} %copy-done), channel_id=1, source_target_pairs={{256,0},{272,16},{288,32},{304,48},{320,64},{336,80},{352,96},{368... | collective-permute-start | bytes 786440 | tf_op jit(solution)/shard_map/ppermute | solution.py:385
  26.5 0.5 collective-permute-done.3.refs_6_
  27.0 1.9 %collective-permute-start.9 = (bf16[2,256,512]{2,1,0:T(8,128)(2,1)S(1)}, bf16[2,256,512]{2,1,0:T(8,128)(2,1)}, u32[]{:S(2)}, u32[]{:S(2)}) collective-permute-start(bf16[2,256,512]{2,1,0:T(8,128)(2,1)S(1)} %collective-permute-done.3.refs_6_), channel_id=1, source_target_pairs={{0,32},{16,240},{32,64},{48,16},{64,96},{80,48},{96,128},{112,80},... | collective-permute-start | bytes 1572872 | tf_op jit(solution)/shard_map/ppermute | solution.py:374
  29.0 0.7 slice.7
  29.7 4.2 %collective-permute-start.5 = (bf16[2,6,512]{2,1,0:T(8,128)(2,1)S(1)}, bf16[2,6,512]{2,1,0:T(8,128)(2,1)S(1)}, u32[]{:S(2)}, u32[]{:S(2)}) collective-permute-start(bf16[2,6,512]{2,1,0:T(8,128)(2,1)S(1)} %slice.7), channel_id=1, source_target_pairs={{0,16},{16,32},{32,48},{48,64},{64,80},{80,96},{96,112},{112,128},... | collective-permute-start | bytes 36872 | tf_op jit(solution)/shard_map/ppermute | solution.py:365
  34.0 0.1 stack.55.where_ref
  34.1 3.1 %shard_map.65 = (f32[2,512,256]{2,1,0:T(8,128)S(1)}, f32[2,8,256]{2,1,0:T(8,128)S(1)}) custom-call(s32[13]{0:T(128)S(1)} %stack.55.where_ref, bf16[3,256,512]{2,1,0:T(8,128)(2,1)S(1)} %get-tuple-element.27.refs_0_, bf16[3,256,512]{2,1,0:T(8,128)(2,1)S(1)} %collective-permute-done.refs_1_, bf16[256,512]{1,0:T(8,128)(2,1)S(1)} %copy-done, ...), custom_call_target="tpu_custom_call" | custom-call | flops 805306368 | bytes 3145728 | tf_op jit(solution)/shard_map/pallas_call | solution.py:221
  37.2 0.0 collective-permute-done.5.rim_ref
  37.2 0.0 collective-permute-done.4.refs_2_
  37.3 0.0 collective-permute-done.2.refs_4_
  37.3 2.8 %collective-permute-start.7 = (bf16[2,256,512]{2,1,0:T(8,128)(2,1)}, bf16[2,256,512]{2,1,0:T(8,128)(2,1)S(1)}, u32[]{:S(2)}, u32[]{:S(2)}) collective-permute-start(bf16[2,256,512]{2,1,0:T(8,128)(2,1)} %collective-permute-done.2.refs_4_), channel_id=1, source_target_pairs={{0,32},{16,240},{32,64},{48,16},{64,96},{80,48},{96,128},{112,80},... | collective-permute-start | bytes 1572872 | tf_op jit(solution)/shard_map/ppermute | solution.py:374
  40.1 1.9 %collective-permute-start.6 = (bf16[256,512]{1,0:T(8,128)(2,1)}, bf16[256,512]{1,0:T(8,128)(2,1)S(1)}, u32[]{:S(2)}, u32[]{:S(2)}) collective-permute-start(bf16[256,512]{1,0:T(8,128)(2,1)} %collective-permute-done.4.refs_2_), channel_id=1, source_target_pairs={{0,16},{16,0},{32,48},{48,32},{64,80},{80,64},{96,112},{112,96},{1... | collective-permute-start | bytes 786440 | tf_op jit(solution)/shard_map/ppermute | solution.py:398
  42.0 0.0 collective-permute-done.9.refs_5_
  42.0 3.1 %collective-permute-start.10 = (bf16[2,256,512]{2,1,0:T(8,128)(2,1)}, bf16[2,256,512]{2,1,0:T(8,128)(2,1)S(1)}, u32[]{:S(2)}, u32[]{:S(2)}) collective-permute-start(bf16[2,256,512]{2,1,0:T(8,128)(2,1)} %collective-permute-done.9.refs_5_), channel_id=1, source_target_pairs={{0,32},{16,240},{32,64},{48,16},{64,96},{80,48},{96,128},{112,80},... | collective-permute-start | bytes 1572872 | tf_op jit(solution)/shard_map/ppermute | solution.py:374
  45.2 0.0 collective-permute-done.6.refs_3_
  45.2 1.0 %shard_map.66 = (f32[2,512,256]{2,1,0:T(8,128)S(1)}, f32[2,8,256]{2,1,0:T(8,128)S(1)}) custom-call(s32[13]{0:T(128)S(1)} %stack.55.where_ref, bf16[3,256,512]{2,1,0:T(8,128)(2,1)S(1)} %get-tuple-element.27.refs_0_, bf16[3,256,512]{2,1,0:T(8,128)(2,1)S(1)} %collective-permute-done.refs_1_, bf16[256,512]{1,0:T(8,128)(2,1)} %collective-permute-done.4.refs_2_, ...), custom_call_target="tpu_custom_call" | custom-call | flops 805306368 | bytes 3145728 | tf_op jit(solution)/shard_map/pallas_call | solution.py:221
  46.2 3.5 %collective-permute-done.7.refs_6_ = bf16[2,256,512]{2,1,0:T(8,128)(2,1)S(1)} collective-permute-done((bf16[2,256,512]{2,1,0:T(8,128)(2,1)}, bf16[2,256,512]{2,1,0:T(8,128)(2,1)S(1)}, u32[]{:S(2)}, u32[]{:S(2)}) %collective-permute-start.7) | collective-permute-done | bytes 524320 | tf_op jit(solution)/shard_map/ppermute | solution.py:374
  49.8 1.9 %collective-permute-start.8 = (bf16[2,256,512]{2,1,0:T(8,128)(2,1)S(1)}, bf16[2,256,512]{2,1,0:T(8,128)(2,1)S(1)}, u32[]{:S(2)}, u32[]{:S(2)}) collective-permute-start(bf16[2,256,512]{2,1,0:T(8,128)(2,1)S(1)} %collective-permute-done.7.refs_6_), channel_id=1, source_target_pairs={{0,32},{16,240},{32,64},{48,16},{64,96},{80,48},{96,128},{112,80},... | collective-permute-start | bytes 1572872 | tf_op jit(solution)/shard_map/ppermute | solution.py:374
  51.7 3.7 %collective-permute-done.10.refs_7_ = bf16[2,256,512]{2,1,0:T(8,128)(2,1)S(1)} collective-permute-done((bf16[2,256,512]{2,1,0:T(8,128)(2,1)}, bf16[2,256,512]{2,1,0:T(8,128)(2,1)S(1)}, u32[]{:S(2)}, u32[]{:S(2)}) %collective-permute-start.10) | collective-permute-done | bytes 524320 | tf_op jit(solution)/shard_map/ppermute | solution.py:374
  55.4 5.1 %shard_map.67 = (f32[2,512,256]{2,1,0:T(8,128)S(1)}, f32[2,8,256]{2,1,0:T(8,128)S(1)}, f32[2,512,256]{2,1,0:T(8,128)S(1)}, f32[2,8,256]{2,1,0:T(8,128)S(1)}) custom-call(s32[13]{0:T(128)S(1)} %stack.55.where_ref, bf16[3,256,512]{2,1,0:T(8,128)(2,1)S(1)} %get-tuple-element.27.refs_0_, bf16[3,256,512]{2,1,0:T(8,128)(2,1)S(1)} %collective-permute-done.refs_1_, ...), custom_call_target="tpu_custom_call" | custom-call | flops 2147483648 | bytes 8388608 | tf_op jit(solution)/shard_map/pallas_call | solution.py:221
  60.5 1.5 %collective-permute-done.8.refs_4_ = bf16[2,256,512]{2,1,0:T(8,128)(2,1)S(1)} collective-permute-done((bf16[2,256,512]{2,1,0:T(8,128)(2,1)S(1)}, bf16[2,256,512]{2,1,0:T(8,128)(2,1)S(1)}, u32[]{:S(2)}, u32[]{:S(2)}) %collective-permute-start.8) | collective-permute-done | bytes 524320 | tf_op jit(solution)/shard_map/ppermute | solution.py:374
  62.0 2.1 %shard_map.68 = (bf16[2,528,256]{2,1,0:T(8,128)(2,1)S(1)}, bf16[2,528,256]{2,1,0:T(8,128)(2,1)S(1)}) custom-call(s32[13]{0:T(128)S(1)} %stack.55.where_ref, bf16[3,256,512]{2,1,0:T(8,128)(2,1)S(1)} %get-tuple-element.27.refs_0_, bf16[3,256,512]{2,1,0:T(8,128)(2,1)S(1)} %collective-permute-done.refs_1_, bf16[256,512]{1,0:T(8,128)(2,1)} %collective-permute-done.4.refs_2_, ...), custom_call_target="tpu_custom_call" | custom-call | flops 536870912 | bytes 2097152 | tf_op jit(solution)/shard_map/pallas_call | solution.py:221
  64.2 1.9 %collective-permute-start.11 = (bf16[2,528,256]{2,1,0:T(8,128)(2,1)S(1)}, bf16[2,528,256]{2,1,0:T(8,128)(2,1)S(1)}, u32[]{:S(2)}, u32[]{:S(2)}) collective-permute-start(bf16[2,528,256]{2,1,0:T(8,128)(2,1)S(1)} %get-tuple-element.43), channel_id=1, source_target_pairs={{0,16},{16,0},{32,48},{48,32},{64,80},{80,64},{96,112},{112,96},{1... | collective-permute-start | bytes 1622024 | tf_op jit(solution)/shard_map/ppermute | solution.py:421
  66.1 1.9 %collective-permute-done.11.b_ref = bf16[2,528,256]{2,1,0:T(8,128)(2,1)S(1)} collective-permute-done((bf16[2,528,256]{2,1,0:T(8,128)(2,1)S(1)}, bf16[2,528,256]{2,1,0:T(8,128)(2,1)S(1)}, u32[]{:S(2)}, u32[]{:S(2)}) %collective-permute-start.11) | collective-permute-done | bytes 540704 | tf_op jit(solution)/shard_map/ppermute | solution.py:421
  68.0 0.1 shard_map.69
  68.1 0.0 copy-start.1
  68.2 1.4 %collective-permute-start.12 = (bf16[528,256]{1,0:T(8,128)(2,1)S(1)}, bf16[528,256]{1,0:T(8,128)(2,1)S(1)}, u32[]{:S(2)}, u32[]{:S(2)}) collective-permute-start(bf16[528,256]{1,0:T(8,128)(2,1)S(1)} %shard_map.69), channel_id=1, source_target_pairs={{0,256},{16,272},{32,288},{48,304},{64,320},{80,336},{96,352},{112... | collective-permute-start | bytes 811016 | tf_op jit(solution)/shard_map/ppermute | solution.py:424
  69.6 9.9 %collective-permute-done.12.s_ref = bf16[528,256]{1,0:T(8,128)(2,1)S(1)} collective-permute-done((bf16[528,256]{1,0:T(8,128)(2,1)S(1)}, bf16[528,256]{1,0:T(8,128)(2,1)S(1)}, u32[]{:S(2)}, u32[]{:S(2)}) %collective-permute-start.12) | collective-permute-done | bytes 270368 | tf_op jit(solution)/shard_map/ppermute | solution.py:424
  79.5 1.4 %shard_map.70 = (bf16[512,256]{1,0:T(8,128)(2,1)S(1)}, f32[16,1,256]{2,1,0:T(1,128)}) custom-call(s32[13]{0:T(128)S(1)} %stack.55.where_ref, bf16[2,528,256]{2,1,0:T(8,128)(2,1)S(1)} %get-tuple-element.42.a_ref, bf16[2,528,256]{2,1,0:T(8,128)(2,1)S(1)} %collective-permute-done.11.b_ref, bf16[528,256]{1,0:T(8,128)(2,1)S(1)} %collective-permute-done.12.s_ref), custom_call_target="tpu_custom_call" | custom-call | tf_op jit(solution)/shard_map/pallas_call | solution.py:300
  80.9 0.0 copy-start.2
  80.9 9.2 %all-to-all-start = ((f32[16,1,256]{2,1,0:T(1,128)}), f32[16,1,256]{2,1,0:T(1,128)S(1)}, u32[]{:S(2)}, u32[]{:S(2)}) async-start(f32[16,1,256]{2,1,0:T(1,128)} %get-tuple-element.46), calls=%async_computation | async-start | bytes 32768 | tf_op jit(solution)/shard_map/all_to_all | solution.py:429
  90.1 0.0 copy-done.1
  90.1 0.0 copy-done.2
  90.1 0.8 shard_map.72.hyena_ref
  91.0 0.0 copy-start.3
  91.0 0.7 copy-done.3
  91.7 0.1 shard_map.71.wide_ref
  91.8 8.3 %all-to-all-done.spread_ref = f32[16,1,256]{2,1,0:T(1,128)S(1)} async-done(((f32[16,1,256]{2,1,0:T(1,128)}), f32[16,1,256]{2,1,0:T(1,128)S(1)}, u32[]{:S(2)}, u32[]{:S(2)}) %all-to-all-start) | async-done | bytes 16416 | tf_op jit(solution)/shard_map/all_to_all | solution.py:429
  100.1 0.9 shard_map.73
  (1 shorter events, 0.0 us)
Async XLA Ops:
  1.2 6.4 %collective-permute-start = (bf16[3,256,512]{2,1,0:T(8,128)(2,1)S(1)}, bf16[3,256,512]{2,1,0:T(8,128)(2,1)S(1)}, u32[]{:S(2)}, u32[]{:S(2)}) collective-permute-start(bf16[3,256,512]{2,1,0:T(8,128)(2,1)S(1)} %get-tuple-element.27.refs_0_), channel_id=1, source_target_pairs={{0,16},{16,0},{32,48},{48,32},{64,80},{80,64},{96,112},{112,96},{1... | collective-permute-start | bytes 2359304 | tf_op jit(solution)/shard_map/ppermute | solution.py:373
  3.2 20.2 %copy-start = (bf16[256,512]{1,0:T(8,128)(2,1)S(1)}, bf16[256,512]{1,0:T(8,128)(2,1)}, u32[]{:S(2)}) copy-start(bf16[256,512]{1,0:T(8,128)(2,1)} %refs_3_.1) | copy-start | bytes 786436
  3.2 18.2 %collective-permute-start.1 = (bf16[2,256,512]{2,1,0:T(8,128)(2,1)S(1)}, bf16[2,256,512]{2,1,0:T(8,128)(2,1)S(1)}, u32[]{:S(2)}, u32[]{:S(2)}) collective-permute-start(bf16[2,256,512]{2,1,0:T(8,128)(2,1)S(1)} %get-tuple-element.28.refs_4_), channel_id=1, source_target_pairs={{0,32},{16,240},{32,64},{48,16},{64,96},{80,48},{96,128},{112,80},... | collective-permute-start | bytes 1572872 | tf_op jit(solution)/shard_map/ppermute | solution.py:374
  7.7 19.4 %collective-permute-start.3 = (bf16[2,256,512]{2,1,0:T(8,128)(2,1)S(1)}, bf16[2,256,512]{2,1,0:T(8,128)(2,1)S(1)}, u32[]{:S(2)}, u32[]{:S(2)}) collective-permute-start(bf16[2,256,512]{2,1,0:T(8,128)(2,1)S(1)} %slice.8), channel_id=1, source_target_pairs={{0,32},{16,240},{32,64},{48,16},{64,96},{80,48},{96,128},{112,80},... | collective-permute-start | bytes 1572872 | tf_op jit(solution)/shard_map/ppermute | solution.py:374
  21.4 15.8 %collective-permute-start.2 = (bf16[2,256,512]{2,1,0:T(8,128)(2,1)S(1)}, bf16[2,256,512]{2,1,0:T(8,128)(2,1)}, u32[]{:S(2)}, u32[]{:S(2)}) collective-permute-start(bf16[2,256,512]{2,1,0:T(8,128)(2,1)S(1)} %collective-permute-done.1.refs_5_), channel_id=1, source_target_pairs={{0,32},{16,240},{32,64},{48,16},{64,96},{80,48},{96,128},{112,80},... | collective-permute-start | bytes 1572872 | tf_op jit(solution)/shard_map/ppermute | solution.py:374
  23.3 13.9 %collective-permute-start.4 = (bf16[256,512]{1,0:T(8,128)(2,1)S(1)}, bf16[256,512]{1,0:T(8,128)(2,1)}, u32[]{:S(2)}, u32[]{:S(2)}) collective-permute-start(bf16[256,512]{1,0:T(8,128)(2,1)S(1)} %copy-done), channel_id=1, source_target_pairs={{256,0},{272,16},{288,32},{304,48},{320,64},{336,80},{352,96},{368... | collective-permute-start | bytes 786440 | tf_op jit(solution)/shard_map/ppermute | solution.py:385
  27.0 15.0 %collective-permute-start.9 = (bf16[2,256,512]{2,1,0:T(8,128)(2,1)S(1)}, bf16[2,256,512]{2,1,0:T(8,128)(2,1)}, u32[]{:S(2)}, u32[]{:S(2)}) collective-permute-start(bf16[2,256,512]{2,1,0:T(8,128)(2,1)S(1)} %collective-permute-done.3.refs_6_), channel_id=1, source_target_pairs={{0,32},{16,240},{32,64},{48,16},{64,96},{80,48},{96,128},{112,80},... | collective-permute-start | bytes 1572872 | tf_op jit(solution)/shard_map/ppermute | solution.py:374
  29.7 7.6 %collective-permute-start.5 = (bf16[2,6,512]{2,1,0:T(8,128)(2,1)S(1)}, bf16[2,6,512]{2,1,0:T(8,128)(2,1)S(1)}, u32[]{:S(2)}, u32[]{:S(2)}) collective-permute-start(bf16[2,6,512]{2,1,0:T(8,128)(2,1)S(1)} %slice.7), channel_id=1, source_target_pairs={{0,16},{16,32},{32,48},{48,64},{64,80},{80,96},{96,112},{112,128},... | collective-permute-start | bytes 36872 | tf_op jit(solution)/shard_map/ppermute | solution.py:365
  37.3 12.5 %collective-permute-start.7 = (bf16[2,256,512]{2,1,0:T(8,128)(2,1)}, bf16[2,256,512]{2,1,0:T(8,128)(2,1)S(1)}, u32[]{:S(2)}, u32[]{:S(2)}) collective-permute-start(bf16[2,256,512]{2,1,0:T(8,128)(2,1)} %collective-permute-done.2.refs_4_), channel_id=1, source_target_pairs={{0,32},{16,240},{32,64},{48,16},{64,96},{80,48},{96,128},{112,80},... | collective-permute-start | bytes 1572872 | tf_op jit(solution)/shard_map/ppermute | solution.py:374
  40.1 5.1 %collective-permute-start.6 = (bf16[256,512]{1,0:T(8,128)(2,1)}, bf16[256,512]{1,0:T(8,128)(2,1)S(1)}, u32[]{:S(2)}, u32[]{:S(2)}) collective-permute-start(bf16[256,512]{1,0:T(8,128)(2,1)} %collective-permute-done.4.refs_2_), channel_id=1, source_target_pairs={{0,16},{16,0},{32,48},{48,32},{64,80},{80,64},{96,112},{112,96},{1... | collective-permute-start | bytes 786440 | tf_op jit(solution)/shard_map/ppermute | solution.py:398
  42.0 13.3 %collective-permute-start.10 = (bf16[2,256,512]{2,1,0:T(8,128)(2,1)}, bf16[2,256,512]{2,1,0:T(8,128)(2,1)S(1)}, u32[]{:S(2)}, u32[]{:S(2)}) collective-permute-start(bf16[2,256,512]{2,1,0:T(8,128)(2,1)} %collective-permute-done.9.refs_5_), channel_id=1, source_target_pairs={{0,32},{16,240},{32,64},{48,16},{64,96},{80,48},{96,128},{112,80},... | collective-permute-start | bytes 1572872 | tf_op jit(solution)/shard_map/ppermute | solution.py:374
  49.8 12.3 %collective-permute-start.8 = (bf16[2,256,512]{2,1,0:T(8,128)(2,1)S(1)}, bf16[2,256,512]{2,1,0:T(8,128)(2,1)S(1)}, u32[]{:S(2)}, u32[]{:S(2)}) collective-permute-start(bf16[2,256,512]{2,1,0:T(8,128)(2,1)S(1)} %collective-permute-done.7.refs_6_), channel_id=1, source_target_pairs={{0,32},{16,240},{32,64},{48,16},{64,96},{80,48},{96,128},{112,80},... | collective-permute-start | bytes 1572872 | tf_op jit(solution)/shard_map/ppermute | solution.py:374
  64.2 3.8 %collective-permute-start.11 = (bf16[2,528,256]{2,1,0:T(8,128)(2,1)S(1)}, bf16[2,528,256]{2,1,0:T(8,128)(2,1)S(1)}, u32[]{:S(2)}, u32[]{:S(2)}) collective-permute-start(bf16[2,528,256]{2,1,0:T(8,128)(2,1)S(1)} %get-tuple-element.43), channel_id=1, source_target_pairs={{0,16},{16,0},{32,48},{48,32},{64,80},{80,64},{96,112},{112,96},{1... | collective-permute-start | bytes 1622024 | tf_op jit(solution)/shard_map/ppermute | solution.py:421
  68.1 22.0 %copy-start.1 = (bf16[3,256,512]{2,1,0:T(8,128)(2,1)S(1)}, bf16[3,256,512]{2,1,0:T(8,128)(2,1)}, u32[]{:S(2)}) copy-start(bf16[3,256,512]{2,1,0:T(8,128)(2,1)} %input_ref.1) | copy-start | bytes 2359300
  68.2 11.4 %collective-permute-start.12 = (bf16[528,256]{1,0:T(8,128)(2,1)S(1)}, bf16[528,256]{1,0:T(8,128)(2,1)S(1)}, u32[]{:S(2)}, u32[]{:S(2)}) collective-permute-start(bf16[528,256]{1,0:T(8,128)(2,1)S(1)} %shard_map.69), channel_id=1, source_target_pairs={{0,256},{16,272},{32,288},{48,304},{64,320},{80,336},{96,352},{112... | collective-permute-start | bytes 811016 | tf_op jit(solution)/shard_map/ppermute | solution.py:424
  80.9 9.2 %copy-start.2 = (f32[7,512]{1,0:T(8,128)S(1)}, f32[7,512]{1,0:T(8,128)}, u32[]{:S(2)}) copy-start(f32[7,512]{1,0:T(8,128)} %filter_ref.1) | copy-start | bytes 43012
  80.9 19.2 %all-to-all-start = ((f32[16,1,256]{2,1,0:T(1,128)}), f32[16,1,256]{2,1,0:T(1,128)S(1)}, u32[]{:S(2)}, u32[]{:S(2)}) async-start(f32[16,1,256]{2,1,0:T(1,128)} %get-tuple-element.46), calls=%async_computation | async-start | bytes 32768 | tf_op jit(solution)/shard_map/all_to_all | solution.py:429
  91.0 0.7 copy-start.3

commit v3 on v2

--- a/solution.py
+++ b/solution.py
@@ -28,6 +28,7 @@
 ]
 CORES = [(chip(x, z, c), chip(x, z, 1 - c)) for x in range(2) for z in range(Z) for c in range(2)]
 DOWN = [(chip(1, z, c), chip(0, z, c)) for z in range(Z) for c in range(2)]
+CROSS = [(chip(1, z, c), chip(0, z, 1 - c)) for z in range(Z) for c in range(2)]
 UP = [(chip(0, z, c), chip(1, z, c)) for z in range(Z) for c in range(2)]
 
 
@@ -54,36 +55,45 @@
     return high, middle, rest - middle
 
 
-def prepare_kernel(heads, k_ref, v_ref, q_ref, pair_ref, triple_ref, held, sems):
+def corner(h):
+    return slice(h % 2 * DH, (h % 2 + 1) * DH), slice(h // 2 * ROWS, (h // 2 + 1) * ROWS)
+
+
+def prepare_kernel(heads, k_ref, v_ref, q_ref, pair_ref, triple_ref, turned_ref, held, sems):
     copies = [
         pltpu.make_async_copy(source, target, sems.at[number])
         for number, (source, target) in enumerate(
             (
-                (v_ref, held),
+                (v_ref, held.at[0]),
+                (q_ref, held.at[1]),
                 (k_ref, pair_ref.at[0]),
                 (k_ref, triple_ref.at[0]),
-                (q_ref, triple_ref.at[2]),
             )
         )
     ]
     for copy in copies:
         copy.start()
-    copies[0].wait()
-    for h in range(heads):
-        turned = held[:, h * DH : (h + 1) * DH].T
-        place = (slice(h % 2 * DH, (h % 2 + 1) * DH), slice(h // 2 * ROWS, (h // 2 + 1) * ROWS))
-        for ref in (pair_ref, triple_ref):
-            ref[(1, *place)] = turned
-    for copy in copies[1:]:
+    for number, refs in enumerate(
+        ((pair_ref.at[1], triple_ref.at[1]), (triple_ref.at[2], turned_ref))
+    ):
+        copies[number].wait()
+        for h in range(heads):
+            turned = held[number, :, h * DH : (h + 1) * DH].T
+            for ref in refs:
+                ref[corner(h)] = turned
+    for copy in copies[2:]:
         copy.wait()
 
 
 def prepare_call(keys, values, queries):
     return pl.pallas_call(
         functools.partial(prepare_kernel, keys.shape[1] // DH),
-        out_shape=tuple(kept((n, *keys.shape), BF16) for n in (2, 3)),
+        out_shape=(
+            *(kept((n, *keys.shape), BF16) for n in (2, 3)),
+            kept(queries.shape, BF16),
+        ),
         in_specs=[pl.BlockSpec(memory_space=pl.ANY)] * 3,
-        scratch_shapes=[pltpu.VMEM(values.shape, BF16), pltpu.SemaphoreType.DMA((4,))],
+        scratch_shapes=[pltpu.VMEM((2, *values.shape), BF16), pltpu.SemaphoreType.DMA((4,))],
         compiler_params=room(56),
     )(keys, values, queries)
 
@@ -110,10 +120,9 @@
             spans = [slice(h * DH, (h + 1) * DH) for h in range(heads)]
             scores = [
                 [
-                    lax.dot_general(
+                    jnp.dot(
                         chunk[0, :, spans[h]],
-                        query_refs[tile][:, spans[h]],
-                        (((1,), (1,)), ((), ())),
+                        query_refs[tile][corner(h)],
                         preferred_element_type=F32,
                     )
                     for chunk in chunks
@@ -153,7 +162,7 @@
                     jnp.add,
                     [
                         jnp.dot(
-                            chunk[1, h % 2 * DH : (h % 2 + 1) * DH, h // 2 * ROWS : (h // 2 + 1) * ROWS],
+                            chunk[(1, *corner(h))],
                             weight.astype(BF16),
                             preferred_element_type=F32,
                         )
@@ -320,7 +329,7 @@
         functools.partial(turn_kernel, attention.shape[0] // DH),
         out_shape=kept(attention.shape[::-1], F32),
         compiler_params=room(8),
-    )(attention, gain.reshape(1, -1))
+    )(attention, gain)
 
 
 def finish_kernel(heads, spread_ref, wide_ref, hyena_ref, o_ref):
@@ -339,7 +348,8 @@
     )(spread, wide, hyena_out)
 
 
-def gate_kernel(rim_ref, input_ref, filter_ref, o_ref, product):
+def gate_kernel(rim_ref, input_ref, filter_ref, gain_ref, o_ref, gain_out, product):
+    gain_out[...] = gain_ref[...]
     rim_rows = rim_ref.shape[1]
     product[8 - rim_rows : 8] = rim_ref[0].astype(F32) * rim_ref[1].astype(F32)
     product[8:] = input_ref[1].astype(F32) * input_ref[2].astype(F32)
@@ -349,18 +359,17 @@
     o_ref[...] = input_ref[0].astype(F32) * convolved
 
 
-def gate_call(rim, hyena_inputs, hyena_filter):
+def gate_call(rim, hyena_inputs, hyena_filter, gain):
     width = hyena_filter.shape[1]
     return pl.pallas_call(
         gate_kernel,
-        out_shape=kept((ROWS, width), F32),
+        out_shape=(kept((ROWS, width), F32), kept((1, width), F32)),
         scratch_shapes=[pltpu.VMEM((8 + ROWS, width), F32)],
         compiler_params=room(8),
-    )(rim, hyena_inputs, hyena_filter)
-
-
-def rim_of(hyena_inputs, rim_rows):
-    tails = hyena_inputs[1:, hyena_inputs.shape[1] - rim_rows :, :]
+    )(rim, hyena_inputs, hyena_filter, gain.reshape(1, -1))
+
+
+def rim_of(tails):
     size = lax.axis_size("ctx")
     return lax.ppermute(tails, "ctx", [(i, i + 1) for i in range(size - 1)])
 
@@ -369,7 +378,7 @@
     ctx = lax.axis_index("ctx")
     x, z, c = ctx // (2 * Z), (ctx // 2) % Z, ctx % 2
     toward = 2 * c - 1
-    own, own_all = prepare_call(keys, values, queries)
+    own, own_all, turned = prepare_call(keys, values, queries)
     other = lax.ppermute(own_all, "ctx", CORES)
     ring = lambda chunk: lax.ppermute(chunk, "ctx", RING)
     after = lambda chunk, token: lax.optimization_barrier((chunk, token))
@@ -382,34 +391,33 @@
         + [block + far_row for block in blocks]
     ).astype(jnp.int32)
 
-    above = lax.ppermute(queries, "ctx", DOWN)
-    rim = rim_of(hyena_inputs, hyena_filter.shape[0] - 1)
+    queries_near = (own_all, other, turned, turned)
+    above = lax.ppermute(turned, "ctx", DOWN)
     a0, b0 = own, other[:2]
     a1, b1 = ring(a0), ring(b0)
-    a2, b2 = ring(a1), ring(b1)
+    acc, stat = attend_call(where, queries_near, [(0, a0)], [(NEAR, (0,), None)])
+    a1, stat, above = lax.optimization_barrier((a1, stat, above))
+    queries_all = (own_all, other, above, lax.ppermute(above, "ctx", CORES))
+    a2 = ring(a1)
+    acc, stat = attend_call(where, queries_near, [(1, a1)], [(NEAR, (0,), (acc, stat))])
+    b1, stat = after(b1, stat)
+    b2 = ring(b1)
+    high = attend_call(where, queries_all, [(0, a0), (1, a1)], [(ABOVE, (0, 1), None)])
+    a2, mark = after(a2, high[1])
+    a3, b3 = ring(a2), ring(b2)
     near = attend_call(
         where,
-        (own_all, other, queries, queries),
-        [(0, a0), (1, a1), (6, b1)],
-        [(NEAR, (0, 1, 2), None)],
-    )
-    a2, stat, above, rim = lax.optimization_barrier((a2, near[1], above, rim))
-    near = (near[0], stat)
-    queries_all = (own_all, other, above, lax.ppermute(above, "ctx", CORES))
-    a3, b3 = ring(a2), ring(b2)
-    acc, stat = attend_call(
-        where,
-        queries_all,
-        [(0, a0), (1, a1), (6, b1)],
-        [(ABOVE, (0, 1, 2), None)],
-    )
-    a3, stat = after(a3, stat)
+        queries_near,
+        [(6, b1), (2, a2), (7, b2)],
+        [(NEAR, (0, 1, 2), (acc, stat))],
+    )
+    a3, stat = after(a3, near[1])
     a4 = ring(a3)
     *near, acc, stat = attend_call(
         where,
         queries_all,
-        [(2, a2), (7, b2), (3, a3), (8, b3)],
-        [(NEAR, (0, 1, 2, 3), near), (ABOVE, (0, 1, 2, 3), (acc, stat))],
+        [(6, b1), (2, a2), (7, b2), (3, a3), (8, b3)],
+        [(NEAR, (3, 4), (near[0], stat)), (ABOVE, (0, 1, 2, 3, 4), (high[0], mark))],
     )
     near, far = attend_call(
         where,
@@ -419,15 +427,17 @@
         True,
     )
     crossed = lax.ppermute(far, "ctx", CORES)
-    rim, below = after(rim, merge_call(near, crossed))
-    gate = gate_call(rim, hyena_inputs, hyena_filter)
-    across = lax.ppermute(below, "ctx", UP)
+    tails = hyena_inputs[1:, ROWS - hyena_filter.shape[0] + 1 :, :]
+    tails, below = after(tails, merge_call(near, crossed))
+    rim = rim_of(tails)
+    gate, gain = gate_call(rim, hyena_inputs, hyena_filter, norm_gain)
+    across, gain = after(lax.ppermute(below, "ctx", UP), gain)
     group = lax.axis_size("heads")
     attention, squares = combine_call(
         where, near, crossed, across, group
     )
     spread = lax.all_to_all(squares, "heads", 0, 0, tiled=True)
-    wide = turn_call(attention, norm_gain)
+    wide = turn_call(attention, gain)
     return finish_call(spread, wide, gate)
 
 

time: 102 us -> 99.4 us (0.975)
  starting transfers between devices: 44.1 us -> 41.7 us
    ppermute x2, waiting for transfers between devices: 9.93 us -> 2.81 us  [the longest x1 2.81 us: on_device(): across, gain = after(lax.ppermute(below, 'ctx', UP), gain)]
    ppermute x1, waiting for transfers between devices: 0.01 us -> 5.32 us  [rim_of(): return lax.ppermute(tails, 'ctx', [(i, i + 1) for i in range(size - 1)])]
    ppermute x7, starting transfers between devices: 20.4 us -> 15.8 us  [on_device(): ring = lambda chunk: lax.ppermute(chunk, 'ctx', RING)]
    ppermute x1, starting transfers between devices: 1.92 us -> 4.19 us  [on_device(): queries_all = (own_all, other, above, lax.ppermute(above, 'ctx', CORES))]
    ppermute x2, starting transfers between devices: 4.57 us -> 6.76 us  [the longest x1 5.47 us: on_device(): above = lax.ppermute(turned, 'ctx', DOWN)]
    ppermute x1, starting transfers between devices: 4.18 us -> 2.04 us  [rim_of(): return lax.ppermute(tails, 'ctx', [(i, i + 1) for i in range(size - 1)])]
    all_to_all x1, waiting for transfers between devices: 8.31 us -> 9.84 us  [on_device(): spread = lax.all_to_all(squares, 'heads', 0, 0, tiled=True)]
    pallas_call x4 -> x6, Pallas kernels: 11.4 us -> 12.4 us  [attend_call(): pl.pallas_call(functools.partial(attend_kernel, places, [(tiles, used, st...]
  transfers between devices with their start and end apart: 14 -> 14, of which waited for: 8 -> 9; matrix products, arithmetic and copies ran while one was open for 1% -> 1% of each run, Pallas kernels for 10% -> 12%
where the time goes in v3:
time: 99.4 us; the launch traced here: 98.8 us
  starting transfers between devices  41.7 us (42%)
  waiting for transfers between devices  38.8 us (39%)
  Pallas kernels  17 us (17%)
    ppermute x7, waiting for transfers between devices, on_device(): ring = lambda chunk: lax.ppermute(chunk, 'ctx', RING)  19 us
    ppermute x7, starting transfers between devices, on_device(): ring = lambda chunk: lax.ppermute(chunk, 'ctx', RING)  15.8 us
    pallas_call x6, Pallas kernels, attend_call(): pl.pallas_call(functools.partial(attend_kernel, places, [(tiles, used, st...  12.4 us
    all_to_all x1, waiting for transfers between devices, on_device(): spread = lax.all_to_all(squares, 'heads', 0, 0, tiled=True)  9.84 us
    all_to_all x1, starting transfers between devices, on_device(): spread = lax.all_to_all(squares, 'heads', 0, 0, tiled=True)  9.06 us
    ppermute x1, starting transfers between devices, on_device(): above = lax.ppermute(turned, 'ctx', DOWN)  5.47 us
    ppermute x1, waiting for transfers between devices, rim_of(): return lax.ppermute(tails, 'ctx', [(i, i + 1) for i in range(size - 1)])  5.32 us
    ppermute x1, starting transfers between devices, on_device(): queries_all = (own_all, other, above, lax.ppermute(above, 'ctx', CORES))  4.19 us
  transfers between devices with their start and end apart: 14, of which 9 were waited for; matrix products, arithmetic and copies ran while one was open for 1% of the time, Pallas kernels for 12%

profile of v3, /device:TPU:2, one launch (start us, length us, event | category | flops | bytes accessed | tf_op | source)
XLA Modules:
  0.0 98.8 jit_solution(9492418882719432907)
XLA Ops:
  0.0 1.2 %shard_map.64 = (bf16[2,256,512]{2,1,0:T(8,128)(2,1)S(1)}, bf16[3,256,512]{2,1,0:T(8,128)(2,1)S(1)}, bf16[256,512]{1,0:T(8,128)(2,1)S(1)}) custom-call(bf16[256,512]{1,0:T(8,128)(2,1)} %k_ref.1, bf16[256,512]{1,0:T(8,128)(2,1)} %v_ref.1, bf16[256,512]{1,0:T(8,128)(2,1)} %q_ref.1), custom_call_target="tpu_custom_call" | custom-call | tf_op jit(solution)/shard_map/pallas_call | solution.py:89
  1.2 1.9 %collective-permute-start = (bf16[3,256,512]{2,1,0:T(8,128)(2,1)S(1)}, bf16[3,256,512]{2,1,0:T(8,128)(2,1)S(1)}, u32[]{:S(2)}, u32[]{:S(2)}) collective-permute-start(bf16[3,256,512]{2,1,0:T(8,128)(2,1)S(1)} %get-tuple-element.39.refs_0_), channel_id=1, source_target_pairs={{0,16},{16,0},{32,48},{48,32},{64,80},{80,64},{96,112},{112,96},{1... | collective-permute-start | bytes 2359304 | tf_op jit(solution)/shard_map/ppermute | solution.py:382
  3.2 4.3 %collective-permute-start.1 = (bf16[2,256,512]{2,1,0:T(8,128)(2,1)S(1)}, bf16[2,256,512]{2,1,0:T(8,128)(2,1)S(1)}, u32[]{:S(2)}, u32[]{:S(2)}) collective-permute-start(bf16[2,256,512]{2,1,0:T(8,128)(2,1)S(1)} %get-tuple-element.40.refs_4_), channel_id=1, source_target_pairs={{0,32},{16,240},{32,64},{48,16},{64,96},{80,48},{96,128},{112,80},... | collective-permute-start | bytes 1572872 | tf_op jit(solution)/shard_map/ppermute | solution.py:383
  7.5 5.5 %collective-permute-start.2 = (bf16[256,512]{1,0:T(8,128)(2,1)S(1)}, bf16[256,512]{1,0:T(8,128)(2,1)S(1)}, u32[]{:S(2)}, u32[]{:S(2)}) collective-permute-start(bf16[256,512]{1,0:T(8,128)(2,1)S(1)} %get-tuple-element.41.refs_2_.refs_3_), channel_id=1, source_target_pairs={{256,0},{272,16},{288,32},{304,48},{320,64},{336,80},{352,96},{368... | collective-permute-start | bytes 786440 | tf_op jit(solution)/shard_map/ppermute | solution.py:395
  12.9 0.0 collective-permute-done.refs_1_
  12.9 0.8 slice.8
  13.8 1.9 %collective-permute-start.6 = (bf16[2,256,512]{2,1,0:T(8,128)(2,1)}, bf16[2,256,512]{2,1,0:T(8,128)(2,1)}, u32[]{:S(2)}, u32[]{:S(2)}) collective-permute-start(bf16[2,256,512]{2,1,0:T(8,128)(2,1)} %slice.8), channel_id=1, source_target_pairs={{0,32},{16,240},{32,64},{48,16},{64,96},{80,48},{96,128},{112,80},... | collective-permute-start | bytes 1572872 | tf_op jit(solution)/shard_map/ppermute | solution.py:383
  15.8 0.1 stack.55.where_ref
  15.9 1.5 %shard_map.65 = (f32[2,512,256]{2,1,0:T(8,128)S(1)}, f32[2,8,256]{2,1,0:T(8,128)S(1)}) custom-call(s32[13]{0:T(128)S(1)} %stack.55.where_ref, bf16[3,256,512]{2,1,0:T(8,128)(2,1)S(1)} %get-tuple-element.39.refs_0_, bf16[3,256,512]{2,1,0:T(8,128)(2,1)S(1)} %collective-permute-done.refs_1_, bf16[256,512]{1,0:T(8,128)(2,1)S(1)} %get-tuple-element.41.refs_2_.refs_3_, ...), custom_call_target="tpu_custom_call" | custom-call | flops 268435456 | bytes 1048576 | tf_op jit(solution)/shard_map/pallas_call | solution.py:230
  17.5 0.0 collective-permute-done.2.refs_2_
  17.5 3.8 %collective-permute-done.1.refs_5_.refs_4_ = bf16[2,256,512]{2,1,0:T(8,128)(2,1)S(1)} collective-permute-done((bf16[2,256,512]{2,1,0:T(8,128)(2,1)S(1)}, bf16[2,256,512]{2,1,0:T(8,128)(2,1)S(1)}, u32[]{:S(2)}, u32[]{:S(2)}) %collective-permute-start.1) | collective-permute-done | bytes 524320 | tf_op jit(solution)/shard_map/ppermute | solution.py:383
  21.3 1.9 %collective-permute-start.4 = (bf16[2,256,512]{2,1,0:T(8,128)(2,1)S(1)}, bf16[2,256,512]{2,1,0:T(8,128)(2,1)S(1)}, u32[]{:S(2)}, u32[]{:S(2)}) collective-permute-start(bf16[2,256,512]{2,1,0:T(8,128)(2,1)S(1)} %collective-permute-done.1.refs_5_.refs_4_), channel_id=1, source_target_pairs={{0,32},{16,240},{32,64},{48,16},{64,96},{80,48},{96,128},{112,80},... | collective-permute-start | bytes 1572872 | tf_op jit(solution)/shard_map/ppermute | solution.py:383
  23.2 4.2 %collective-permute-start.3 = (bf16[256,512]{1,0:T(8,128)(2,1)S(1)}, bf16[256,512]{1,0:T(8,128)(2,1)S(1)}, u32[]{:S(2)}, u32[]{:S(2)}) collective-permute-start(bf16[256,512]{1,0:T(8,128)(2,1)S(1)} %collective-permute-done.2.refs_2_), channel_id=1, source_target_pairs={{0,16},{16,0},{32,48},{48,32},{64,80},{80,64},{96,112},{112,96},{1... | collective-permute-start | bytes 786440 | tf_op jit(solution)/shard_map/ppermute | solution.py:400
  27.4 1.6 %shard_map.67 = (f32[2,512,256]{2,1,0:T(8,128)S(1)}, f32[2,8,256]{2,1,0:T(8,128)S(1)}) custom-call(s32[13]{0:T(128)S(1)} %stack.55.where_ref, bf16[3,256,512]{2,1,0:T(8,128)(2,1)S(1)} %get-tuple-element.39.refs_0_, bf16[3,256,512]{2,1,0:T(8,128)(2,1)S(1)} %collective-permute-done.refs_1_, bf16[256,512]{1,0:T(8,128)(2,1)S(1)} %get-tuple-element.41.refs_2_.refs_3_, ...), custom_call_target="tpu_custom_call" | custom-call | flops 268435456 | bytes 1048576 | tf_op jit(solution)/shard_map/pallas_call | solution.py:230
  29.0 0.0 collective-permute-done.6.refs_4_
  29.0 1.9 %collective-permute-start.7 = (bf16[2,256,512]{2,1,0:T(8,128)(2,1)}, bf16[2,256,512]{2,1,0:T(8,128)(2,1)S(1)}, u32[]{:S(2)}, u32[]{:S(2)}) collective-permute-start(bf16[2,256,512]{2,1,0:T(8,128)(2,1)} %collective-permute-done.6.refs_4_), channel_id=1, source_target_pairs={{0,32},{16,240},{32,64},{48,16},{64,96},{80,48},{96,128},{112,80},... | collective-permute-start | bytes 1572872 | tf_op jit(solution)/shard_map/ppermute | solution.py:383
  30.9 0.0 collective-permute-done.3.refs_3_
  30.9 0.6 shard_map.66
  31.6 2.0 %collective-permute-done.4.refs_5_ = bf16[2,256,512]{2,1,0:T(8,128)(2,1)S(1)} collective-permute-done((bf16[2,256,512]{2,1,0:T(8,128)(2,1)S(1)}, bf16[2,256,512]{2,1,0:T(8,128)(2,1)S(1)}, u32[]{:S(2)}, u32[]{:S(2)}) %collective-permute-start.4) | collective-permute-done | bytes 524320 | tf_op jit(solution)/shard_map/ppermute | solution.py:383
  33.5 1.9 %collective-permute-start.5 = (bf16[2,256,512]{2,1,0:T(8,128)(2,1)S(1)}, bf16[2,256,512]{2,1,0:T(8,128)(2,1)S(1)}, u32[]{:S(2)}, u32[]{:S(2)}) collective-permute-start(bf16[2,256,512]{2,1,0:T(8,128)(2,1)S(1)} %collective-permute-done.4.refs_5_), channel_id=1, source_target_pairs={{0,32},{16,240},{32,64},{48,16},{64,96},{80,48},{96,128},{112,80},... | collective-permute-start | bytes 1572872 | tf_op jit(solution)/shard_map/ppermute | solution.py:383
  35.5 6.0 %collective-permute-done.7.refs_6_ = bf16[2,256,512]{2,1,0:T(8,128)(2,1)S(1)} collective-permute-done((bf16[2,256,512]{2,1,0:T(8,128)(2,1)}, bf16[2,256,512]{2,1,0:T(8,128)(2,1)S(1)}, u32[]{:S(2)}, u32[]{:S(2)}) %collective-permute-start.7) | collective-permute-done | bytes 524320 | tf_op jit(solution)/shard_map/ppermute | solution.py:383
  41.5 1.9 %collective-permute-start.9 = (bf16[2,256,512]{2,1,0:T(8,128)(2,1)S(1)}, bf16[2,256,512]{2,1,0:T(8,128)(2,1)S(1)}, u32[]{:S(2)}, u32[]{:S(2)}) collective-permute-start(bf16[2,256,512]{2,1,0:T(8,128)(2,1)S(1)} %collective-permute-done.7.refs_6_), channel_id=1, source_target_pairs={{0,32},{16,240},{32,64},{48,16},{64,96},{80,48},{96,128},{112,80},... | collective-permute-start | bytes 1572872 | tf_op jit(solution)/shard_map/ppermute | solution.py:383
  43.4 3.8 %shard_map.68 = (f32[2,512,256]{2,1,0:T(8,128)S(1)}, f32[2,8,256]{2,1,0:T(8,128)S(1)}) custom-call(s32[13]{0:T(128)S(1)} %stack.55.where_ref, bf16[3,256,512]{2,1,0:T(8,128)(2,1)S(1)} %get-tuple-element.39.refs_0_, bf16[3,256,512]{2,1,0:T(8,128)(2,1)S(1)} %collective-permute-done.refs_1_, bf16[256,512]{1,0:T(8,128)(2,1)S(1)} %get-tuple-element.41.refs_2_.refs_3_, ...), custom_call_target="tpu_custom_call" | custom-call | flops 805306368 | bytes 3145728 | tf_op jit(solution)/shard_map/pallas_call | solution.py:230
  47.2 0.0 collective-permute-done.5.refs_7_
  47.2 1.9 %collective-permute-start.8 = (bf16[2,256,512]{2,1,0:T(8,128)(2,1)S(1)}, bf16[2,256,512]{2,1,0:T(8,128)(2,1)S(1)}, u32[]{:S(2)}, u32[]{:S(2)}) collective-permute-start(bf16[2,256,512]{2,1,0:T(8,128)(2,1)S(1)} %collective-permute-done.5.refs_7_), channel_id=1, source_target_pairs={{0,32},{16,240},{32,64},{48,16},{64,96},{80,48},{96,128},{112,80},... | collective-permute-start | bytes 1572872 | tf_op jit(solution)/shard_map/ppermute | solution.py:383
  49.1 4.7 %collective-permute-done.9.refs_8_ = bf16[2,256,512]{2,1,0:T(8,128)(2,1)S(1)} collective-permute-done((bf16[2,256,512]{2,1,0:T(8,128)(2,1)S(1)}, bf16[2,256,512]{2,1,0:T(8,128)(2,1)S(1)}, u32[]{:S(2)}, u32[]{:S(2)}) %collective-permute-start.9) | collective-permute-done | bytes 524320 | tf_op jit(solution)/shard_map/ppermute | solution.py:383
  53.8 3.2 %shard_map.69 = (f32[2,512,256]{2,1,0:T(8,128)S(1)}, f32[2,8,256]{2,1,0:T(8,128)S(1)}, f32[2,512,256]{2,1,0:T(8,128)S(1)}, f32[2,8,256]{2,1,0:T(8,128)S(1)}) custom-call(s32[13]{0:T(128)S(1)} %stack.55.where_ref, bf16[3,256,512]{2,1,0:T(8,128)(2,1)S(1)} %get-tuple-element.39.refs_0_, bf16[3,256,512]{2,1,0:T(8,128)(2,1)S(1)} %collective-permute-done.refs_1_, ...), custom_call_target="tpu_custom_call" | custom-call | flops 1879048192 | bytes 7340032 | tf_op jit(solution)/shard_map/pallas_call | solution.py:230
  57.0 2.5 %collective-permute-done.8.refs_4_ = bf16[2,256,512]{2,1,0:T(8,128)(2,1)S(1)} collective-permute-done((bf16[2,256,512]{2,1,0:T(8,128)(2,1)S(1)}, bf16[2,256,512]{2,1,0:T(8,128)(2,1)S(1)}, u32[]{:S(2)}, u32[]{:S(2)}) %collective-permute-start.8) | collective-permute-done | bytes 524320 | tf_op jit(solution)/shard_map/ppermute | solution.py:383
  59.5 0.0 copy-start
  59.5 1.7 %shard_map.70 = (bf16[2,528,256]{2,1,0:T(8,128)(2,1)S(1)}, bf16[2,528,256]{2,1,0:T(8,128)(2,1)S(1)}) custom-call(s32[13]{0:T(128)S(1)} %stack.55.where_ref, bf16[3,256,512]{2,1,0:T(8,128)(2,1)S(1)} %get-tuple-element.39.refs_0_, bf16[3,256,512]{2,1,0:T(8,128)(2,1)S(1)} %collective-permute-done.refs_1_, bf16[256,512]{1,0:T(8,128)(2,1)S(1)} %collective-permute-done.2.refs_2_, ...), custom_call_target="tpu_custom_call" | custom-call | flops 536870912 | bytes 2097152 | tf_op jit(solution)/shard_map/pallas_call | solution.py:230
  61.2 1.9 %collective-permute-start.10 = (bf16[2,528,256]{2,1,0:T(8,128)(2,1)S(1)}, bf16[2,528,256]{2,1,0:T(8,128)(2,1)S(1)}, u32[]{:S(2)}, u32[]{:S(2)}) collective-permute-start(bf16[2,528,256]{2,1,0:T(8,128)(2,1)S(1)} %get-tuple-element.64), channel_id=1, source_target_pairs={{0,16},{16,0},{32,48},{48,32},{64,80},{80,64},{96,112},{112,96},{1... | collective-permute-start | bytes 1622024 | tf_op jit(solution)/shard_map/ppermute | solution.py:429
  63.1 0.0 copy-done
  63.2 1.9 %collective-permute-done.10.b_ref = bf16[2,528,256]{2,1,0:T(8,128)(2,1)S(1)} collective-permute-done((bf16[2,528,256]{2,1,0:T(8,128)(2,1)S(1)}, bf16[2,528,256]{2,1,0:T(8,128)(2,1)S(1)}, u32[]{:S(2)}, u32[]{:S(2)}) %collective-permute-start.10) | collective-permute-done | bytes 540704 | tf_op jit(solution)/shard_map/ppermute | solution.py:429
  65.0 0.0 copy-start.1
  65.0 0.0 copy-start.2
  65.0 0.1 shard_map.71
  65.2 1.3 %collective-permute-start.11 = (bf16[528,256]{1,0:T(8,128)(2,1)S(1)}, bf16[528,256]{1,0:T(8,128)(2,1)S(1)}, u32[]{:S(2)}, u32[]{:S(2)}) collective-permute-start(bf16[528,256]{1,0:T(8,128)(2,1)S(1)} %shard_map.71), channel_id=1, source_target_pairs={{0,256},{16,272},{32,288},{48,304},{64,320},{80,336},{96,352},{112... | collective-permute-start | bytes 811016 | tf_op jit(solution)/shard_map/ppermute | solution.py:434
  66.5 2.0 %collective-permute-start.12 = (bf16[2,6,512]{2,1,0:T(8,128)(2,1)S(1)}, bf16[2,6,512]{2,1,0:T(8,128)(2,1)S(1)}, u32[]{:S(2)}, u32[]{:S(2)}) collective-permute-start(bf16[2,6,512]{2,1,0:T(8,128)(2,1)S(1)} %slice.7), channel_id=1, source_target_pairs={{0,16},{16,32},{32,48},{48,64},{64,80},{80,96},{96,112},{112,128},... | collective-permute-start | bytes 36872 | tf_op jit(solution)/shard_map/ppermute | solution.py:374
  68.5 5.3 %collective-permute-done.12.rim_ref = bf16[2,6,512]{2,1,0:T(8,128)(2,1)S(1)} collective-permute-done((bf16[2,6,512]{2,1,0:T(8,128)(2,1)S(1)}, bf16[2,6,512]{2,1,0:T(8,128)(2,1)S(1)}, u32[]{:S(2)}, u32[]{:S(2)}) %collective-permute-start.12) | collective-permute-done | bytes 12320 | tf_op jit(solution)/shard_map/ppermute | solution.py:374
  73.9 0.0 copy-done.1
  73.9 0.0 copy-done.2
  73.9 0.8 shard_map.72
  74.7 2.8 %collective-permute-done.11.s_ref = bf16[528,256]{1,0:T(8,128)(2,1)S(1)} collective-permute-done((bf16[528,256]{1,0:T(8,128)(2,1)S(1)}, bf16[528,256]{1,0:T(8,128)(2,1)S(1)}, u32[]{:S(2)}, u32[]{:S(2)}) %collective-permute-start.11) | collective-permute-done | bytes 270368 | tf_op jit(solution)/shard_map/ppermute | solution.py:434
  77.5 1.4 %shard_map.73 = (bf16[512,256]{1,0:T(8,128)(2,1)S(1)}, f32[16,1,256]{2,1,0:T(1,128)}) custom-call(s32[13]{0:T(128)S(1)} %stack.55.where_ref, bf16[2,528,256]{2,1,0:T(8,128)(2,1)S(1)} %get-tuple-element.63.a_ref, bf16[2,528,256]{2,1,0:T(8,128)(2,1)S(1)} %collective-permute-done.10.b_ref, bf16[528,256]{1,0:T(8,128)(2,1)S(1)} %collective-permute-done.11.s_ref), custom_call_target="tpu_custom_call" | custom-call | tf_op jit(solution)/shard_map/pallas_call | solution.py:309
  78.9 9.1 %all-to-all-start = ((f32[16,1,256]{2,1,0:T(1,128)}), f32[16,1,256]{2,1,0:T(1,128)S(1)}, u32[]{:S(2)}, u32[]{:S(2)}) async-start(f32[16,1,256]{2,1,0:T(1,128)} %get-tuple-element.69), calls=%async_computation | async-start | bytes 32768 | tf_op jit(solution)/shard_map/all_to_all | solution.py:439
  88.0 0.1 shard_map.74.wide_ref
  88.1 9.8 %all-to-all-done.spread_ref = f32[16,1,256]{2,1,0:T(1,128)S(1)} async-done(((f32[16,1,256]{2,1,0:T(1,128)}), f32[16,1,256]{2,1,0:T(1,128)S(1)}, u32[]{:S(2)}, u32[]{:S(2)}) %all-to-all-start) | async-done | bytes 16416 | tf_op jit(solution)/shard_map/all_to_all | solution.py:439
  98.0 0.9 shard_map.75
  (1 shorter events, 0.0 us)
Async XLA Ops:
  1.2 11.7 %collective-permute-start = (bf16[3,256,512]{2,1,0:T(8,128)(2,1)S(1)}, bf16[3,256,512]{2,1,0:T(8,128)(2,1)S(1)}, u32[]{:S(2)}, u32[]{:S(2)}) collective-permute-start(bf16[3,256,512]{2,1,0:T(8,128)(2,1)S(1)} %get-tuple-element.39.refs_0_), channel_id=1, source_target_pairs={{0,16},{16,0},{32,48},{48,32},{64,80},{80,64},{96,112},{112,96},{1... | collective-permute-start | bytes 2359304 | tf_op jit(solution)/shard_map/ppermute | solution.py:382
  3.2 18.1 %collective-permute-start.1 = (bf16[2,256,512]{2,1,0:T(8,128)(2,1)S(1)}, bf16[2,256,512]{2,1,0:T(8,128)(2,1)S(1)}, u32[]{:S(2)}, u32[]{:S(2)}) collective-permute-start(bf16[2,256,512]{2,1,0:T(8,128)(2,1)S(1)} %get-tuple-element.40.refs_4_), channel_id=1, source_target_pairs={{0,32},{16,240},{32,64},{48,16},{64,96},{80,48},{96,128},{112,80},... | collective-permute-start | bytes 1572872 | tf_op jit(solution)/shard_map/ppermute | solution.py:383
  7.5 10.0 %collective-permute-start.2 = (bf16[256,512]{1,0:T(8,128)(2,1)S(1)}, bf16[256,512]{1,0:T(8,128)(2,1)S(1)}, u32[]{:S(2)}, u32[]{:S(2)}) collective-permute-start(bf16[256,512]{1,0:T(8,128)(2,1)S(1)} %get-tuple-element.41.refs_2_.refs_3_), channel_id=1, source_target_pairs={{256,0},{272,16},{288,32},{304,48},{320,64},{336,80},{352,96},{368... | collective-permute-start | bytes 786440 | tf_op jit(solution)/shard_map/ppermute | solution.py:395
  13.8 15.2 %collective-permute-start.6 = (bf16[2,256,512]{2,1,0:T(8,128)(2,1)}, bf16[2,256,512]{2,1,0:T(8,128)(2,1)}, u32[]{:S(2)}, u32[]{:S(2)}) collective-permute-start(bf16[2,256,512]{2,1,0:T(8,128)(2,1)} %slice.8), channel_id=1, source_target_pairs={{0,32},{16,240},{32,64},{48,16},{64,96},{80,48},{96,128},{112,80},... | collective-permute-start | bytes 1572872 | tf_op jit(solution)/shard_map/ppermute | solution.py:383
  21.3 12.3 %collective-permute-start.4 = (bf16[2,256,512]{2,1,0:T(8,128)(2,1)S(1)}, bf16[2,256,512]{2,1,0:T(8,128)(2,1)S(1)}, u32[]{:S(2)}, u32[]{:S(2)}) collective-permute-start(bf16[2,256,512]{2,1,0:T(8,128)(2,1)S(1)} %collective-permute-done.1.refs_5_.refs_4_), channel_id=1, source_target_pairs={{0,32},{16,240},{32,64},{48,16},{64,96},{80,48},{96,128},{112,80},... | collective-permute-start | bytes 1572872 | tf_op jit(solution)/shard_map/ppermute | solution.py:383
  23.2 7.8 %collective-permute-start.3 = (bf16[256,512]{1,0:T(8,128)(2,1)S(1)}, bf16[256,512]{1,0:T(8,128)(2,1)S(1)}, u32[]{:S(2)}, u32[]{:S(2)}) collective-permute-start(bf16[256,512]{1,0:T(8,128)(2,1)S(1)} %collective-permute-done.2.refs_2_), channel_id=1, source_target_pairs={{0,16},{16,0},{32,48},{48,32},{64,80},{80,64},{96,112},{112,96},{1... | collective-permute-start | bytes 786440 | tf_op jit(solution)/shard_map/ppermute | solution.py:400
  29.0 12.5 %collective-permute-start.7 = (bf16[2,256,512]{2,1,0:T(8,128)(2,1)}, bf16[2,256,512]{2,1,0:T(8,128)(2,1)S(1)}, u32[]{:S(2)}, u32[]{:S(2)}) collective-permute-start(bf16[2,256,512]{2,1,0:T(8,128)(2,1)} %collective-permute-done.6.refs_4_), channel_id=1, source_target_pairs={{0,32},{16,240},{32,64},{48,16},{64,96},{80,48},{96,128},{112,80},... | collective-permute-start | bytes 1572872 | tf_op jit(solution)/shard_map/ppermute | solution.py:383
  33.5 13.6 %collective-permute-start.5 = (bf16[2,256,512]{2,1,0:T(8,128)(2,1)S(1)}, bf16[2,256,512]{2,1,0:T(8,128)(2,1)S(1)}, u32[]{:S(2)}, u32[]{:S(2)}) collective-permute-start(bf16[2,256,512]{2,1,0:T(8,128)(2,1)S(1)} %collective-permute-done.4.refs_5_), channel_id=1, source_target_pairs={{0,32},{16,240},{32,64},{48,16},{64,96},{80,48},{96,128},{112,80},... | collective-permute-start | bytes 1572872 | tf_op jit(solution)/shard_map/ppermute | solution.py:383
  41.5 12.3 %collective-permute-start.9 = (bf16[2,256,512]{2,1,0:T(8,128)(2,1)S(1)}, bf16[2,256,512]{2,1,0:T(8,128)(2,1)S(1)}, u32[]{:S(2)}, u32[]{:S(2)}) collective-permute-start(bf16[2,256,512]{2,1,0:T(8,128)(2,1)S(1)} %collective-permute-done.7.refs_6_), channel_id=1, source_target_pairs={{0,32},{16,240},{32,64},{48,16},{64,96},{80,48},{96,128},{112,80},... | collective-permute-start | bytes 1572872 | tf_op jit(solution)/shard_map/ppermute | solution.py:383
  47.2 12.3 %collective-permute-start.8 = (bf16[2,256,512]{2,1,0:T(8,128)(2,1)S(1)}, bf16[2,256,512]{2,1,0:T(8,128)(2,1)S(1)}, u32[]{:S(2)}, u32[]{:S(2)}) collective-permute-start(bf16[2,256,512]{2,1,0:T(8,128)(2,1)S(1)} %collective-permute-done.5.refs_7_), channel_id=1, source_target_pairs={{0,32},{16,240},{32,64},{48,16},{64,96},{80,48},{96,128},{112,80},... | collective-permute-start | bytes 1572872 | tf_op jit(solution)/shard_map/ppermute | solution.py:383
  59.5 3.7 %copy-start = (bf16[3,256,512]{2,1,0:T(8,128)(2,1)S(1)}, bf16[3,256,512]{2,1,0:T(8,128)(2,1)}, u32[]{:S(2)}) copy-start(bf16[3,256,512]{2,1,0:T(8,128)(2,1)} %input_ref.1) | copy-start | bytes 2359300
  61.2 3.8 %collective-permute-start.10 = (bf16[2,528,256]{2,1,0:T(8,128)(2,1)S(1)}, bf16[2,528,256]{2,1,0:T(8,128)(2,1)S(1)}, u32[]{:S(2)}, u32[]{:S(2)}) collective-permute-start(bf16[2,528,256]{2,1,0:T(8,128)(2,1)S(1)} %get-tuple-element.64), channel_id=1, source_target_pairs={{0,16},{16,0},{32,48},{48,32},{64,80},{80,64},{96,112},{112,96},{1... | collective-permute-start | bytes 1622024 | tf_op jit(solution)/shard_map/ppermute | solution.py:429
  65.0 8.8 %copy-start.1 = (f32[7,512]{1,0:T(8,128)S(1)}, f32[7,512]{1,0:T(8,128)}, u32[]{:S(2)}) copy-start(f32[7,512]{1,0:T(8,128)} %filter_ref.1) | copy-start | bytes 43012
  65.0 8.8 %copy-start.2 = (f32[512]{0:T(512)S(1)}, f32[512]{0:T(512)}, u32[]{:S(2)}) copy-start(f32[512]{0:T(512)} %param.11) | copy-start | bytes 6148
  65.2 12.3 %collective-permute-start.11 = (bf16[528,256]{1,0:T(8,128)(2,1)S(1)}, bf16[528,256]{1,0:T(8,128)(2,1)S(1)}, u32[]{:S(2)}, u32[]{:S(2)}) collective-permute-start(bf16[528,256]{1,0:T(8,128)(2,1)S(1)} %shard_map.71), channel_id=1, source_target_pairs={{0,256},{16,272},{32,288},{48,304},{64,320},{80,336},{96,352},{112... | collective-permute-start | bytes 811016 | tf_op jit(solution)/shard_map/ppermute | solution.py:434
  66.5 7.4 %collective-permute-start.12 = (bf16[2,6,512]{2,1,0:T(8,128)(2,1)S(1)}, bf16[2,6,512]{2,1,0:T(8,128)(2,1)S(1)}, u32[]{:S(2)}, u32[]{:S(2)}) collective-permute-start(bf16[2,6,512]{2,1,0:T(8,128)(2,1)S(1)} %slice.7), channel_id=1, source_target_pairs={{0,16},{16,32},{32,48},{48,64},{64,80},{80,96},{96,112},{112,128},... | collective-permute-start | bytes 36872 | tf_op jit(solution)/shard_map/ppermute | solution.py:374
  78.9 19.1 %all-to-all-start = ((f32[16,1,256]{2,1,0:T(1,128)}), f32[16,1,256]{2,1,0:T(1,128)S(1)}, u32[]{:S(2)}, u32[]{:S(2)}) async-start(f32[16,1,256]{2,1,0:T(1,128)} %get-tuple-element.69), calls=%async_computation | async-start | bytes 32768 | tf_op jit(solution)/shard_map/all_to_all | solution.py:439

commit v4 on v3

--- a/solution.py
+++ b/solution.py
@@ -397,27 +397,33 @@
     a1, b1 = ring(a0), ring(b0)
     acc, stat = attend_call(where, queries_near, [(0, a0)], [(NEAR, (0,), None)])
     a1, stat, above = lax.optimization_barrier((a1, stat, above))
-    queries_all = (own_all, other, above, lax.ppermute(above, "ctx", CORES))
     a2 = ring(a1)
     acc, stat = attend_call(where, queries_near, [(1, a1)], [(NEAR, (0,), (acc, stat))])
+    stat, late = after(stat, above)
     b1, stat = after(b1, stat)
+    queries_all = (own_all, other, above, lax.ppermute(late, "ctx", CORES))
     b2 = ring(b1)
     high = attend_call(where, queries_all, [(0, a0), (1, a1)], [(ABOVE, (0, 1), None)])
     a2, mark = after(a2, high[1])
-    a3, b3 = ring(a2), ring(b2)
+    a3 = ring(a2)
+    high = attend_call(
+        where, queries_all, [(6, b1), (2, a2)], [(ABOVE, (0, 1), (high[0], mark))]
+    )
+    b2, mark = after(b2, high[1])
+    b3 = ring(b2)
     near = attend_call(
         where,
         queries_near,
         [(6, b1), (2, a2), (7, b2)],
         [(NEAR, (0, 1, 2), (acc, stat))],
     )
-    a3, stat = after(a3, near[1])
+    stat = near[1]
     a4 = ring(a3)
     *near, acc, stat = attend_call(
         where,
         queries_all,
-        [(6, b1), (2, a2), (7, b2), (3, a3), (8, b3)],
-        [(NEAR, (3, 4), (near[0], stat)), (ABOVE, (0, 1, 2, 3, 4), (high[0], mark))],
+        [(7, b2), (3, a3), (8, b3)],
+        [(NEAR, (1, 2), (near[0], stat)), (ABOVE, (0, 1, 2), (high[0], mark))],
     )
     near, far = attend_call(
         where,

time: 99.4 us -> 98.2 us (0.988)
  waiting for transfers between devices: 38.8 us -> 36.9 us
    ppermute x1, waiting for transfers between devices: 2.81 us -> 1.34 us  [on_device(): across, gain = after(lax.ppermute(below, 'ctx', UP), gain)]
    pallas_call x6 -> x7, Pallas kernels: 12.4 us -> 13.2 us  [attend_call(): pl.pallas_call(functools.partial(attend_kernel, places, [(tiles, used, st...]
  transfers between devices with their start and end apart: 14 -> 14, of which waited for: 9 -> 10; matrix products, arithmetic and copies ran while one was open for 1% -> 1% of each run, Pallas kernels for 12% -> 13%
where the time goes in v4:
time: 98.2 us; the launch traced here: 97.6 us
  starting transfers between devices  41.6 us (42%)
  waiting for transfers between devices  36.9 us (38%)
  Pallas kernels  17.7 us (18%)
    ppermute x7, waiting for transfers between devices, on_device(): ring = lambda chunk: lax.ppermute(chunk, 'ctx', RING)  18.6 us
    ppermute x7, starting transfers between devices, on_device(): ring = lambda chunk: lax.ppermute(chunk, 'ctx', RING)  15.7 us
    pallas_call x7, Pallas kernels, attend_call(): pl.pallas_call(functools.partial(attend_kernel, places, [(tiles, used, st...  13.2 us
    all_to_all x1, waiting for transfers between devices, on_device(): spread = lax.all_to_all(squares, 'heads', 0, 0, tiled=True)  9.84 us
    all_to_all x1, starting transfers between devices, on_device(): spread = lax.all_to_all(squares, 'heads', 0, 0, tiled=True)  9.06 us
    ppermute x1, starting transfers between devices, on_device(): above = lax.ppermute(turned, 'ctx', DOWN)  5.47 us
    ppermute x1, waiting for transfers between devices, rim_of(): return lax.ppermute(tails, 'ctx', [(i, i + 1) for i in range(size - 1)])  5.22 us
    ppermute x1, starting transfers between devices, on_device(): queries_all = (own_all, other, above, lax.ppermute(late, 'ctx', CORES))  4.18 us
  transfers between devices with their start and end apart: 14, of which 10 were waited for; matrix products, arithmetic and copies ran while one was open for 1% of the time, Pallas kernels for 13%

profile of v4, /device:TPU:2, one launch (start us, length us, event | category | flops | bytes accessed | tf_op | source)
XLA Modules:
  0.0 97.6 jit_solution(71246637526502054)
XLA Ops:
  0.0 1.2 %shard_map.64 = (bf16[2,256,512]{2,1,0:T(8,128)(2,1)S(1)}, bf16[3,256,512]{2,1,0:T(8,128)(2,1)S(1)}, bf16[256,512]{1,0:T(8,128)(2,1)S(1)}) custom-call(bf16[256,512]{1,0:T(8,128)(2,1)} %k_ref.1, bf16[256,512]{1,0:T(8,128)(2,1)} %v_ref.1, bf16[256,512]{1,0:T(8,128)(2,1)} %q_ref.1), custom_call_target="tpu_custom_call" | custom-call | tf_op jit(solution)/shard_map/pallas_call | solution.py:89
  1.2 1.9 %collective-permute-start = (bf16[3,256,512]{2,1,0:T(8,128)(2,1)S(1)}, bf16[3,256,512]{2,1,0:T(8,128)(2,1)S(1)}, u32[]{:S(2)}, u32[]{:S(2)}) collective-permute-start(bf16[3,256,512]{2,1,0:T(8,128)(2,1)S(1)} %get-tuple-element.43.refs_0_), channel_id=1, source_target_pairs={{0,16},{16,0},{32,48},{48,32},{64,80},{80,64},{96,112},{112,96},{1... | collective-permute-start | bytes 2359304 | tf_op jit(solution)/shard_map/ppermute | solution.py:382
  3.2 4.3 %collective-permute-start.1 = (bf16[2,256,512]{2,1,0:T(8,128)(2,1)S(1)}, bf16[2,256,512]{2,1,0:T(8,128)(2,1)}, u32[]{:S(2)}, u32[]{:S(2)}) collective-permute-start(bf16[2,256,512]{2,1,0:T(8,128)(2,1)S(1)} %get-tuple-element.44.refs_4_), channel_id=1, source_target_pairs={{0,32},{16,240},{32,64},{48,16},{64,96},{80,48},{96,128},{112,80},... | collective-permute-start | bytes 1572872 | tf_op jit(solution)/shard_map/ppermute | solution.py:383
  7.5 5.5 %collective-permute-start.2 = (bf16[256,512]{1,0:T(8,128)(2,1)S(1)}, bf16[256,512]{1,0:T(8,128)(2,1)S(1)}, u32[]{:S(2)}, u32[]{:S(2)}) collective-permute-start(bf16[256,512]{1,0:T(8,128)(2,1)S(1)} %get-tuple-element.45.refs_2_.refs_3_), channel_id=1, source_target_pairs={{256,0},{272,16},{288,32},{304,48},{320,64},{336,80},{352,96},{368... | collective-permute-start | bytes 786440 | tf_op jit(solution)/shard_map/ppermute | solution.py:395
  12.9 0.0 collective-permute-done.refs_1_
  12.9 0.8 slice.8
  13.8 1.9 %collective-permute-start.7 = (bf16[2,256,512]{2,1,0:T(8,128)(2,1)}, bf16[2,256,512]{2,1,0:T(8,128)(2,1)S(1)}, u32[]{:S(2)}, u32[]{:S(2)}) collective-permute-start(bf16[2,256,512]{2,1,0:T(8,128)(2,1)} %slice.8), channel_id=1, source_target_pairs={{0,32},{16,240},{32,64},{48,16},{64,96},{80,48},{96,128},{112,80},... | collective-permute-start | bytes 1572872 | tf_op jit(solution)/shard_map/ppermute | solution.py:383
  15.8 0.1 stack.55.where_ref
  15.9 1.5 %shard_map.65 = (f32[2,512,256]{2,1,0:T(8,128)S(1)}, f32[2,8,256]{2,1,0:T(8,128)S(1)}) custom-call(s32[13]{0:T(128)S(1)} %stack.55.where_ref, bf16[3,256,512]{2,1,0:T(8,128)(2,1)S(1)} %get-tuple-element.43.refs_0_, bf16[3,256,512]{2,1,0:T(8,128)(2,1)S(1)} %collective-permute-done.refs_1_, bf16[256,512]{1,0:T(8,128)(2,1)S(1)} %get-tuple-element.45.refs_2_.refs_3_, ...), custom_call_target="tpu_custom_call" | custom-call | flops 268435456 | bytes 1048576 | tf_op jit(solution)/shard_map/pallas_call | solution.py:230
  17.5 0.0 collective-permute-done.2.refs_2_
  17.5 3.9 %collective-permute-done.1.refs_4_.refs_5_ = bf16[2,256,512]{2,1,0:T(8,128)(2,1)} collective-permute-done((bf16[2,256,512]{2,1,0:T(8,128)(2,1)S(1)}, bf16[2,256,512]{2,1,0:T(8,128)(2,1)}, u32[]{:S(2)}, u32[]{:S(2)}) %collective-permute-start.1) | collective-permute-done | bytes 524320 | tf_op jit(solution)/shard_map/ppermute | solution.py:383
  21.4 1.9 %collective-permute-start.4 = (bf16[2,256,512]{2,1,0:T(8,128)(2,1)}, bf16[2,256,512]{2,1,0:T(8,128)(2,1)S(1)}, u32[]{:S(2)}, u32[]{:S(2)}) collective-permute-start(bf16[2,256,512]{2,1,0:T(8,128)(2,1)} %collective-permute-done.1.refs_4_.refs_5_), channel_id=1, source_target_pairs={{0,32},{16,240},{32,64},{48,16},{64,96},{80,48},{96,128},{112,80},... | collective-permute-start | bytes 1572872 | tf_op jit(solution)/shard_map/ppermute | solution.py:383
  23.3 2.1 %shard_map.66 = (f32[2,512,256]{2,1,0:T(8,128)S(1)}, f32[2,8,256]{2,1,0:T(8,128)S(1)}) custom-call(s32[13]{0:T(128)S(1)} %stack.55.where_ref, bf16[3,256,512]{2,1,0:T(8,128)(2,1)S(1)} %get-tuple-element.43.refs_0_, bf16[3,256,512]{2,1,0:T(8,128)(2,1)S(1)} %collective-permute-done.refs_1_, bf16[256,512]{1,0:T(8,128)(2,1)S(1)} %get-tuple-element.45.refs_2_.refs_3_, ...), custom_call_target="tpu_custom_call" | custom-call | flops 268435456 | bytes 1048576 | tf_op jit(solution)/shard_map/pallas_call | solution.py:230
  25.4 4.2 %collective-permute-start.3 = (bf16[256,512]{1,0:T(8,128)(2,1)S(1)}, bf16[256,512]{1,0:T(8,128)(2,1)S(1)}, u32[]{:S(2)}, u32[]{:S(2)}) collective-permute-start(bf16[256,512]{1,0:T(8,128)(2,1)S(1)} %collective-permute-done.2.refs_2_), channel_id=1, source_target_pairs={{0,16},{16,0},{32,48},{48,32},{64,80},{80,64},{96,112},{112,96},{1... | collective-permute-start | bytes 786440 | tf_op jit(solution)/shard_map/ppermute | solution.py:404
  29.6 0.0 collective-permute-done.7.refs_4_
  29.6 1.9 %collective-permute-start.8 = (bf16[2,256,512]{2,1,0:T(8,128)(2,1)S(1)}, bf16[2,256,512]{2,1,0:T(8,128)(2,1)S(1)}, u32[]{:S(2)}, u32[]{:S(2)}) collective-permute-start(bf16[2,256,512]{2,1,0:T(8,128)(2,1)S(1)} %collective-permute-done.7.refs_4_), channel_id=1, source_target_pairs={{0,32},{16,240},{32,64},{48,16},{64,96},{80,48},{96,128},{112,80},... | collective-permute-start | bytes 1572872 | tf_op jit(solution)/shard_map/ppermute | solution.py:383
  31.6 0.0 collective-permute-done.3.refs_3_
  31.6 1.1 %shard_map.67 = (f32[2,512,256]{2,1,0:T(8,128)S(1)}, f32[2,8,256]{2,1,0:T(8,128)S(1)}) custom-call(s32[13]{0:T(128)S(1)} %stack.55.where_ref, bf16[3,256,512]{2,1,0:T(8,128)(2,1)S(1)} %get-tuple-element.43.refs_0_, bf16[3,256,512]{2,1,0:T(8,128)(2,1)S(1)} %collective-permute-done.refs_1_, bf16[256,512]{1,0:T(8,128)(2,1)S(1)} %collective-permute-done.2.refs_2_, ...), custom_call_target="tpu_custom_call" | custom-call | flops 536870912 | bytes 2097152 | tf_op jit(solution)/shard_map/pallas_call | solution.py:230
  32.7 1.2 %collective-permute-done.4.refs_5_ = bf16[2,256,512]{2,1,0:T(8,128)(2,1)S(1)} collective-permute-done((bf16[2,256,512]{2,1,0:T(8,128)(2,1)}, bf16[2,256,512]{2,1,0:T(8,128)(2,1)S(1)}, u32[]{:S(2)}, u32[]{:S(2)}) %collective-permute-start.4) | collective-permute-done | bytes 524320 | tf_op jit(solution)/shard_map/ppermute | solution.py:383
  33.9 1.9 %collective-permute-start.5 = (bf16[2,256,512]{2,1,0:T(8,128)(2,1)S(1)}, bf16[2,256,512]{2,1,0:T(8,128)(2,1)S(1)}, u32[]{:S(2)}, u32[]{:S(2)}) collective-permute-start(bf16[2,256,512]{2,1,0:T(8,128)(2,1)S(1)} %collective-permute-done.4.refs_5_), channel_id=1, source_target_pairs={{0,32},{16,240},{32,64},{48,16},{64,96},{80,48},{96,128},{112,80},... | collective-permute-start | bytes 1572872 | tf_op jit(solution)/shard_map/ppermute | solution.py:383
  35.8 0.6 shard_map.68
  36.4 5.5 %collective-permute-done.8.refs_6_.refs_4_ = bf16[2,256,512]{2,1,0:T(8,128)(2,1)S(1)} collective-permute-done((bf16[2,256,512]{2,1,0:T(8,128)(2,1)S(1)}, bf16[2,256,512]{2,1,0:T(8,128)(2,1)S(1)}, u32[]{:S(2)}, u32[]{:S(2)}) %collective-permute-start.8) | collective-permute-done | bytes 524320 | tf_op jit(solution)/shard_map/ppermute | solution.py:383
  41.9 1.9 %collective-permute-start.9 = (bf16[2,256,512]{2,1,0:T(8,128)(2,1)S(1)}, bf16[2,256,512]{2,1,0:T(8,128)(2,1)S(1)}, u32[]{:S(2)}, u32[]{:S(2)}) collective-permute-start(bf16[2,256,512]{2,1,0:T(8,128)(2,1)S(1)} %collective-permute-done.8.refs_6_.refs_4_), channel_id=1, source_target_pairs={{0,32},{16,240},{32,64},{48,16},{64,96},{80,48},{96,128},{112,80},... | collective-permute-start | bytes 1572872 | tf_op jit(solution)/shard_map/ppermute | solution.py:383
  43.8 3.7 %collective-permute-done.5.refs_5_ = bf16[2,256,512]{2,1,0:T(8,128)(2,1)S(1)} collective-permute-done((bf16[2,256,512]{2,1,0:T(8,128)(2,1)S(1)}, bf16[2,256,512]{2,1,0:T(8,128)(2,1)S(1)}, u32[]{:S(2)}, u32[]{:S(2)}) %collective-permute-start.5) | collective-permute-done | bytes 524320 | tf_op jit(solution)/shard_map/ppermute | solution.py:383
  47.5 1.9 %collective-permute-start.6 = (bf16[2,256,512]{2,1,0:T(8,128)(2,1)S(1)}, bf16[2,256,512]{2,1,0:T(8,128)(2,1)S(1)}, u32[]{:S(2)}, u32[]{:S(2)}) collective-permute-start(bf16[2,256,512]{2,1,0:T(8,128)(2,1)S(1)} %collective-permute-done.5.refs_5_), channel_id=1, source_target_pairs={{0,32},{16,240},{32,64},{48,16},{64,96},{80,48},{96,128},{112,80},... | collective-permute-start | bytes 1572872 | tf_op jit(solution)/shard_map/ppermute | solution.py:383
  49.5 3.3 %shard_map.69 = (f32[2,512,256]{2,1,0:T(8,128)S(1)}, f32[2,8,256]{2,1,0:T(8,128)S(1)}) custom-call(s32[13]{0:T(128)S(1)} %stack.55.where_ref, bf16[3,256,512]{2,1,0:T(8,128)(2,1)S(1)} %get-tuple-element.43.refs_0_, bf16[3,256,512]{2,1,0:T(8,128)(2,1)S(1)} %collective-permute-done.refs_1_, bf16[256,512]{1,0:T(8,128)(2,1)S(1)} %get-tuple-element.45.refs_2_.refs_3_, ...), custom_call_target="tpu_custom_call" | custom-call | flops 805306368 | bytes 3145728 | tf_op jit(solution)/shard_map/pallas_call | solution.py:230
  52.8 1.4 %collective-permute-done.9.refs_6_ = bf16[2,256,512]{2,1,0:T(8,128)(2,1)S(1)} collective-permute-done((bf16[2,256,512]{2,1,0:T(8,128)(2,1)S(1)}, bf16[2,256,512]{2,1,0:T(8,128)(2,1)S(1)}, u32[]{:S(2)}, u32[]{:S(2)}) %collective-permute-start.9) | collective-permute-done | bytes 524320 | tf_op jit(solution)/shard_map/ppermute | solution.py:383
  54.2 2.7 %shard_map.70 = (f32[2,512,256]{2,1,0:T(8,128)S(1)}, f32[2,8,256]{2,1,0:T(8,128)S(1)}, f32[2,512,256]{2,1,0:T(8,128)S(1)}, f32[2,8,256]{2,1,0:T(8,128)S(1)}) custom-call(s32[13]{0:T(128)S(1)} %stack.55.where_ref, bf16[3,256,512]{2,1,0:T(8,128)(2,1)S(1)} %get-tuple-element.43.refs_0_, bf16[3,256,512]{2,1,0:T(8,128)(2,1)S(1)} %collective-permute-done.refs_1_, ...), custom_call_target="tpu_custom_call" | custom-call | flops 1342177280 | bytes 5242880 | tf_op jit(solution)/shard_map/pallas_call | solution.py:230
  56.9 2.9 %collective-permute-done.6.refs_4_ = bf16[2,256,512]{2,1,0:T(8,128)(2,1)S(1)} collective-permute-done((bf16[2,256,512]{2,1,0:T(8,128)(2,1)S(1)}, bf16[2,256,512]{2,1,0:T(8,128)(2,1)S(1)}, u32[]{:S(2)}, u32[]{:S(2)}) %collective-permute-start.6) | collective-permute-done | bytes 524320 | tf_op jit(solution)/shard_map/ppermute | solution.py:383
  59.8 0.0 copy-start
  59.8 1.7 %shard_map.71 = (bf16[2,528,256]{2,1,0:T(8,128)(2,1)S(1)}, bf16[2,528,256]{2,1,0:T(8,128)(2,1)S(1)}) custom-call(s32[13]{0:T(128)S(1)} %stack.55.where_ref, bf16[3,256,512]{2,1,0:T(8,128)(2,1)S(1)} %get-tuple-element.43.refs_0_, bf16[3,256,512]{2,1,0:T(8,128)(2,1)S(1)} %collective-permute-done.refs_1_, bf16[256,512]{1,0:T(8,128)(2,1)S(1)} %collective-permute-done.2.refs_2_, ...), custom_call_target="tpu_custom_call" | custom-call | flops 536870912 | bytes 2097152 | tf_op jit(solution)/shard_map/pallas_call | solution.py:230
  61.5 1.9 %collective-permute-start.10 = (bf16[2,528,256]{2,1,0:T(8,128)(2,1)S(1)}, bf16[2,528,256]{2,1,0:T(8,128)(2,1)S(1)}, u32[]{:S(2)}, u32[]{:S(2)}) collective-permute-start(bf16[2,528,256]{2,1,0:T(8,128)(2,1)S(1)} %get-tuple-element.72), channel_id=1, source_target_pairs={{0,16},{16,0},{32,48},{48,32},{64,80},{80,64},{96,112},{112,96},{1... | collective-permute-start | bytes 1622024 | tf_op jit(solution)/shard_map/ppermute | solution.py:435
  63.5 0.0 copy-done
  63.5 1.9 %collective-permute-done.10.b_ref = bf16[2,528,256]{2,1,0:T(8,128)(2,1)S(1)} collective-permute-done((bf16[2,528,256]{2,1,0:T(8,128)(2,1)S(1)}, bf16[2,528,256]{2,1,0:T(8,128)(2,1)S(1)}, u32[]{:S(2)}, u32[]{:S(2)}) %collective-permute-start.10) | collective-permute-done | bytes 540704 | tf_op jit(solution)/shard_map/ppermute | solution.py:435
  65.4 0.0 copy-start.1
  65.4 0.1 shard_map.72
  65.5 1.3 %collective-permute-start.11 = (bf16[528,256]{1,0:T(8,128)(2,1)S(1)}, bf16[528,256]{1,0:T(8,128)(2,1)S(1)}, u32[]{:S(2)}, u32[]{:S(2)}) collective-permute-start(bf16[528,256]{1,0:T(8,128)(2,1)S(1)} %shard_map.72), channel_id=1, source_target_pairs={{0,256},{16,272},{32,288},{48,304},{64,320},{80,336},{96,352},{112... | collective-permute-start | bytes 811016 | tf_op jit(solution)/shard_map/ppermute | solution.py:440
  66.8 2.0 %collective-permute-start.12 = (bf16[2,6,512]{2,1,0:T(8,128)(2,1)S(1)}, bf16[2,6,512]{2,1,0:T(8,128)(2,1)S(1)}, u32[]{:S(2)}, u32[]{:S(2)}) collective-permute-start(bf16[2,6,512]{2,1,0:T(8,128)(2,1)S(1)} %slice.7), channel_id=1, source_target_pairs={{0,16},{16,32},{32,48},{48,64},{64,80},{80,96},{96,112},{112,128},... | collective-permute-start | bytes 36872 | tf_op jit(solution)/shard_map/ppermute | solution.py:374
  68.9 5.2 %collective-permute-done.12.rim_ref = bf16[2,6,512]{2,1,0:T(8,128)(2,1)S(1)} collective-permute-done((bf16[2,6,512]{2,1,0:T(8,128)(2,1)S(1)}, bf16[2,6,512]{2,1,0:T(8,128)(2,1)S(1)}, u32[]{:S(2)}, u32[]{:S(2)}) %collective-permute-start.12) | collective-permute-done | bytes 12320 | tf_op jit(solution)/shard_map/ppermute | solution.py:374
  74.1 0.0 copy-done.1
  74.1 0.0 copy-done.2
  74.1 0.8 shard_map.73
  74.9 1.3 %collective-permute-done.11.s_ref = bf16[528,256]{1,0:T(8,128)(2,1)S(1)} collective-permute-done((bf16[528,256]{1,0:T(8,128)(2,1)S(1)}, bf16[528,256]{1,0:T(8,128)(2,1)S(1)}, u32[]{:S(2)}, u32[]{:S(2)}) %collective-permute-start.11) | collective-permute-done | bytes 270368 | tf_op jit(solution)/shard_map/ppermute | solution.py:440
  76.3 1.4 %shard_map.74 = (bf16[512,256]{1,0:T(8,128)(2,1)S(1)}, f32[16,1,256]{2,1,0:T(1,128)}) custom-call(s32[13]{0:T(128)S(1)} %stack.55.where_ref, bf16[2,528,256]{2,1,0:T(8,128)(2,1)S(1)} %get-tuple-element.71.a_ref, bf16[2,528,256]{2,1,0:T(8,128)(2,1)S(1)} %collective-permute-done.10.b_ref, bf16[528,256]{1,0:T(8,128)(2,1)S(1)} %collective-permute-done.11.s_ref), custom_call_target="tpu_custom_call" | custom-call | tf_op jit(solution)/shard_map/pallas_call | solution.py:309
  77.7 9.1 %all-to-all-start = ((f32[16,1,256]{2,1,0:T(1,128)}), f32[16,1,256]{2,1,0:T(1,128)S(1)}, u32[]{:S(2)}, u32[]{:S(2)}) async-start(f32[16,1,256]{2,1,0:T(1,128)} %get-tuple-element.77), calls=%async_computation | async-start | bytes 32768 | tf_op jit(solution)/shard_map/all_to_all | solution.py:445
  86.7 0.1 shard_map.75.wide_ref
  86.9 9.8 %all-to-all-done.spread_ref = f32[16,1,256]{2,1,0:T(1,128)S(1)} async-done(((f32[16,1,256]{2,1,0:T(1,128)}), f32[16,1,256]{2,1,0:T(1,128)S(1)}, u32[]{:S(2)}, u32[]{:S(2)}) %all-to-all-start) | async-done | bytes 16416 | tf_op jit(solution)/shard_map/all_to_all | solution.py:445
  96.7 0.9 shard_map.76
  (2 shorter events, 0.0 us)
Async XLA Ops:
  1.2 11.7 %collective-permute-start = (bf16[3,256,512]{2,1,0:T(8,128)(2,1)S(1)}, bf16[3,256,512]{2,1,0:T(8,128)(2,1)S(1)}, u32[]{:S(2)}, u32[]{:S(2)}) collective-permute-start(bf16[3,256,512]{2,1,0:T(8,128)(2,1)S(1)} %get-tuple-element.43.refs_0_), channel_id=1, source_target_pairs={{0,16},{16,0},{32,48},{48,32},{64,80},{80,64},{96,112},{112,96},{1... | collective-permute-start | bytes 2359304 | tf_op jit(solution)/shard_map/ppermute | solution.py:382
  3.2 18.2 %collective-permute-start.1 = (bf16[2,256,512]{2,1,0:T(8,128)(2,1)S(1)}, bf16[2,256,512]{2,1,0:T(8,128)(2,1)}, u32[]{:S(2)}, u32[]{:S(2)}) collective-permute-start(bf16[2,256,512]{2,1,0:T(8,128)(2,1)S(1)} %get-tuple-element.44.refs_4_), channel_id=1, source_target_pairs={{0,32},{16,240},{32,64},{48,16},{64,96},{80,48},{96,128},{112,80},... | collective-permute-start | bytes 1572872 | tf_op jit(solution)/shard_map/ppermute | solution.py:383
  7.5 10.0 %collective-permute-start.2 = (bf16[256,512]{1,0:T(8,128)(2,1)S(1)}, bf16[256,512]{1,0:T(8,128)(2,1)S(1)}, u32[]{:S(2)}, u32[]{:S(2)}) collective-permute-start(bf16[256,512]{1,0:T(8,128)(2,1)S(1)} %get-tuple-element.45.refs_2_.refs_3_), channel_id=1, source_target_pairs={{256,0},{272,16},{288,32},{304,48},{320,64},{336,80},{352,96},{368... | collective-permute-start | bytes 786440 | tf_op jit(solution)/shard_map/ppermute | solution.py:395
  13.8 15.8 %collective-permute-start.7 = (bf16[2,256,512]{2,1,0:T(8,128)(2,1)}, bf16[2,256,512]{2,1,0:T(8,128)(2,1)S(1)}, u32[]{:S(2)}, u32[]{:S(2)}) collective-permute-start(bf16[2,256,512]{2,1,0:T(8,128)(2,1)} %slice.8), channel_id=1, source_target_pairs={{0,32},{16,240},{32,64},{48,16},{64,96},{80,48},{96,128},{112,80},... | collective-permute-start | bytes 1572872 | tf_op jit(solution)/shard_map/ppermute | solution.py:383
  21.4 12.5 %collective-permute-start.4 = (bf16[2,256,512]{2,1,0:T(8,128)(2,1)}, bf16[2,256,512]{2,1,0:T(8,128)(2,1)S(1)}, u32[]{:S(2)}, u32[]{:S(2)}) collective-permute-start(bf16[2,256,512]{2,1,0:T(8,128)(2,1)} %collective-permute-done.1.refs_4_.refs_5_), channel_id=1, source_target_pairs={{0,32},{16,240},{32,64},{48,16},{64,96},{80,48},{96,128},{112,80},... | collective-permute-start | bytes 1572872 | tf_op jit(solution)/shard_map/ppermute | solution.py:383
  25.4 6.1 %collective-permute-start.3 = (bf16[256,512]{1,0:T(8,128)(2,1)S(1)}, bf16[256,512]{1,0:T(8,128)(2,1)S(1)}, u32[]{:S(2)}, u32[]{:S(2)}) collective-permute-start(bf16[256,512]{1,0:T(8,128)(2,1)S(1)} %collective-permute-done.2.refs_2_), channel_id=1, source_target_pairs={{0,16},{16,0},{32,48},{48,32},{64,80},{80,64},{96,112},{112,96},{1... | collective-permute-start | bytes 786440 | tf_op jit(solution)/shard_map/ppermute | solution.py:404
  29.6 12.3 %collective-permute-start.8 = (bf16[2,256,512]{2,1,0:T(8,128)(2,1)S(1)}, bf16[2,256,512]{2,1,0:T(8,128)(2,1)S(1)}, u32[]{:S(2)}, u32[]{:S(2)}) collective-permute-start(bf16[2,256,512]{2,1,0:T(8,128)(2,1)S(1)} %collective-permute-done.7.refs_4_), channel_id=1, source_target_pairs={{0,32},{16,240},{32,64},{48,16},{64,96},{80,48},{96,128},{112,80},... | collective-permute-start | bytes 1572872 | tf_op jit(solution)/shard_map/ppermute | solution.py:383
  33.9 13.7 %collective-permute-start.5 = (bf16[2,256,512]{2,1,0:T(8,128)(2,1)S(1)}, bf16[2,256,512]{2,1,0:T(8,128)(2,1)S(1)}, u32[]{:S(2)}, u32[]{:S(2)}) collective-permute-start(bf16[2,256,512]{2,1,0:T(8,128)(2,1)S(1)} %collective-permute-done.4.refs_5_), channel_id=1, source_target_pairs={{0,32},{16,240},{32,64},{48,16},{64,96},{80,48},{96,128},{112,80},... | collective-permute-start | bytes 1572872 | tf_op jit(solution)/shard_map/ppermute | solution.py:383
  41.9 12.3 %collective-permute-start.9 = (bf16[2,256,512]{2,1,0:T(8,128)(2,1)S(1)}, bf16[2,256,512]{2,1,0:T(8,128)(2,1)S(1)}, u32[]{:S(2)}, u32[]{:S(2)}) collective-permute-start(bf16[2,256,512]{2,1,0:T(8,128)(2,1)S(1)} %collective-permute-done.8.refs_6_.refs_4_), channel_id=1, source_target_pairs={{0,32},{16,240},{32,64},{48,16},{64,96},{80,48},{96,128},{112,80},... | collective-permute-start | bytes 1572872 | tf_op jit(solution)/shard_map/ppermute | solution.py:383
  47.5 12.3 %collective-permute-start.6 = (bf16[2,256,512]{2,1,0:T(8,128)(2,1)S(1)}, bf16[2,256,512]{2,1,0:T(8,128)(2,1)S(1)}, u32[]{:S(2)}, u32[]{:S(2)}) collective-permute-start(bf16[2,256,512]{2,1,0:T(8,128)(2,1)S(1)} %collective-permute-done.5.refs_5_), channel_id=1, source_target_pairs={{0,32},{16,240},{32,64},{48,16},{64,96},{80,48},{96,128},{112,80},... | collective-permute-start | bytes 1572872 | tf_op jit(solution)/shard_map/ppermute | solution.py:383
  59.8 3.7 %copy-start = (bf16[3,256,512]{2,1,0:T(8,128)(2,1)S(1)}, bf16[3,256,512]{2,1,0:T(8,128)(2,1)}, u32[]{:S(2)}) copy-start(bf16[3,256,512]{2,1,0:T(8,128)(2,1)} %input_ref.1) | copy-start | bytes 2359300
  61.5 3.8 %collective-permute-start.10 = (bf16[2,528,256]{2,1,0:T(8,128)(2,1)S(1)}, bf16[2,528,256]{2,1,0:T(8,128)(2,1)S(1)}, u32[]{:S(2)}, u32[]{:S(2)}) collective-permute-start(bf16[2,528,256]{2,1,0:T(8,128)(2,1)S(1)} %get-tuple-element.72), channel_id=1, source_target_pairs={{0,16},{16,0},{32,48},{48,32},{64,80},{80,64},{96,112},{112,96},{1... | collective-permute-start | bytes 1622024 | tf_op jit(solution)/shard_map/ppermute | solution.py:435
  65.4 8.7 %copy-start.1 = (f32[7,512]{1,0:T(8,128)S(1)}, f32[7,512]{1,0:T(8,128)}, u32[]{:S(2)}) copy-start(f32[7,512]{1,0:T(8,128)} %filter_ref.1) | copy-start | bytes 43012
  65.4 8.7 %copy-start.2 = (f32[512]{0:T(512)S(1)}, f32[512]{0:T(512)}, u32[]{:S(2)}) copy-start(f32[512]{0:T(512)} %param.11) | copy-start | bytes 6148
  65.5 10.8 %collective-permute-start.11 = (bf16[528,256]{1,0:T(8,128)(2,1)S(1)}, bf16[528,256]{1,0:T(8,128)(2,1)S(1)}, u32[]{:S(2)}, u32[]{:S(2)}) collective-permute-start(bf16[528,256]{1,0:T(8,128)(2,1)S(1)} %shard_map.72), channel_id=1, source_target_pairs={{0,256},{16,272},{32,288},{48,304},{64,320},{80,336},{96,352},{112... | collective-permute-start | bytes 811016 | tf_op jit(solution)/shard_map/ppermute | solution.py:440
  66.8 7.3 %collective-permute-start.12 = (bf16[2,6,512]{2,1,0:T(8,128)(2,1)S(1)}, bf16[2,6,512]{2,1,0:T(8,128)(2,1)S(1)}, u32[]{:S(2)}, u32[]{:S(2)}) collective-permute-start(bf16[2,6,512]{2,1,0:T(8,128)(2,1)S(1)} %slice.7), channel_id=1, source_target_pairs={{0,16},{16,32},{32,48},{48,64},{64,80},{80,96},{96,112},{112,128},... | collective-permute-start | bytes 36872 | tf_op jit(solution)/shard_map/ppermute | solution.py:374
  77.7 19.1 %all-to-all-start = ((f32[16,1,256]{2,1,0:T(1,128)}), f32[16,1,256]{2,1,0:T(1,128)S(1)}, u32[]{:S(2)}, u32[]{:S(2)}) async-start(f32[16,1,256]{2,1,0:T(1,128)} %get-tuple-element.77), calls=%async_computation | async-start | bytes 32768 | tf_op jit(solution)/shard_map/all_to_all | solution.py:445

commit v5 on v4

--- a/solution.py
+++ b/solution.py
@@ -398,12 +398,16 @@
     acc, stat = attend_call(where, queries_near, [(0, a0)], [(NEAR, (0,), None)])
     a1, stat, above = lax.optimization_barrier((a1, stat, above))
     a2 = ring(a1)
-    acc, stat = attend_call(where, queries_near, [(1, a1)], [(NEAR, (0,), (acc, stat))])
     stat, late = after(stat, above)
     b1, stat = after(b1, stat)
     queries_all = (own_all, other, above, lax.ppermute(late, "ctx", CORES))
     b2 = ring(b1)
-    high = attend_call(where, queries_all, [(0, a0), (1, a1)], [(ABOVE, (0, 1), None)])
+    acc, stat, *high = attend_call(
+        where,
+        queries_all,
+        [(0, a0), (1, a1)],
+        [(NEAR, (1,), (acc, stat)), (ABOVE, (0, 1), None)],
+    )
     a2, mark = after(a2, high[1])
     a3 = ring(a2)
     high = attend_call(

time: 98.2 us -> 96.3 us (0.981)
  Pallas kernels: 17.7 us -> 16.7 us
    pallas_call x7 -> x6, Pallas kernels: 13.2 us -> 12.1 us  [attend_call(): pl.pallas_call(functools.partial(attend_kernel, places, [(tiles, used, st...]
  transfers between devices with their start and end apart: 14 -> 14, of which waited for: 10 -> 10; matrix products, arithmetic and copies ran while one was open for 1% -> 1% of each run, Pallas kernels for 13% -> 12%
where the time goes in v5:
time: 96.3 us; the launch traced here: 95.7 us
  starting transfers between devices  41.3 us (43%)
  waiting for transfers between devices  36.4 us (38%)
  Pallas kernels  16.7 us (17%)
    ppermute x7, waiting for transfers between devices, on_device(): ring = lambda chunk: lax.ppermute(chunk, 'ctx', RING)  18.2 us
    ppermute x7, starting transfers between devices, on_device(): ring = lambda chunk: lax.ppermute(chunk, 'ctx', RING)  15.7 us
    pallas_call x6, Pallas kernels, attend_call(): pl.pallas_call(functools.partial(attend_kernel, places, [(tiles, used, st...  12.1 us
    all_to_all x1, waiting for transfers between devices, on_device(): spread = lax.all_to_all(squares, 'heads', 0, 0, tiled=True)  9.84 us
    all_to_all x1, starting transfers between devices, on_device(): spread = lax.all_to_all(squares, 'heads', 0, 0, tiled=True)  8.77 us
    ppermute x1, starting transfers between devices, on_device(): above = lax.ppermute(turned, 'ctx', DOWN)  5.47 us
    ppermute x1, waiting for transfers between devices, rim_of(): return lax.ppermute(tails, 'ctx', [(i, i + 1) for i in range(size - 1)])  5.22 us
    ppermute x1, starting transfers between devices, on_device(): queries_all = (own_all, other, above, lax.ppermute(late, 'ctx', CORES))  4.19 us
  transfers between devices with their start and end apart: 14, of which 10 were waited for; matrix products, arithmetic and copies ran while one was open for 1% of the time, Pallas kernels for 12%

profile of v5, /device:TPU:2, one launch (start us, length us, event | category | flops | bytes accessed | tf_op | source)
XLA Modules:
  0.0 95.7 jit_solution(14204676814024048860)
XLA Ops:
  0.0 1.2 %shard_map.64 = (bf16[2,256,512]{2,1,0:T(8,128)(2,1)S(1)}, bf16[3,256,512]{2,1,0:T(8,128)(2,1)S(1)}, bf16[256,512]{1,0:T(8,128)(2,1)S(1)}) custom-call(bf16[256,512]{1,0:T(8,128)(2,1)} %k_ref.1, bf16[256,512]{1,0:T(8,128)(2,1)} %v_ref.1, bf16[256,512]{1,0:T(8,128)(2,1)} %q_ref.1), custom_call_target="tpu_custom_call" | custom-call | tf_op jit(solution)/shard_map/pallas_call | solution.py:89
  1.2 1.9 %collective-permute-start = (bf16[3,256,512]{2,1,0:T(8,128)(2,1)S(1)}, bf16[3,256,512]{2,1,0:T(8,128)(2,1)S(1)}, u32[]{:S(2)}, u32[]{:S(2)}) collective-permute-start(bf16[3,256,512]{2,1,0:T(8,128)(2,1)S(1)} %get-tuple-element.43.refs_0_), channel_id=1, source_target_pairs={{0,16},{16,0},{32,48},{48,32},{64,80},{80,64},{96,112},{112,96},{1... | collective-permute-start | bytes 2359304 | tf_op jit(solution)/shard_map/ppermute | solution.py:382
  3.2 4.3 %collective-permute-start.1 = (bf16[2,256,512]{2,1,0:T(8,128)(2,1)S(1)}, bf16[2,256,512]{2,1,0:T(8,128)(2,1)}, u32[]{:S(2)}, u32[]{:S(2)}) collective-permute-start(bf16[2,256,512]{2,1,0:T(8,128)(2,1)S(1)} %get-tuple-element.44.refs_4_), channel_id=1, source_target_pairs={{0,32},{16,240},{32,64},{48,16},{64,96},{80,48},{96,128},{112,80},... | collective-permute-start | bytes 1572872 | tf_op jit(solution)/shard_map/ppermute | solution.py:383
  7.5 5.5 %collective-permute-start.2 = (bf16[256,512]{1,0:T(8,128)(2,1)S(1)}, bf16[256,512]{1,0:T(8,128)(2,1)S(1)}, u32[]{:S(2)}, u32[]{:S(2)}) collective-permute-start(bf16[256,512]{1,0:T(8,128)(2,1)S(1)} %get-tuple-element.45.refs_2_.refs_3_), channel_id=1, source_target_pairs={{256,0},{272,16},{288,32},{304,48},{320,64},{336,80},{352,96},{368... | collective-permute-start | bytes 786440 | tf_op jit(solution)/shard_map/ppermute | solution.py:395
  12.9 0.0 collective-permute-done.refs_1_
  12.9 0.8 slice.8
  13.8 1.9 %collective-permute-start.5 = (bf16[2,256,512]{2,1,0:T(8,128)(2,1)}, bf16[2,256,512]{2,1,0:T(8,128)(2,1)S(1)}, u32[]{:S(2)}, u32[]{:S(2)}) collective-permute-start(bf16[2,256,512]{2,1,0:T(8,128)(2,1)} %slice.8), channel_id=1, source_target_pairs={{0,32},{16,240},{32,64},{48,16},{64,96},{80,48},{96,128},{112,80},... | collective-permute-start | bytes 1572872 | tf_op jit(solution)/shard_map/ppermute | solution.py:383
  15.8 0.1 stack.55.where_ref
  15.9 1.5 %shard_map.65 = (f32[2,512,256]{2,1,0:T(8,128)S(1)}, f32[2,8,256]{2,1,0:T(8,128)S(1)}) custom-call(s32[13]{0:T(128)S(1)} %stack.55.where_ref, bf16[3,256,512]{2,1,0:T(8,128)(2,1)S(1)} %get-tuple-element.43.refs_0_, bf16[3,256,512]{2,1,0:T(8,128)(2,1)S(1)} %collective-permute-done.refs_1_, bf16[256,512]{1,0:T(8,128)(2,1)S(1)} %get-tuple-element.45.refs_2_.refs_3_, ...), custom_call_target="tpu_custom_call" | custom-call | flops 268435456 | bytes 1048576 | tf_op jit(solution)/shard_map/pallas_call | solution.py:230
  17.5 0.0 collective-permute-done.2.refs_2_
  17.5 3.9 %collective-permute-done.1.refs_5_ = bf16[2,256,512]{2,1,0:T(8,128)(2,1)} collective-permute-done((bf16[2,256,512]{2,1,0:T(8,128)(2,1)S(1)}, bf16[2,256,512]{2,1,0:T(8,128)(2,1)}, u32[]{:S(2)}, u32[]{:S(2)}) %collective-permute-start.1) | collective-permute-done | bytes 524320 | tf_op jit(solution)/shard_map/ppermute | solution.py:383
  21.4 1.9 %collective-permute-start.4 = (bf16[2,256,512]{2,1,0:T(8,128)(2,1)}, bf16[2,256,512]{2,1,0:T(8,128)(2,1)S(1)}, u32[]{:S(2)}, u32[]{:S(2)}) collective-permute-start(bf16[2,256,512]{2,1,0:T(8,128)(2,1)} %collective-permute-done.1.refs_5_), channel_id=1, source_target_pairs={{0,32},{16,240},{32,64},{48,16},{64,96},{80,48},{96,128},{112,80},... | collective-permute-start | bytes 1572872 | tf_op jit(solution)/shard_map/ppermute | solution.py:383
  23.3 4.2 %collective-permute-start.3 = (bf16[256,512]{1,0:T(8,128)(2,1)S(1)}, bf16[256,512]{1,0:T(8,128)(2,1)S(1)}, u32[]{:S(2)}, u32[]{:S(2)}) collective-permute-start(bf16[256,512]{1,0:T(8,128)(2,1)S(1)} %collective-permute-done.2.refs_2_), channel_id=1, source_target_pairs={{0,16},{16,0},{32,48},{48,32},{64,80},{80,64},{96,112},{112,96},{1... | collective-permute-start | bytes 786440 | tf_op jit(solution)/shard_map/ppermute | solution.py:403
  27.5 0.0 collective-permute-done.5.refs_4_
  27.5 1.9 %collective-permute-start.8 = (bf16[2,256,512]{2,1,0:T(8,128)(2,1)S(1)}, bf16[2,256,512]{2,1,0:T(8,128)(2,1)S(1)}, u32[]{:S(2)}, u32[]{:S(2)}) collective-permute-start(bf16[2,256,512]{2,1,0:T(8,128)(2,1)S(1)} %collective-permute-done.5.refs_4_), channel_id=1, source_target_pairs={{0,32},{16,240},{32,64},{48,16},{64,96},{80,48},{96,128},{112,80},... | collective-permute-start | bytes 1572872 | tf_op jit(solution)/shard_map/ppermute | solution.py:383
  29.4 0.0 collective-permute-done.3.refs_3_
  29.4 2.2 %shard_map.66 = (f32[2,512,256]{2,1,0:T(8,128)S(1)}, f32[2,8,256]{2,1,0:T(8,128)S(1)}, f32[2,512,256]{2,1,0:T(8,128)S(1)}, f32[2,8,256]{2,1,0:T(8,128)S(1)}) custom-call(s32[13]{0:T(128)S(1)} %stack.55.where_ref, bf16[3,256,512]{2,1,0:T(8,128)(2,1)S(1)} %get-tuple-element.43.refs_0_, bf16[3,256,512]{2,1,0:T(8,128)(2,1)S(1)} %collective-permute-done.refs_1_, ...), custom_call_target="tpu_custom_call" | custom-call | flops 805306368 | bytes 3145728 | tf_op jit(solution)/shard_map/pallas_call | solution.py:230
  31.7 2.2 %collective-permute-done.4.refs_5_ = bf16[2,256,512]{2,1,0:T(8,128)(2,1)S(1)} collective-permute-done((bf16[2,256,512]{2,1,0:T(8,128)(2,1)}, bf16[2,256,512]{2,1,0:T(8,128)(2,1)S(1)}, u32[]{:S(2)}, u32[]{:S(2)}) %collective-permute-start.4) | collective-permute-done | bytes 524320 | tf_op jit(solution)/shard_map/ppermute | solution.py:383
  33.9 1.9 %collective-permute-start.6 = (bf16[2,256,512]{2,1,0:T(8,128)(2,1)S(1)}, bf16[2,256,512]{2,1,0:T(8,128)(2,1)S(1)}, u32[]{:S(2)}, u32[]{:S(2)}) collective-permute-start(bf16[2,256,512]{2,1,0:T(8,128)(2,1)S(1)} %collective-permute-done.4.refs_5_), channel_id=1, source_target_pairs={{0,32},{16,240},{32,64},{48,16},{64,96},{80,48},{96,128},{112,80},... | collective-permute-start | bytes 1572872 | tf_op jit(solution)/shard_map/ppermute | solution.py:383
  35.8 0.6 shard_map.67
  36.4 3.4 %collective-permute-done.8.refs_6_.refs_4_ = bf16[2,256,512]{2,1,0:T(8,128)(2,1)S(1)} collective-permute-done((bf16[2,256,512]{2,1,0:T(8,128)(2,1)S(1)}, bf16[2,256,512]{2,1,0:T(8,128)(2,1)S(1)}, u32[]{:S(2)}, u32[]{:S(2)}) %collective-permute-start.8) | collective-permute-done | bytes 524320 | tf_op jit(solution)/shard_map/ppermute | solution.py:383
  39.8 1.9 %collective-permute-start.9 = (bf16[2,256,512]{2,1,0:T(8,128)(2,1)S(1)}, bf16[2,256,512]{2,1,0:T(8,128)(2,1)S(1)}, u32[]{:S(2)}, u32[]{:S(2)}) collective-permute-start(bf16[2,256,512]{2,1,0:T(8,128)(2,1)S(1)} %collective-permute-done.8.refs_6_.refs_4_), channel_id=1, source_target_pairs={{0,32},{16,240},{32,64},{48,16},{64,96},{80,48},{96,128},{112,80},... | collective-permute-start | bytes 1572872 | tf_op jit(solution)/shard_map/ppermute | solution.py:383
  41.7 4.4 %collective-permute-done.6.refs_5_ = bf16[2,256,512]{2,1,0:T(8,128)(2,1)S(1)} collective-permute-done((bf16[2,256,512]{2,1,0:T(8,128)(2,1)S(1)}, bf16[2,256,512]{2,1,0:T(8,128)(2,1)S(1)}, u32[]{:S(2)}, u32[]{:S(2)}) %collective-permute-start.6) | collective-permute-done | bytes 524320 | tf_op jit(solution)/shard_map/ppermute | solution.py:383
  46.1 1.9 %collective-permute-start.7 = (bf16[2,256,512]{2,1,0:T(8,128)(2,1)S(1)}, bf16[2,256,512]{2,1,0:T(8,128)(2,1)S(1)}, u32[]{:S(2)}, u32[]{:S(2)}) collective-permute-start(bf16[2,256,512]{2,1,0:T(8,128)(2,1)S(1)} %collective-permute-done.6.refs_5_), channel_id=1, source_target_pairs={{0,32},{16,240},{32,64},{48,16},{64,96},{80,48},{96,128},{112,80},... | collective-permute-start | bytes 1572872 | tf_op jit(solution)/shard_map/ppermute | solution.py:383
  48.1 3.3 %shard_map.68 = (f32[2,512,256]{2,1,0:T(8,128)S(1)}, f32[2,8,256]{2,1,0:T(8,128)S(1)}) custom-call(s32[13]{0:T(128)S(1)} %stack.55.where_ref, bf16[3,256,512]{2,1,0:T(8,128)(2,1)S(1)} %get-tuple-element.43.refs_0_, bf16[3,256,512]{2,1,0:T(8,128)(2,1)S(1)} %collective-permute-done.refs_1_, bf16[256,512]{1,0:T(8,128)(2,1)S(1)} %get-tuple-element.45.refs_2_.refs_3_, ...), custom_call_target="tpu_custom_call" | custom-call | flops 805306368 | bytes 3145728 | tf_op jit(solution)/shard_map/pallas_call | solution.py:230
  51.4 0.7 collective-permute-done.9.refs_6_
  52.1 2.7 %shard_map.69 = (f32[2,512,256]{2,1,0:T(8,128)S(1)}, f32[2,8,256]{2,1,0:T(8,128)S(1)}, f32[2,512,256]{2,1,0:T(8,128)S(1)}, f32[2,8,256]{2,1,0:T(8,128)S(1)}) custom-call(s32[13]{0:T(128)S(1)} %stack.55.where_ref, bf16[3,256,512]{2,1,0:T(8,128)(2,1)S(1)} %get-tuple-element.43.refs_0_, bf16[3,256,512]{2,1,0:T(8,128)(2,1)S(1)} %collective-permute-done.refs_1_, ...), custom_call_target="tpu_custom_call" | custom-call | flops 1342177280 | bytes 5242880 | tf_op jit(solution)/shard_map/pallas_call | solution.py:230
  54.8 3.6 %collective-permute-done.7.refs_4_ = bf16[2,256,512]{2,1,0:T(8,128)(2,1)S(1)} collective-permute-done((bf16[2,256,512]{2,1,0:T(8,128)(2,1)S(1)}, bf16[2,256,512]{2,1,0:T(8,128)(2,1)S(1)}, u32[]{:S(2)}, u32[]{:S(2)}) %collective-permute-start.7) | collective-permute-done | bytes 524320 | tf_op jit(solution)/shard_map/ppermute | solution.py:383
  58.4 0.0 copy-start
  58.4 1.7 %shard_map.70 = (bf16[2,528,256]{2,1,0:T(8,128)(2,1)S(1)}, bf16[2,528,256]{2,1,0:T(8,128)(2,1)S(1)}) custom-call(s32[13]{0:T(128)S(1)} %stack.55.where_ref, bf16[3,256,512]{2,1,0:T(8,128)(2,1)S(1)} %get-tuple-element.43.refs_0_, bf16[3,256,512]{2,1,0:T(8,128)(2,1)S(1)} %collective-permute-done.refs_1_, bf16[256,512]{1,0:T(8,128)(2,1)S(1)} %collective-permute-done.2.refs_2_, ...), custom_call_target="tpu_custom_call" | custom-call | flops 536870912 | bytes 2097152 | tf_op jit(solution)/shard_map/pallas_call | solution.py:230
  60.1 1.9 %collective-permute-start.10 = (bf16[2,528,256]{2,1,0:T(8,128)(2,1)S(1)}, bf16[2,528,256]{2,1,0:T(8,128)(2,1)S(1)}, u32[]{:S(2)}, u32[]{:S(2)}) collective-permute-start(bf16[2,528,256]{2,1,0:T(8,128)(2,1)S(1)} %get-tuple-element.72), channel_id=1, source_target_pairs={{0,16},{16,0},{32,48},{48,32},{64,80},{80,64},{96,112},{112,96},{1... | collective-permute-start | bytes 1622024 | tf_op jit(solution)/shard_map/ppermute | solution.py:439
  62.1 0.0 copy-done
  62.1 1.9 %collective-permute-done.10.b_ref = bf16[2,528,256]{2,1,0:T(8,128)(2,1)S(1)} collective-permute-done((bf16[2,528,256]{2,1,0:T(8,128)(2,1)S(1)}, bf16[2,528,256]{2,1,0:T(8,128)(2,1)S(1)}, u32[]{:S(2)}, u32[]{:S(2)}) %collective-permute-start.10) | collective-permute-done | bytes 540704 | tf_op jit(solution)/shard_map/ppermute | solution.py:439
  64.0 0.0 copy-start.1
  64.0 0.0 copy-start.2
  64.0 0.1 shard_map.71
  64.1 1.3 %collective-permute-start.11 = (bf16[528,256]{1,0:T(8,128)(2,1)S(1)}, bf16[528,256]{1,0:T(8,128)(2,1)S(1)}, u32[]{:S(2)}, u32[]{:S(2)}) collective-permute-start(bf16[528,256]{1,0:T(8,128)(2,1)S(1)} %shard_map.71), channel_id=1, source_target_pairs={{0,256},{16,272},{32,288},{48,304},{64,320},{80,336},{96,352},{112... | collective-permute-start | bytes 811016 | tf_op jit(solution)/shard_map/ppermute | solution.py:444
  65.4 2.0 %collective-permute-start.12 = (bf16[2,6,512]{2,1,0:T(8,128)(2,1)S(1)}, bf16[2,6,512]{2,1,0:T(8,128)(2,1)S(1)}, u32[]{:S(2)}, u32[]{:S(2)}) collective-permute-start(bf16[2,6,512]{2,1,0:T(8,128)(2,1)S(1)} %slice.7), channel_id=1, source_target_pairs={{0,16},{16,32},{32,48},{48,64},{64,80},{80,96},{96,112},{112,128},... | collective-permute-start | bytes 36872 | tf_op jit(solution)/shard_map/ppermute | solution.py:374
  67.5 5.2 %collective-permute-done.12.rim_ref = bf16[2,6,512]{2,1,0:T(8,128)(2,1)S(1)} collective-permute-done((bf16[2,6,512]{2,1,0:T(8,128)(2,1)S(1)}, bf16[2,6,512]{2,1,0:T(8,128)(2,1)S(1)}, u32[]{:S(2)}, u32[]{:S(2)}) %collective-permute-start.12) | collective-permute-done | bytes 12320 | tf_op jit(solution)/shard_map/ppermute | solution.py:374
  72.7 0.0 copy-done.1
  72.7 0.0 copy-done.2
  72.7 0.8 shard_map.72
  73.5 1.2 %collective-permute-done.11.s_ref = bf16[528,256]{1,0:T(8,128)(2,1)S(1)} collective-permute-done((bf16[528,256]{1,0:T(8,128)(2,1)S(1)}, bf16[528,256]{1,0:T(8,128)(2,1)S(1)}, u32[]{:S(2)}, u32[]{:S(2)}) %collective-permute-start.11) | collective-permute-done | bytes 270368 | tf_op jit(solution)/shard_map/ppermute | solution.py:444
  74.7 1.4 %shard_map.73 = (bf16[512,256]{1,0:T(8,128)(2,1)S(1)}, f32[16,1,256]{2,1,0:T(1,128)}) custom-call(s32[13]{0:T(128)S(1)} %stack.55.where_ref, bf16[2,528,256]{2,1,0:T(8,128)(2,1)S(1)} %get-tuple-element.71.a_ref, bf16[2,528,256]{2,1,0:T(8,128)(2,1)S(1)} %collective-permute-done.10.b_ref, bf16[528,256]{1,0:T(8,128)(2,1)S(1)} %collective-permute-done.11.s_ref), custom_call_target="tpu_custom_call" | custom-call | tf_op jit(solution)/shard_map/pallas_call | solution.py:309
  76.1 8.8 %all-to-all-start = ((f32[16,1,256]{2,1,0:T(1,128)}), f32[16,1,256]{2,1,0:T(1,128)S(1)}, u32[]{:S(2)}, u32[]{:S(2)}) async-start(f32[16,1,256]{2,1,0:T(1,128)} %get-tuple-element.77), calls=%async_computation | async-start | bytes 32768 | tf_op jit(solution)/shard_map/all_to_all | solution.py:449
  84.9 0.1 shard_map.74.wide_ref
  85.0 9.8 %all-to-all-done.spread_ref = f32[16,1,256]{2,1,0:T(1,128)S(1)} async-done(((f32[16,1,256]{2,1,0:T(1,128)}), f32[16,1,256]{2,1,0:T(1,128)S(1)}, u32[]{:S(2)}, u32[]{:S(2)}) %all-to-all-start) | async-done | bytes 16416 | tf_op jit(solution)/shard_map/all_to_all | solution.py:449
  94.9 0.9 shard_map.75
  (1 shorter events, 0.0 us)
Async XLA Ops:
  1.2 11.7 %collective-permute-start = (bf16[3,256,512]{2,1,0:T(8,128)(2,1)S(1)}, bf16[3,256,512]{2,1,0:T(8,128)(2,1)S(1)}, u32[]{:S(2)}, u32[]{:S(2)}) collective-permute-start(bf16[3,256,512]{2,1,0:T(8,128)(2,1)S(1)} %get-tuple-element.43.refs_0_), channel_id=1, source_target_pairs={{0,16},{16,0},{32,48},{48,32},{64,80},{80,64},{96,112},{112,96},{1... | collective-permute-start | bytes 2359304 | tf_op jit(solution)/shard_map/ppermute | solution.py:382
  3.2 18.2 %collective-permute-start.1 = (bf16[2,256,512]{2,1,0:T(8,128)(2,1)S(1)}, bf16[2,256,512]{2,1,0:T(8,128)(2,1)}, u32[]{:S(2)}, u32[]{:S(2)}) collective-permute-start(bf16[2,256,512]{2,1,0:T(8,128)(2,1)S(1)} %get-tuple-element.44.refs_4_), channel_id=1, source_target_pairs={{0,32},{16,240},{32,64},{48,16},{64,96},{80,48},{96,128},{112,80},... | collective-permute-start | bytes 1572872 | tf_op jit(solution)/shard_map/ppermute | solution.py:383
  7.5 10.0 %collective-permute-start.2 = (bf16[256,512]{1,0:T(8,128)(2,1)S(1)}, bf16[256,512]{1,0:T(8,128)(2,1)S(1)}, u32[]{:S(2)}, u32[]{:S(2)}) collective-permute-start(bf16[256,512]{1,0:T(8,128)(2,1)S(1)} %get-tuple-element.45.refs_2_.refs_3_), channel_id=1, source_target_pairs={{256,0},{272,16},{288,32},{304,48},{320,64},{336,80},{352,96},{368... | collective-permute-start | bytes 786440 | tf_op jit(solution)/shard_map/ppermute | solution.py:395
  13.8 13.7 %collective-permute-start.5 = (bf16[2,256,512]{2,1,0:T(8,128)(2,1)}, bf16[2,256,512]{2,1,0:T(8,128)(2,1)S(1)}, u32[]{:S(2)}, u32[]{:S(2)}) collective-permute-start(bf16[2,256,512]{2,1,0:T(8,128)(2,1)} %slice.8), channel_id=1, source_target_pairs={{0,32},{16,240},{32,64},{48,16},{64,96},{80,48},{96,128},{112,80},... | collective-permute-start | bytes 1572872 | tf_op jit(solution)/shard_map/ppermute | solution.py:383
  21.4 12.5 %collective-permute-start.4 = (bf16[2,256,512]{2,1,0:T(8,128)(2,1)}, bf16[2,256,512]{2,1,0:T(8,128)(2,1)S(1)}, u32[]{:S(2)}, u32[]{:S(2)}) collective-permute-start(bf16[2,256,512]{2,1,0:T(8,128)(2,1)} %collective-permute-done.1.refs_5_), channel_id=1, source_target_pairs={{0,32},{16,240},{32,64},{48,16},{64,96},{80,48},{96,128},{112,80},... | collective-permute-start | bytes 1572872 | tf_op jit(solution)/shard_map/ppermute | solution.py:383
  23.3 6.1 %collective-permute-start.3 = (bf16[256,512]{1,0:T(8,128)(2,1)S(1)}, bf16[256,512]{1,0:T(8,128)(2,1)S(1)}, u32[]{:S(2)}, u32[]{:S(2)}) collective-permute-start(bf16[256,512]{1,0:T(8,128)(2,1)S(1)} %collective-permute-done.2.refs_2_), channel_id=1, source_target_pairs={{0,16},{16,0},{32,48},{48,32},{64,80},{80,64},{96,112},{112,96},{1... | collective-permute-start | bytes 786440 | tf_op jit(solution)/shard_map/ppermute | solution.py:403
  27.5 12.3 %collective-permute-start.8 = (bf16[2,256,512]{2,1,0:T(8,128)(2,1)S(1)}, bf16[2,256,512]{2,1,0:T(8,128)(2,1)S(1)}, u32[]{:S(2)}, u32[]{:S(2)}) collective-permute-start(bf16[2,256,512]{2,1,0:T(8,128)(2,1)S(1)} %collective-permute-done.5.refs_4_), channel_id=1, source_target_pairs={{0,32},{16,240},{32,64},{48,16},{64,96},{80,48},{96,128},{112,80},... | collective-permute-start | bytes 1572872 | tf_op jit(solution)/shard_map/ppermute | solution.py:383
  33.9 12.3 %collective-permute-start.6 = (bf16[2,256,512]{2,1,0:T(8,128)(2,1)S(1)}, bf16[2,256,512]{2,1,0:T(8,128)(2,1)S(1)}, u32[]{:S(2)}, u32[]{:S(2)}) collective-permute-start(bf16[2,256,512]{2,1,0:T(8,128)(2,1)S(1)} %collective-permute-done.4.refs_5_), channel_id=1, source_target_pairs={{0,32},{16,240},{32,64},{48,16},{64,96},{80,48},{96,128},{112,80},... | collective-permute-start | bytes 1572872 | tf_op jit(solution)/shard_map/ppermute | solution.py:383
  39.8 12.3 %collective-permute-start.9 = (bf16[2,256,512]{2,1,0:T(8,128)(2,1)S(1)}, bf16[2,256,512]{2,1,0:T(8,128)(2,1)S(1)}, u32[]{:S(2)}, u32[]{:S(2)}) collective-permute-start(bf16[2,256,512]{2,1,0:T(8,128)(2,1)S(1)} %collective-permute-done.8.refs_6_.refs_4_), channel_id=1, source_target_pairs={{0,32},{16,240},{32,64},{48,16},{64,96},{80,48},{96,128},{112,80},... | collective-permute-start | bytes 1572872 | tf_op jit(solution)/shard_map/ppermute | solution.py:383
  46.1 12.3 %collective-permute-start.7 = (bf16[2,256,512]{2,1,0:T(8,128)(2,1)S(1)}, bf16[2,256,512]{2,1,0:T(8,128)(2,1)S(1)}, u32[]{:S(2)}, u32[]{:S(2)}) collective-permute-start(bf16[2,256,512]{2,1,0:T(8,128)(2,1)S(1)} %collective-permute-done.6.refs_5_), channel_id=1, source_target_pairs={{0,32},{16,240},{32,64},{48,16},{64,96},{80,48},{96,128},{112,80},... | collective-permute-start | bytes 1572872 | tf_op jit(solution)/shard_map/ppermute | solution.py:383
  58.4 3.7 %copy-start = (bf16[3,256,512]{2,1,0:T(8,128)(2,1)S(1)}, bf16[3,256,512]{2,1,0:T(8,128)(2,1)}, u32[]{:S(2)}) copy-start(bf16[3,256,512]{2,1,0:T(8,128)(2,1)} %input_ref.1) | copy-start | bytes 2359300
  60.1 3.8 %collective-permute-start.10 = (bf16[2,528,256]{2,1,0:T(8,128)(2,1)S(1)}, bf16[2,528,256]{2,1,0:T(8,128)(2,1)S(1)}, u32[]{:S(2)}, u32[]{:S(2)}) collective-permute-start(bf16[2,528,256]{2,1,0:T(8,128)(2,1)S(1)} %get-tuple-element.72), channel_id=1, source_target_pairs={{0,16},{16,0},{32,48},{48,32},{64,80},{80,64},{96,112},{112,96},{1... | collective-permute-start | bytes 1622024 | tf_op jit(solution)/shard_map/ppermute | solution.py:439
  64.0 8.7 %copy-start.1 = (f32[7,512]{1,0:T(8,128)S(1)}, f32[7,512]{1,0:T(8,128)}, u32[]{:S(2)}) copy-start(f32[7,512]{1,0:T(8,128)} %filter_ref.1) | copy-start | bytes 43012
  64.0 8.7 %copy-start.2 = (f32[512]{0:T(512)S(1)}, f32[512]{0:T(512)}, u32[]{:S(2)}) copy-start(f32[512]{0:T(512)} %param.11) | copy-start | bytes 6148
  64.1 10.6 %collective-permute-start.11 = (bf16[528,256]{1,0:T(8,128)(2,1)S(1)}, bf16[528,256]{1,0:T(8,128)(2,1)S(1)}, u32[]{:S(2)}, u32[]{:S(2)}) collective-permute-start(bf16[528,256]{1,0:T(8,128)(2,1)S(1)} %shard_map.71), channel_id=1, source_target_pairs={{0,256},{16,272},{32,288},{48,304},{64,320},{80,336},{96,352},{112... | collective-permute-start | bytes 811016 | tf_op jit(solution)/shard_map/ppermute | solution.py:444
  65.4 7.3 %collective-permute-start.12 = (bf16[2,6,512]{2,1,0:T(8,128)(2,1)S(1)}, bf16[2,6,512]{2,1,0:T(8,128)(2,1)S(1)}, u32[]{:S(2)}, u32[]{:S(2)}) collective-permute-start(bf16[2,6,512]{2,1,0:T(8,128)(2,1)S(1)} %slice.7), channel_id=1, source_target_pairs={{0,16},{16,32},{32,48},{48,64},{64,80},{80,96},{96,112},{112,128},... | collective-permute-start | bytes 36872 | tf_op jit(solution)/shard_map/ppermute | solution.py:374
  76.1 18.8 %all-to-all-start = ((f32[16,1,256]{2,1,0:T(1,128)}), f32[16,1,256]{2,1,0:T(1,128)S(1)}, u32[]{:S(2)}, u32[]{:S(2)}) async-start(f32[16,1,256]{2,1,0:T(1,128)} %get-tuple-element.77), calls=%async_computation | async-start | bytes 32768 | tf_op jit(solution)/shard_map/all_to_all | solution.py:449

commit v6 on v5

--- a/solution.py
+++ b/solution.py
@@ -410,24 +410,20 @@
     )
     a2, mark = after(a2, high[1])
     a3 = ring(a2)
-    high = attend_call(
-        where, queries_all, [(6, b1), (2, a2)], [(ABOVE, (0, 1), (high[0], mark))]
+    acc, stat, *high = attend_call(
+        where,
+        queries_all,
+        [(6, b1), (2, a2)],
+        [(NEAR, (0, 1), (acc, stat)), (ABOVE, (0, 1), (high[0], mark))],
     )
     b2, mark = after(b2, high[1])
     b3 = ring(b2)
-    near = attend_call(
-        where,
-        queries_near,
-        [(6, b1), (2, a2), (7, b2)],
-        [(NEAR, (0, 1, 2), (acc, stat))],
-    )
-    stat = near[1]
     a4 = ring(a3)
     *near, acc, stat = attend_call(
         where,
         queries_all,
         [(7, b2), (3, a3), (8, b3)],
-        [(NEAR, (1, 2), (near[0], stat)), (ABOVE, (0, 1, 2), (high[0], mark))],
+        [(NEAR, (0, 1, 2), (acc, stat)), (ABOVE, (0, 1, 2), (high[0], mark))],
     )
     near, far = attend_call(
         where,

time: 96.3 us -> 96.7 us (level)
    pallas_call x6 -> x5, Pallas kernels: 12.1 us -> 11.5 us  [attend_call(): pl.pallas_call(functools.partial(attend_kernel, places, [(tiles, used, st...]
  transfers between devices with their start and end apart: 14 -> 14, of which waited for: 10 -> 10; matrix products, arithmetic and copies ran while one was open for 1% -> 1% of each run, Pallas kernels for 12% -> 11%
where the time goes in v6:
time: 96.7 us; the launch traced here: 96.2 us
  starting transfers between devices  41.6 us (43%)
  waiting for transfers between devices  37.1 us (38%)
  Pallas kernels  16.1 us (17%)
    ppermute x7, waiting for transfers between devices, on_device(): ring = lambda chunk: lax.ppermute(chunk, 'ctx', RING)  18.5 us
    ppermute x7, starting transfers between devices, on_device(): ring = lambda chunk: lax.ppermute(chunk, 'ctx', RING)  15.7 us
    pallas_call x5, Pallas kernels, attend_call(): pl.pallas_call(functools.partial(attend_kernel, places, [(tiles, used, st...  11.5 us
    all_to_all x1, waiting for transfers between devices, on_device(): spread = lax.all_to_all(squares, 'heads', 0, 0, tiled=True)  9.84 us
    all_to_all x1, starting transfers between devices, on_device(): spread = lax.all_to_all(squares, 'heads', 0, 0, tiled=True)  9.06 us
    ppermute x1, starting transfers between devices, on_device(): above = lax.ppermute(turned, 'ctx', DOWN)  5.47 us
    ppermute x1, waiting for transfers between devices, rim_of(): return lax.ppermute(tails, 'ctx', [(i, i + 1) for i in range(size - 1)])  5.22 us
    ppermute x1, starting transfers between devices, on_device(): queries_all = (own_all, other, above, lax.ppermute(late, 'ctx', CORES))  4.19 us
  transfers between devices with their start and end apart: 14, of which 10 were waited for; matrix products, arithmetic and copies ran while one was open for 1% of the time, Pallas kernels for 11%

profile of v6, /device:TPU:2, one launch (start us, length us, event | category | flops | bytes accessed | tf_op | source)
XLA Modules:
  0.0 96.2 jit_solution(389246877011586701)
XLA Ops:
  0.0 1.2 %shard_map.64 = (bf16[2,256,512]{2,1,0:T(8,128)(2,1)S(1)}, bf16[3,256,512]{2,1,0:T(8,128)(2,1)S(1)}, bf16[256,512]{1,0:T(8,128)(2,1)S(1)}) custom-call(bf16[256,512]{1,0:T(8,128)(2,1)} %k_ref.1, bf16[256,512]{1,0:T(8,128)(2,1)} %v_ref.1, bf16[256,512]{1,0:T(8,128)(2,1)} %q_ref.1), custom_call_target="tpu_custom_call" | custom-call | tf_op jit(solution)/shard_map/pallas_call | solution.py:89
  1.2 1.9 %collective-permute-start = (bf16[3,256,512]{2,1,0:T(8,128)(2,1)S(1)}, bf16[3,256,512]{2,1,0:T(8,128)(2,1)S(1)}, u32[]{:S(2)}, u32[]{:S(2)}) collective-permute-start(bf16[3,256,512]{2,1,0:T(8,128)(2,1)S(1)} %get-tuple-element.43.refs_0_), channel_id=1, source_target_pairs={{0,16},{16,0},{32,48},{48,32},{64,80},{80,64},{96,112},{112,96},{1... | collective-permute-start | bytes 2359304 | tf_op jit(solution)/shard_map/ppermute | solution.py:382
  3.2 4.3 %collective-permute-start.1 = (bf16[2,256,512]{2,1,0:T(8,128)(2,1)S(1)}, bf16[2,256,512]{2,1,0:T(8,128)(2,1)S(1)}, u32[]{:S(2)}, u32[]{:S(2)}) collective-permute-start(bf16[2,256,512]{2,1,0:T(8,128)(2,1)S(1)} %get-tuple-element.44.refs_4_), channel_id=1, source_target_pairs={{0,32},{16,240},{32,64},{48,16},{64,96},{80,48},{96,128},{112,80},... | collective-permute-start | bytes 1572872 | tf_op jit(solution)/shard_map/ppermute | solution.py:383
  7.5 5.5 %collective-permute-start.2 = (bf16[256,512]{1,0:T(8,128)(2,1)S(1)}, bf16[256,512]{1,0:T(8,128)(2,1)S(1)}, u32[]{:S(2)}, u32[]{:S(2)}) collective-permute-start(bf16[256,512]{1,0:T(8,128)(2,1)S(1)} %get-tuple-element.45.refs_2_.refs_3_), channel_id=1, source_target_pairs={{256,0},{272,16},{288,32},{304,48},{320,64},{336,80},{352,96},{368... | collective-permute-start | bytes 786440 | tf_op jit(solution)/shard_map/ppermute | solution.py:395
  12.9 0.0 collective-permute-done.refs_1_
  12.9 0.8 slice.8
  13.8 1.9 %collective-permute-start.5 = (bf16[2,256,512]{2,1,0:T(8,128)(2,1)}, bf16[2,256,512]{2,1,0:T(8,128)(2,1)}, u32[]{:S(2)}, u32[]{:S(2)}) collective-permute-start(bf16[2,256,512]{2,1,0:T(8,128)(2,1)} %slice.8), channel_id=1, source_target_pairs={{0,32},{16,240},{32,64},{48,16},{64,96},{80,48},{96,128},{112,80},... | collective-permute-start | bytes 1572872 | tf_op jit(solution)/shard_map/ppermute | solution.py:383
  15.8 0.1 stack.55.where_ref
  15.9 1.5 %shard_map.65 = (f32[2,512,256]{2,1,0:T(8,128)S(1)}, f32[2,8,256]{2,1,0:T(8,128)S(1)}) custom-call(s32[13]{0:T(128)S(1)} %stack.55.where_ref, bf16[3,256,512]{2,1,0:T(8,128)(2,1)S(1)} %get-tuple-element.43.refs_0_, bf16[3,256,512]{2,1,0:T(8,128)(2,1)S(1)} %collective-permute-done.refs_1_, bf16[256,512]{1,0:T(8,128)(2,1)S(1)} %get-tuple-element.45.refs_2_.refs_3_, ...), custom_call_target="tpu_custom_call" | custom-call | flops 268435456 | bytes 1048576 | tf_op jit(solution)/shard_map/pallas_call | solution.py:230
  17.5 0.0 collective-permute-done.2.refs_2_
  17.5 3.8 %collective-permute-done.1.refs_5_ = bf16[2,256,512]{2,1,0:T(8,128)(2,1)S(1)} collective-permute-done((bf16[2,256,512]{2,1,0:T(8,128)(2,1)S(1)}, bf16[2,256,512]{2,1,0:T(8,128)(2,1)S(1)}, u32[]{:S(2)}, u32[]{:S(2)}) %collective-permute-start.1) | collective-permute-done | bytes 524320 | tf_op jit(solution)/shard_map/ppermute | solution.py:383
  21.3 1.9 %collective-permute-start.4 = (bf16[2,256,512]{2,1,0:T(8,128)(2,1)S(1)}, bf16[2,256,512]{2,1,0:T(8,128)(2,1)S(1)}, u32[]{:S(2)}, u32[]{:S(2)}) collective-permute-start(bf16[2,256,512]{2,1,0:T(8,128)(2,1)S(1)} %collective-permute-done.1.refs_5_), channel_id=1, source_target_pairs={{0,32},{16,240},{32,64},{48,16},{64,96},{80,48},{96,128},{112,80},... | collective-permute-start | bytes 1572872 | tf_op jit(solution)/shard_map/ppermute | solution.py:383
  23.2 4.2 %collective-permute-start.3 = (bf16[256,512]{1,0:T(8,128)(2,1)S(1)}, bf16[256,512]{1,0:T(8,128)(2,1)S(1)}, u32[]{:S(2)}, u32[]{:S(2)}) collective-permute-start(bf16[256,512]{1,0:T(8,128)(2,1)S(1)} %collective-permute-done.2.refs_2_), channel_id=1, source_target_pairs={{0,16},{16,0},{32,48},{48,32},{64,80},{80,64},{96,112},{112,96},{1... | collective-permute-start | bytes 786440 | tf_op jit(solution)/shard_map/ppermute | solution.py:403
  27.4 0.0 collective-permute-done.5.refs_4_
  27.4 1.9 %collective-permute-start.8 = (bf16[2,256,512]{2,1,0:T(8,128)(2,1)}, bf16[2,256,512]{2,1,0:T(8,128)(2,1)S(1)}, u32[]{:S(2)}, u32[]{:S(2)}) collective-permute-start(bf16[2,256,512]{2,1,0:T(8,128)(2,1)} %collective-permute-done.5.refs_4_), channel_id=1, source_target_pairs={{0,32},{16,240},{32,64},{48,16},{64,96},{80,48},{96,128},{112,80},... | collective-permute-start | bytes 1572872 | tf_op jit(solution)/shard_map/ppermute | solution.py:383
  29.3 0.0 collective-permute-done.3.refs_3_
  29.3 1.7 %shard_map.66 = (f32[2,512,256]{2,1,0:T(8,128)S(1)}, f32[2,8,256]{2,1,0:T(8,128)S(1)}, f32[2,512,256]{2,1,0:T(8,128)S(1)}, f32[2,8,256]{2,1,0:T(8,128)S(1)}) custom-call(s32[13]{0:T(128)S(1)} %stack.55.where_ref, bf16[3,256,512]{2,1,0:T(8,128)(2,1)S(1)} %get-tuple-element.43.refs_0_, bf16[3,256,512]{2,1,0:T(8,128)(2,1)S(1)} %collective-permute-done.refs_1_, ...), custom_call_target="tpu_custom_call" | custom-call | flops 805306368 | bytes 3145728 | tf_op jit(solution)/shard_map/pallas_call | solution.py:230
  31.0 2.5 %collective-permute-done.4.refs_5_ = bf16[2,256,512]{2,1,0:T(8,128)(2,1)S(1)} collective-permute-done((bf16[2,256,512]{2,1,0:T(8,128)(2,1)S(1)}, bf16[2,256,512]{2,1,0:T(8,128)(2,1)S(1)}, u32[]{:S(2)}, u32[]{:S(2)}) %collective-permute-start.4) | collective-permute-done | bytes 524320 | tf_op jit(solution)/shard_map/ppermute | solution.py:383
  33.5 1.9 %collective-permute-start.6 = (bf16[2,256,512]{2,1,0:T(8,128)(2,1)S(1)}, bf16[2,256,512]{2,1,0:T(8,128)(2,1)S(1)}, u32[]{:S(2)}, u32[]{:S(2)}) collective-permute-start(bf16[2,256,512]{2,1,0:T(8,128)(2,1)S(1)} %collective-permute-done.4.refs_5_), channel_id=1, source_target_pairs={{0,32},{16,240},{32,64},{48,16},{64,96},{80,48},{96,128},{112,80},... | collective-permute-start | bytes 1572872 | tf_op jit(solution)/shard_map/ppermute | solution.py:383
  35.5 3.0 %shard_map.67 = (f32[2,512,256]{2,1,0:T(8,128)S(1)}, f32[2,8,256]{2,1,0:T(8,128)S(1)}, f32[2,512,256]{2,1,0:T(8,128)S(1)}, f32[2,8,256]{2,1,0:T(8,128)S(1)}) custom-call(s32[13]{0:T(128)S(1)} %stack.55.where_ref, bf16[3,256,512]{2,1,0:T(8,128)(2,1)S(1)} %get-tuple-element.43.refs_0_, bf16[3,256,512]{2,1,0:T(8,128)(2,1)S(1)} %collective-permute-done.refs_1_, ...), custom_call_target="tpu_custom_call" | custom-call | flops 1073741824 | bytes 4194304 | tf_op jit(solution)/shard_map/pallas_call | solution.py:230
  38.5 1.4 %collective-permute-done.8.refs_4_ = bf16[2,256,512]{2,1,0:T(8,128)(2,1)S(1)} collective-permute-done((bf16[2,256,512]{2,1,0:T(8,128)(2,1)}, bf16[2,256,512]{2,1,0:T(8,128)(2,1)S(1)}, u32[]{:S(2)}, u32[]{:S(2)}) %collective-permute-start.8) | collective-permute-done | bytes 524320 | tf_op jit(solution)/shard_map/ppermute | solution.py:383
  39.9 1.9 %collective-permute-start.9 = (bf16[2,256,512]{2,1,0:T(8,128)(2,1)S(1)}, bf16[2,256,512]{2,1,0:T(8,128)(2,1)S(1)}, u32[]{:S(2)}, u32[]{:S(2)}) collective-permute-start(bf16[2,256,512]{2,1,0:T(8,128)(2,1)S(1)} %collective-permute-done.8.refs_4_), channel_id=1, source_target_pairs={{0,32},{16,240},{32,64},{48,16},{64,96},{80,48},{96,128},{112,80},... | collective-permute-start | bytes 1572872 | tf_op jit(solution)/shard_map/ppermute | solution.py:383
  41.8 4.0 %collective-permute-done.6.refs_5_ = bf16[2,256,512]{2,1,0:T(8,128)(2,1)S(1)} collective-permute-done((bf16[2,256,512]{2,1,0:T(8,128)(2,1)S(1)}, bf16[2,256,512]{2,1,0:T(8,128)(2,1)S(1)}, u32[]{:S(2)}, u32[]{:S(2)}) %collective-permute-start.6) | collective-permute-done | bytes 524320 | tf_op jit(solution)/shard_map/ppermute | solution.py:383
  45.8 1.9 %collective-permute-start.7 = (bf16[2,256,512]{2,1,0:T(8,128)(2,1)S(1)}, bf16[2,256,512]{2,1,0:T(8,128)(2,1)S(1)}, u32[]{:S(2)}, u32[]{:S(2)}) collective-permute-start(bf16[2,256,512]{2,1,0:T(8,128)(2,1)S(1)} %collective-permute-done.6.refs_5_), channel_id=1, source_target_pairs={{0,32},{16,240},{32,64},{48,16},{64,96},{80,48},{96,128},{112,80},... | collective-permute-start | bytes 1572872 | tf_op jit(solution)/shard_map/ppermute | solution.py:383
  47.7 4.4 %collective-permute-done.9.refs_6_ = bf16[2,256,512]{2,1,0:T(8,128)(2,1)S(1)} collective-permute-done((bf16[2,256,512]{2,1,0:T(8,128)(2,1)S(1)}, bf16[2,256,512]{2,1,0:T(8,128)(2,1)S(1)}, u32[]{:S(2)}, u32[]{:S(2)}) %collective-permute-start.9) | collective-permute-done | bytes 524320 | tf_op jit(solution)/shard_map/ppermute | solution.py:383
  52.2 3.6 %shard_map.68 = (f32[2,512,256]{2,1,0:T(8,128)S(1)}, f32[2,8,256]{2,1,0:T(8,128)S(1)}, f32[2,512,256]{2,1,0:T(8,128)S(1)}, f32[2,8,256]{2,1,0:T(8,128)S(1)}) custom-call(s32[13]{0:T(128)S(1)} %stack.55.where_ref, bf16[3,256,512]{2,1,0:T(8,128)(2,1)S(1)} %get-tuple-element.43.refs_0_, bf16[3,256,512]{2,1,0:T(8,128)(2,1)S(1)} %collective-permute-done.refs_1_, ...), custom_call_target="tpu_custom_call" | custom-call | flops 1610612736 | bytes 6291456 | tf_op jit(solution)/shard_map/pallas_call | solution.py:230
  55.8 2.3 %collective-permute-done.7.refs_4_ = bf16[2,256,512]{2,1,0:T(8,128)(2,1)S(1)} collective-permute-done((bf16[2,256,512]{2,1,0:T(8,128)(2,1)S(1)}, bf16[2,256,512]{2,1,0:T(8,128)(2,1)S(1)}, u32[]{:S(2)}, u32[]{:S(2)}) %collective-permute-start.7) | collective-permute-done | bytes 524320 | tf_op jit(solution)/shard_map/ppermute | solution.py:383
  58.1 0.0 copy-start
  58.1 1.7 %shard_map.69 = (bf16[2,528,256]{2,1,0:T(8,128)(2,1)S(1)}, bf16[2,528,256]{2,1,0:T(8,128)(2,1)S(1)}) custom-call(s32[13]{0:T(128)S(1)} %stack.55.where_ref, bf16[3,256,512]{2,1,0:T(8,128)(2,1)S(1)} %get-tuple-element.43.refs_0_, bf16[3,256,512]{2,1,0:T(8,128)(2,1)S(1)} %collective-permute-done.refs_1_, bf16[256,512]{1,0:T(8,128)(2,1)S(1)} %collective-permute-done.2.refs_2_, ...), custom_call_target="tpu_custom_call" | custom-call | flops 536870912 | bytes 2097152 | tf_op jit(solution)/shard_map/pallas_call | solution.py:230
  59.8 1.9 %collective-permute-start.10 = (bf16[2,528,256]{2,1,0:T(8,128)(2,1)S(1)}, bf16[2,528,256]{2,1,0:T(8,128)(2,1)S(1)}, u32[]{:S(2)}, u32[]{:S(2)}) collective-permute-start(bf16[2,528,256]{2,1,0:T(8,128)(2,1)S(1)} %get-tuple-element.72), channel_id=1, source_target_pairs={{0,16},{16,0},{32,48},{48,32},{64,80},{80,64},{96,112},{112,96},{1... | collective-permute-start | bytes 1622024 | tf_op jit(solution)/shard_map/ppermute | solution.py:435
  61.7 0.0 copy-done
  61.8 1.9 %collective-permute-done.10.b_ref = bf16[2,528,256]{2,1,0:T(8,128)(2,1)S(1)} collective-permute-done((bf16[2,528,256]{2,1,0:T(8,128)(2,1)S(1)}, bf16[2,528,256]{2,1,0:T(8,128)(2,1)S(1)}, u32[]{:S(2)}, u32[]{:S(2)}) %collective-permute-start.10) | collective-permute-done | bytes 540704 | tf_op jit(solution)/shard_map/ppermute | solution.py:435
  63.6 0.0 copy-start.1
  63.7 0.0 copy-start.2
  63.7 0.1 shard_map.70
  63.8 1.3 %collective-permute-start.11 = (bf16[528,256]{1,0:T(8,128)(2,1)S(1)}, bf16[528,256]{1,0:T(8,128)(2,1)S(1)}, u32[]{:S(2)}, u32[]{:S(2)}) collective-permute-start(bf16[528,256]{1,0:T(8,128)(2,1)S(1)} %shard_map.70), channel_id=1, source_target_pairs={{0,256},{16,272},{32,288},{48,304},{64,320},{80,336},{96,352},{112... | collective-permute-start | bytes 811016 | tf_op jit(solution)/shard_map/ppermute | solution.py:440
  65.1 2.0 %collective-permute-start.12 = (bf16[2,6,512]{2,1,0:T(8,128)(2,1)S(1)}, bf16[2,6,512]{2,1,0:T(8,128)(2,1)S(1)}, u32[]{:S(2)}, u32[]{:S(2)}) collective-permute-start(bf16[2,6,512]{2,1,0:T(8,128)(2,1)S(1)} %slice.7), channel_id=1, source_target_pairs={{0,16},{16,32},{32,48},{48,64},{64,80},{80,96},{96,112},{112,128},... | collective-permute-start | bytes 36872 | tf_op jit(solution)/shard_map/ppermute | solution.py:374
  67.1 5.2 %collective-permute-done.12.rim_ref = bf16[2,6,512]{2,1,0:T(8,128)(2,1)S(1)} collective-permute-done((bf16[2,6,512]{2,1,0:T(8,128)(2,1)S(1)}, bf16[2,6,512]{2,1,0:T(8,128)(2,1)S(1)}, u32[]{:S(2)}, u32[]{:S(2)}) %collective-permute-start.12) | collective-permute-done | bytes 12320 | tf_op jit(solution)/shard_map/ppermute | solution.py:374
  72.4 0.0 copy-done.1
  72.4 0.0 copy-done.2
  72.4 0.8 shard_map.71
  73.2 1.6 %collective-permute-done.11.s_ref = bf16[528,256]{1,0:T(8,128)(2,1)S(1)} collective-permute-done((bf16[528,256]{1,0:T(8,128)(2,1)S(1)}, bf16[528,256]{1,0:T(8,128)(2,1)S(1)}, u32[]{:S(2)}, u32[]{:S(2)}) %collective-permute-start.11) | collective-permute-done | bytes 270368 | tf_op jit(solution)/shard_map/ppermute | solution.py:440
  74.8 1.4 %shard_map.72 = (bf16[512,256]{1,0:T(8,128)(2,1)S(1)}, f32[16,1,256]{2,1,0:T(1,128)}) custom-call(s32[13]{0:T(128)S(1)} %stack.55.where_ref, bf16[2,528,256]{2,1,0:T(8,128)(2,1)S(1)} %get-tuple-element.71.a_ref, bf16[2,528,256]{2,1,0:T(8,128)(2,1)S(1)} %collective-permute-done.10.b_ref, bf16[528,256]{1,0:T(8,128)(2,1)S(1)} %collective-permute-done.11.s_ref), custom_call_target="tpu_custom_call" | custom-call | tf_op jit(solution)/shard_map/pallas_call | solution.py:309
  76.3 9.1 %all-to-all-start = ((f32[16,1,256]{2,1,0:T(1,128)}), f32[16,1,256]{2,1,0:T(1,128)S(1)}, u32[]{:S(2)}, u32[]{:S(2)}) async-start(f32[16,1,256]{2,1,0:T(1,128)} %get-tuple-element.77), calls=%async_computation | async-start | bytes 32768 | tf_op jit(solution)/shard_map/all_to_all | solution.py:445
  85.3 0.1 shard_map.73.wide_ref
  85.5 9.8 %all-to-all-done.spread_ref = f32[16,1,256]{2,1,0:T(1,128)S(1)} async-done(((f32[16,1,256]{2,1,0:T(1,128)}), f32[16,1,256]{2,1,0:T(1,128)S(1)}, u32[]{:S(2)}, u32[]{:S(2)}) %all-to-all-start) | async-done | bytes 16416 | tf_op jit(solution)/shard_map/all_to_all | solution.py:445
  95.3 0.9 shard_map.74
  (1 shorter events, 0.0 us)
Async XLA Ops:
  1.2 11.7 %collective-permute-start = (bf16[3,256,512]{2,1,0:T(8,128)(2,1)S(1)}, bf16[3,256,512]{2,1,0:T(8,128)(2,1)S(1)}, u32[]{:S(2)}, u32[]{:S(2)}) collective-permute-start(bf16[3,256,512]{2,1,0:T(8,128)(2,1)S(1)} %get-tuple-element.43.refs_0_), channel_id=1, source_target_pairs={{0,16},{16,0},{32,48},{48,32},{64,80},{80,64},{96,112},{112,96},{1... | collective-permute-start | bytes 2359304 | tf_op jit(solution)/shard_map/ppermute | solution.py:382
  3.2 18.1 %collective-permute-start.1 = (bf16[2,256,512]{2,1,0:T(8,128)(2,1)S(1)}, bf16[2,256,512]{2,1,0:T(8,128)(2,1)S(1)}, u32[]{:S(2)}, u32[]{:S(2)}) collective-permute-start(bf16[2,256,512]{2,1,0:T(8,128)(2,1)S(1)} %get-tuple-element.44.refs_4_), channel_id=1, source_target_pairs={{0,32},{16,240},{32,64},{48,16},{64,96},{80,48},{96,128},{112,80},... | collective-permute-start | bytes 1572872 | tf_op jit(solution)/shard_map/ppermute | solution.py:383
  7.5 10.0 %collective-permute-start.2 = (bf16[256,512]{1,0:T(8,128)(2,1)S(1)}, bf16[256,512]{1,0:T(8,128)(2,1)S(1)}, u32[]{:S(2)}, u32[]{:S(2)}) collective-permute-start(bf16[256,512]{1,0:T(8,128)(2,1)S(1)} %get-tuple-element.45.refs_2_.refs_3_), channel_id=1, source_target_pairs={{256,0},{272,16},{288,32},{304,48},{320,64},{336,80},{352,96},{368... | collective-permute-start | bytes 786440 | tf_op jit(solution)/shard_map/ppermute | solution.py:395
  13.8 13.6 %collective-permute-start.5 = (bf16[2,256,512]{2,1,0:T(8,128)(2,1)}, bf16[2,256,512]{2,1,0:T(8,128)(2,1)}, u32[]{:S(2)}, u32[]{:S(2)}) collective-permute-start(bf16[2,256,512]{2,1,0:T(8,128)(2,1)} %slice.8), channel_id=1, source_target_pairs={{0,32},{16,240},{32,64},{48,16},{64,96},{80,48},{96,128},{112,80},... | collective-permute-start | bytes 1572872 | tf_op jit(solution)/shard_map/ppermute | solution.py:383
  21.3 12.3 %collective-permute-start.4 = (bf16[2,256,512]{2,1,0:T(8,128)(2,1)S(1)}, bf16[2,256,512]{2,1,0:T(8,128)(2,1)S(1)}, u32[]{:S(2)}, u32[]{:S(2)}) collective-permute-start(bf16[2,256,512]{2,1,0:T(8,128)(2,1)S(1)} %collective-permute-done.1.refs_5_), channel_id=1, source_target_pairs={{0,32},{16,240},{32,64},{48,16},{64,96},{80,48},{96,128},{112,80},... | collective-permute-start | bytes 1572872 | tf_op jit(solution)/shard_map/ppermute | solution.py:383
  23.2 6.1 %collective-permute-start.3 = (bf16[256,512]{1,0:T(8,128)(2,1)S(1)}, bf16[256,512]{1,0:T(8,128)(2,1)S(1)}, u32[]{:S(2)}, u32[]{:S(2)}) collective-permute-start(bf16[256,512]{1,0:T(8,128)(2,1)S(1)} %collective-permute-done.2.refs_2_), channel_id=1, source_target_pairs={{0,16},{16,0},{32,48},{48,32},{64,80},{80,64},{96,112},{112,96},{1... | collective-permute-start | bytes 786440 | tf_op jit(solution)/shard_map/ppermute | solution.py:403
  27.4 12.5 %collective-permute-start.8 = (bf16[2,256,512]{2,1,0:T(8,128)(2,1)}, bf16[2,256,512]{2,1,0:T(8,128)(2,1)S(1)}, u32[]{:S(2)}, u32[]{:S(2)}) collective-permute-start(bf16[2,256,512]{2,1,0:T(8,128)(2,1)} %collective-permute-done.5.refs_4_), channel_id=1, source_target_pairs={{0,32},{16,240},{32,64},{48,16},{64,96},{80,48},{96,128},{112,80},... | collective-permute-start | bytes 1572872 | tf_op jit(solution)/shard_map/ppermute | solution.py:383
  33.5 12.3 %collective-permute-start.6 = (bf16[2,256,512]{2,1,0:T(8,128)(2,1)S(1)}, bf16[2,256,512]{2,1,0:T(8,128)(2,1)S(1)}, u32[]{:S(2)}, u32[]{:S(2)}) collective-permute-start(bf16[2,256,512]{2,1,0:T(8,128)(2,1)S(1)} %collective-permute-done.4.refs_5_), channel_id=1, source_target_pairs={{0,32},{16,240},{32,64},{48,16},{64,96},{80,48},{96,128},{112,80},... | collective-permute-start | bytes 1572872 | tf_op jit(solution)/shard_map/ppermute | solution.py:383
  39.9 12.3 %collective-permute-start.9 = (bf16[2,256,512]{2,1,0:T(8,128)(2,1)S(1)}, bf16[2,256,512]{2,1,0:T(8,128)(2,1)S(1)}, u32[]{:S(2)}, u32[]{:S(2)}) collective-permute-start(bf16[2,256,512]{2,1,0:T(8,128)(2,1)S(1)} %collective-permute-done.8.refs_4_), channel_id=1, source_target_pairs={{0,32},{16,240},{32,64},{48,16},{64,96},{80,48},{96,128},{112,80},... | collective-permute-start | bytes 1572872 | tf_op jit(solution)/shard_map/ppermute | solution.py:383
  45.8 12.3 %collective-permute-start.7 = (bf16[2,256,512]{2,1,0:T(8,128)(2,1)S(1)}, bf16[2,256,512]{2,1,0:T(8,128)(2,1)S(1)}, u32[]{:S(2)}, u32[]{:S(2)}) collective-permute-start(bf16[2,256,512]{2,1,0:T(8,128)(2,1)S(1)} %collective-permute-done.6.refs_5_), channel_id=1, source_target_pairs={{0,32},{16,240},{32,64},{48,16},{64,96},{80,48},{96,128},{112,80},... | collective-permute-start | bytes 1572872 | tf_op jit(solution)/shard_map/ppermute | solution.py:383
  58.1 3.7 %copy-start = (bf16[3,256,512]{2,1,0:T(8,128)(2,1)S(1)}, bf16[3,256,512]{2,1,0:T(8,128)(2,1)}, u32[]{:S(2)}) copy-start(bf16[3,256,512]{2,1,0:T(8,128)(2,1)} %input_ref.1) | copy-start | bytes 2359300
  59.8 3.8 %collective-permute-start.10 = (bf16[2,528,256]{2,1,0:T(8,128)(2,1)S(1)}, bf16[2,528,256]{2,1,0:T(8,128)(2,1)S(1)}, u32[]{:S(2)}, u32[]{:S(2)}) collective-permute-start(bf16[2,528,256]{2,1,0:T(8,128)(2,1)S(1)} %get-tuple-element.72), channel_id=1, source_target_pairs={{0,16},{16,0},{32,48},{48,32},{64,80},{80,64},{96,112},{112,96},{1... | collective-permute-start | bytes 1622024 | tf_op jit(solution)/shard_map/ppermute | solution.py:435
  63.6 8.7 %copy-start.1 = (f32[7,512]{1,0:T(8,128)S(1)}, f32[7,512]{1,0:T(8,128)}, u32[]{:S(2)}) copy-start(f32[7,512]{1,0:T(8,128)} %filter_ref.1) | copy-start | bytes 43012
  63.7 8.7 %copy-start.2 = (f32[512]{0:T(512)S(1)}, f32[512]{0:T(512)}, u32[]{:S(2)}) copy-start(f32[512]{0:T(512)} %param.11) | copy-start | bytes 6148
  63.8 11.1 %collective-permute-start.11 = (bf16[528,256]{1,0:T(8,128)(2,1)S(1)}, bf16[528,256]{1,0:T(8,128)(2,1)S(1)}, u32[]{:S(2)}, u32[]{:S(2)}) collective-permute-start(bf16[528,256]{1,0:T(8,128)(2,1)S(1)} %shard_map.70), channel_id=1, source_target_pairs={{0,256},{16,272},{32,288},{48,304},{64,320},{80,336},{96,352},{112... | collective-permute-start | bytes 811016 | tf_op jit(solution)/shard_map/ppermute | solution.py:440
  65.1 7.3 %collective-permute-start.12 = (bf16[2,6,512]{2,1,0:T(8,128)(2,1)S(1)}, bf16[2,6,512]{2,1,0:T(8,128)(2,1)S(1)}, u32[]{:S(2)}, u32[]{:S(2)}) collective-permute-start(bf16[2,6,512]{2,1,0:T(8,128)(2,1)S(1)} %slice.7), channel_id=1, source_target_pairs={{0,16},{16,32},{32,48},{48,64},{64,80},{80,96},{96,112},{112,128},... | collective-permute-start | bytes 36872 | tf_op jit(solution)/shard_map/ppermute | solution.py:374
  76.3 19.1 %all-to-all-start = ((f32[16,1,256]{2,1,0:T(1,128)}), f32[16,1,256]{2,1,0:T(1,128)S(1)}, u32[]{:S(2)}, u32[]{:S(2)}) async-start(f32[16,1,256]{2,1,0:T(1,128)} %get-tuple-element.77), calls=%async_computation | async-start | bytes 32768 | tf_op jit(solution)/shard_map/all_to_all | solution.py:445
